TPU v7x, 128 devices: a whole 4x4x4 slice. The times are simulated.
128 devices in a mesh: replica: 8 (over y_lo, z), fsdp: 16 (over y_hi, x, core).
Axes of the slice: x: 4, y: 4 (y_hi: 2, y_lo: 2; y = y_hi * 2 + y_lo), z: 4, core: 2. Of those that a mesh axis runs over, the one named last changes fastest.
Arguments:
- activations: bfloat16 [8, 4096, 4608], P('replica', 'fsdp'), may hold values from -6 to 6
- cotangent: bfloat16 [8, 4096, 2, 1024], P('replica', 'fsdp'), may hold values from -0.1796875 to 0.1796875
- weights: float32 [8, 4608, 2, 1024], P('replica', 'fsdp'), may hold values from -0.6 to 0.6
- first_moment: float32 [8, 4608, 2, 1024], P('replica', 'fsdp'), may hold values from -3 to 3
- second_moment: float32 [8, 4608, 2, 1024], P('replica', 'fsdp'), may hold values from 0.1 to 3
- anchor: float32 [4608, 1024], P('fsdp'), may hold values from -0.6 to 0.6
- momentum: float32 [4608, 1024], P('fsdp'), may hold values from -0.3 to 0.3
Outputs:
- weights_out: float32 [8, 4608, 2, 1024], P('replica', 'fsdp')
- first_out: float32 [8, 4608, 2, 1024], P('replica', 'fsdp')
- second_out: float32 [8, 4608, 2, 1024], P('replica', 'fsdp')
- anchor_out: float32 [4608, 1024], P('fsdp')
- momentum_out: float32 [4608, 1024], P('fsdp')
- input_grad: bfloat16 [8, 4096, 4608], P('replica', 'fsdp')
All inputs are finite; a program needn't handle non-finite values.
Results may differ from a plain program's by a relative error of at most 0.0095.
Values may be sent and summed in bfloat16 or wider, within the bound.
No kernel may reach another device: no remote copies, remote signals or barrier semaphores. Data moves between devices by JAX's collectives and lax.ppermute only.
A program may use at most 128 MiB of HBM per device.

v0:
```python
import jax
import jax.numpy as jnp
import numpy as np
from jax import lax
from jax.experimental import pallas as pl
from jax.experimental.pallas import tpu as pltpu
from jax.sharding import Mesh
from jax.sharding import PartitionSpec as P

CORRECT_FIRST = 1.0 - 0.9**8
CORRECT_SECOND = 1.0 - 0.95**8
AXES = ("ylo", "z", "yhi", "x", "core")
SIZES = (2, 4, 2, 4, 2)
BF16 = jnp.bfloat16
F32 = jnp.float32
ANY = pl.BlockSpec(memory_space=pl.ANY)
VMEM_BYTES = 48 * 1024 * 1024


def shift(value, **steps):
    pairs = []
    for source in np.ndindex(*SIZES):
        target = [(s + steps.get(a, 0)) % n for s, a, n in zip(source, AXES, SIZES)]
        pairs.append(
            (int(np.ravel_multi_index(source, SIZES)), int(np.ravel_multi_index(target, SIZES)))
        )
    return lax.ppermute(value, AXES, pairs)


def call(kernel, out_shape, place, inputs, in_specs, out_specs, scratch=(), grid=(1,), flops=0, moved=0):
    return pl.pallas_call(
        kernel,
        out_shape=out_shape,
        grid_spec=pltpu.PrefetchScalarGridSpec(
            num_scalar_prefetch=1,
            grid=grid,
            in_specs=in_specs,
            out_specs=out_specs,
            scratch_shapes=list(scratch),
        ),
        compiler_params=pltpu.CompilerParams(vmem_limit_bytes=VMEM_BYTES),
        cost_estimate=pl.CostEstimate(flops=flops, bytes_accessed=moved, transcendentals=0),
    )(place, *inputs)


def after(value, *others):
    return lax.optimization_barrier((value, *others))[0]


def shape(dims, dtype=BF16):
    return jax.ShapeDtypeStruct(dims, dtype)


def far_half_kernel(place, acts, out, sem):
    n = out.shape[1]
    copy = pltpu.make_async_copy(
        acts.at[:, pl.ds(pl.multiple_of((1 - place[0]) * n, 128), n)], out, sem
    )
    copy.start()
    copy.wait()


def gradient_kernel(
    place, acts, a_far, c_own, c_far, mine, other, both, a_s, c_s, g_s, in_sem, out_sem, both_sem
):
    h, c = place[0], place[1]
    tok, wide = a_far.shape
    rows = mine.shape[1]
    copies = [
        pltpu.make_async_copy(
            acts.at[:, pl.ds(pl.multiple_of(h * wide, 128), wide)],
            a_s.at[pl.ds(0, tok)],
            in_sem.at[0],
        ),
        pltpu.make_async_copy(a_far, a_s.at[pl.ds(tok, tok)], in_sem.at[1]),
        pltpu.make_async_copy(c_own, c_s.at[pl.ds(0, tok)], in_sem.at[2]),
        pltpu.make_async_copy(c_far, c_s.at[pl.ds(tok, tok)], in_sem.at[3]),
    ]
    for copy in copies:
        copy.start()
    for copy in copies:
        copy.wait()
    keep = pltpu.make_async_copy(c_s, both, both_sem)
    keep.start()
    tile = 256
    sent = 0
    for i in range(wide // tile):
        g_s[i * tile : (i + 1) * tile, :] = lax.dot_general(
            a_s[:, i * tile : (i + 1) * tile],
            c_s[...],
            (((0,), (0,)), ((), ())),
            preferred_element_type=F32,
        ).astype(BF16)
        while (sent + 1) * rows <= (i + 1) * tile:
            block = g_s.at[pl.ds(sent * rows, rows)]
            to, core = sent // 2, sent % 2

            @pl.when(c == core)
            def _(block=block, to=to, sent=sent):
                pltpu.make_async_copy(block, mine.at[to], out_sem.at[sent]).start()

            @pl.when(c != core)
            def _(block=block, to=to, sent=sent):
                pltpu.make_async_copy(block, other.at[to], out_sem.at[sent]).start()

            sent += 1
    for b in range(sent):
        pltpu.make_async_copy(
            g_s.at[pl.ds(b * rows, rows)], mine.at[b // 2], out_sem.at[b]
        ).wait()
    keep.wait()


def block_sum(mine, got):
    return mine[0].astype(F32) + got[0].astype(F32)


def first_hop_kernel(place, mine, got, up, down):
    part = block_sum(mine, got).astype(BF16)
    n = up.shape[0]
    up[...] = part[:n]
    down[...] = part[n:]


def second_hop_kernel(place, mine_up, got_up, mine_down, got_down, up, down, to_up, to_down):
    n = up.shape[0]
    part = block_sum(mine_up, got_up)
    to_up[:n] = (part[:n] + up[...].astype(F32)).astype(BF16)
    to_up[n:] = part[n:].astype(BF16)
    part = block_sum(mine_down, got_down)
    to_down[:n] = part[:n].astype(BF16)
    to_down[n:] = (part[n:] + down[...].astype(F32)).astype(BF16)


def owned_sum(mine, got, up, down):
    return block_sum(mine, got) + up[...].astype(F32) + down[...].astype(F32)


def adamw(w, m, v, g):
    m = 0.9 * m + 0.1 * g
    v = 0.95 * v + 0.05 * g * g
    step_dir = m / CORRECT_FIRST / (jnp.sqrt(v / CORRECT_SECOND) + 1e-08)
    return m, v, w - 0.01 * (step_dir + 0.1 * w)


def selected_kernel(place, w, m, v, mine, got, up, down, own, s1, s2, s3, sel):
    g = owned_sum(mine, got, up, down)
    sel[...] = adamw(w[:, 0, :], m[:, 0, :], v[:, 0, :], g)[2]
    n = own.shape[1]
    for step, out in ((0, own), (1, s1), (2, s2), (3, s3)):
        start = pl.multiple_of(lax.rem(place[3] + step, 4) * n, 128)
        out[...] = sel[:, pl.ds(start, n)].astype(out.dtype)


def moments_kernel(place, w, m, v, *rest):
    parts, (first, second, inner) = (rest[:4], rest[4:8]), rest[8:]
    for f in range(2):
        g = owned_sum(*parts[f])
        m_new, v_new, inner_new = adamw(w[:, f, :], m[:, f, :], v[:, f, :], g)
        first[:, f, :] = m_new
        second[:, f, :] = v_new
    inner[...] = inner_new


def outer_kernel(place, m0, m1, m2, m3, anchor, momentum, inner, weights, anchor_new, momentum_new, mean):
    n = m0.shape[1]
    for step, part in enumerate((m0, m1, m2, m3)):
        start = pl.multiple_of(lax.rem(place[3] + step, 4) * n, 128)
        mean[:, pl.ds(start, n)] = part[...].astype(F32)
    delta = anchor[...] - mean[...]
    moved = 0.9 * momentum[...] + delta
    synced = anchor[...] - 0.7 * (delta + 0.9 * moved)
    momentum_new[...] = moved
    anchor_new[...] = synced
    weights[:, 0, :] = synced
    weights[:, 1, :] = inner[...]


def weave_kernel(place, near, far, near_other, far_other, out, held):
    h, c = place[0], place[1]
    held[2 * h + c] = near[...]
    held[2 * (1 - h) + c] = far[...]
    held[2 * h + (1 - c)] = near_other[...]
    held[2 * (1 - h) + (1 - c)] = far_other[...]
    rows = near.shape[1] // 4
    for yhi in range(2):
        for to in range(4):
            for core in range(2):
                b = (yhi * 4 + to) * 2 + core
                out[:, b * rows : (b + 1) * rows] = held[
                    2 * yhi + core, :, to * rows : (to + 1) * rows
                ]


def input_kernel(place, w0, wm, wp, w2a, w2b, k0, v0, k1, v1, out0, out1, w_s, sem):
    x = place[2]
    rows = w0.shape[0]
    part = rows // 2

    def at(step, lo, n):
        return w_s.at[pl.ds(pl.multiple_of(lax.rem(x + step, 4) * rows + lo, 16), n)]

    copies = [
        pltpu.make_async_copy(w0, at(0, 0, rows), sem.at[0]),
        pltpu.make_async_copy(wm, at(3, 0, rows), sem.at[1]),
        pltpu.make_async_copy(wp, at(1, 0, rows), sem.at[2]),
        pltpu.make_async_copy(w2a, at(2, 0, part), sem.at[3]),
        pltpu.make_async_copy(w2b, at(2, part, part), sem.at[4]),
    ]
    for copy in copies:
        copy.start()
    for copy in copies:
        copy.wait()
    feat = k0.shape[1]
    tile = 384
    for j in range(4 * rows // tile):
        wk = w_s[j * tile : (j + 1) * tile, :feat]
        wv = w_s[j * tile : (j + 1) * tile, feat:]
        for key, val, out in ((k0, v0, out0), (k1, v1, out1)):
            dims = (((1,), (1,)), ((), ()))
            acc = lax.dot_general(key[...], wk, dims, preferred_element_type=F32)
            acc += lax.dot_general(val[...], wv, dims, preferred_element_type=F32)
            out[:, j * tile : (j + 1) * tile] = acc.astype(BF16)


def shards(activations, cotangent, weights, first_moment, second_moment, anchor, momentum):
    acts = activations[0]
    tok, width = acts.shape
    weight_here = weights[0]
    rows = weight_here.shape[0]
    feat = weight_here.shape[2]
    ylo, z, h, x, c = [lax.axis_index(a) for a in AXES]
    place = jnp.stack([h, c, x, z]).astype(jnp.int32)
    hr = rows // 2

    a_send = call(
        far_half_kernel,
        shape((tok, width // 2)),
        place,
        (acts,),
        [ANY],
        ANY,
        [pltpu.SemaphoreType.DMA],
        moved=2 * tok * width,
    )
    a_far = shift(a_send, yhi=1)
    w0 = weight_here.astype(BF16).reshape(rows, 2 * feat)
    wm = shift(w0, x=1)
    wp = shift(w0, x=-1)
    cot = after(cotangent, w0, a_send)[0]
    cots = [cot[:, 0, :], cot[:, 1, :]]
    fars = [shift(t, yhi=1) for t in cots]
    w2a = shift(wm[:hr], x=1)
    w2b = shift(wp[hr:], x=-1)

    def partial(f):
        return call(
            gradient_kernel,
            [shape((4, rows, feat))] * 2 + [shape((2 * tok, feat))],
            place,
            (acts, a_far, cots[f], fars[f]),
            [ANY] * 4,
            [ANY] * 3,
            [
                pltpu.VMEM((2 * tok, width // 2), BF16),
                pltpu.VMEM((2 * tok, feat), BF16),
                pltpu.VMEM((width // 2, feat), BF16),
                pltpu.SemaphoreType.DMA((4,)),
                pltpu.SemaphoreType.DMA((8,)),
                pltpu.SemaphoreType.DMA,
            ],
            flops=2 * 2 * tok * width // 2 * feat,
            moved=12 * 2**20,
        )

    def block(step):
        return pl.BlockSpec((1, rows, feat), lambda i, place: (lax.rem(place[2] + step, 4), 0, 0))

    def whole(*dims):
        return pl.BlockSpec(dims, lambda i, place: (0,) * len(dims))

    def first_hop(mine, got):
        up, down = call(
            first_hop_kernel,
            [shape((hr, feat))] * 2,
            place,
            (mine, got),
            [block(2)] * 2,
            [whole(hr, feat)] * 2,
            moved=2**21,
        )
        return up, down

    def second_hop(mine, got, up, down):
        return call(
            second_hop_kernel,
            [shape((rows, feat))] * 2,
            place,
            (mine, got, mine, got, up, down),
            [block(1), block(1), block(3), block(3), whole(hr, feat), whole(hr, feat)],
            [whole(rows, feat)] * 2,
            moved=2**22,
        )

    mine0, other0, both0 = partial(0)
    got0 = shift(other0, core=1)
    oth0 = shift(both0, core=1)
    mine1, other1, both1 = partial(1)
    got1 = shift(other1, core=1)
    oth1 = shift(both1, core=1)
    up0, down0 = first_hop(mine0, got0)
    up0r, down0r = shift(up0, x=1), shift(down0, x=-1)
    up1, down1 = first_hop(mine1, got1)
    up1r, down1r = shift(up1, x=1), shift(down1, x=-1)
    to_up0, to_down0 = second_hop(mine0, got0, up0r, down0r)
    from_down0, from_up0 = shift(to_up0, x=1), shift(to_down0, x=-1)
    to_up1, to_down1 = second_hop(mine1, got1, up1r, down1r)
    from_down1, from_up1 = shift(to_up1, x=1), shift(to_down1, x=-1)

    def input_part(b, first):
        tokens = pl.BlockSpec((tok, feat), lambda i, place: (b, 0))
        return call(
            input_kernel,
            [shape((tok, 4 * rows))] * 2,
            place,
            (first, wm, wp, w2a, w2b, both0, both1, oth0, oth1),
            [ANY] * 5 + [tokens] * 4,
            [whole(tok, 4 * rows)] * 2,
            [pltpu.VMEM((4 * rows, 2 * feat), BF16), pltpu.SemaphoreType.DMA((5,))],
            flops=2 * 2 * tok * 4 * rows * 2 * feat,
            moved=8 * 2**20,
        )

    out_far, out_far_other = input_part(1, after(w0, up0, up1))
    far = shift(out_far, yhi=1)
    far_other = shift(out_far_other, yhi=1, core=1)
    near, out_near_other = input_part(0, after(w0, to_up0, to_up1, out_far))
    near_other = shift(out_near_other, core=1)

    half_rows = pl.BlockSpec((hr, feat), lambda i, place: (i, 0))
    half_both = pl.BlockSpec((hr, 2, feat), lambda i, place: (i, 0, 0))
    half_own = pl.BlockSpec((1, hr, feat), lambda i, place: (place[2], i, 0))
    qc = feat // 4
    half_quarter = pl.BlockSpec((hr, qc), lambda i, place: (i, 0))
    sums0 = (mine0, got0, from_down0, from_up0)
    sums1 = (mine1, got1, from_down1, from_up1)
    sum_specs = [half_own, half_own, half_rows, half_rows]
    own, s1, s2, s3 = call(
        selected_kernel,
        [shape((rows, qc), F32)] + [shape((rows, qc))] * 3,
        place,
        (weight_here, first_moment[0], second_moment[0], *sums0),
        [half_both] * 3 + sum_specs,
        [half_quarter] * 4,
        [pltpu.VMEM((hr, feat), F32)],
        grid=(2,),
        moved=10 * 2**20,
    )
    total = own
    for s, part in ((1, s1), (2, s2), (-1, s3)):
        total = total + shift(part, z=s).astype(F32)
    total = lax.reduce_precision(total, 8, 7)
    total = total + shift(total.astype(BF16), ylo=1).astype(F32)
    mean = (total / 8).astype(BF16)
    means = (mean, shift(mean, z=-1), shift(mean, z=2), shift(mean, z=1))
    first_out, second_out, inner = call(
        moments_kernel,
        [shape((rows, 2, feat), F32)] * 2 + [shape((rows, feat), F32)],
        place,
        (weight_here, first_moment[0], second_moment[0], *sums0, *sums1),
        [half_both] * 3 + sum_specs * 2,
        [half_both] * 2 + [half_rows],
        grid=(2,),
        moved=16 * 2**20,
    )
    weights_out, anchor_out, momentum_out = call(
        outer_kernel,
        [shape((rows, 2, feat), F32)] + [shape((rows, feat), F32)] * 2,
        place,
        (*means, anchor, momentum, inner),
        [half_quarter] * 4 + [half_rows] * 3,
        [half_both] + [half_rows] * 2,
        [pltpu.VMEM((hr, feat), F32)],
        grid=(2,),
        moved=9 * 2**20,
    )

    tile = 64
    strip = pl.BlockSpec((tile, 4 * rows), lambda i, place: (i, 0))
    input_grad = call(
        weave_kernel,
        shape((tok, width)),
        place,
        (near, far, near_other, far_other),
        [strip] * 4,
        pl.BlockSpec((tile, width), lambda i, place: (i, 0)),
        [pltpu.VMEM((4, tile, 4 * rows), BF16)],
        grid=(tok // tile,),
        moved=5 * 2**20,
    )
    return (
        weights_out[None],
        first_out[None],
        second_out[None],
        anchor_out,
        momentum_out,
        input_grad[None],
    )


def solution(mesh):
    fine = Mesh(mesh.devices.reshape(SIZES), AXES)
    rep, fs = ("ylo", "z"), ("yhi", "x", "core")
    in_specs = (
        P(rep, fs, None),
        P(rep, fs, None, None),
        P(rep, fs, None, None),
        P(rep, fs, None, None),
        P(rep, fs, None, None),
        P(fs, None),
        P(fs, None),
    )
    out_specs = (
        P(rep, fs, None, None),
        P(rep, fs, None, None),
        P(rep, fs, None, None),
        P(fs, None),
        P(fs, None),
        P(rep, fs, None),
    )
    return jax.shard_map(shards, mesh=fine, in_specs=in_specs, out_specs=out_specs, check_vma=False)
```

profile of v0, /device:TPU:0, one launch (start us, length us, event | category | flops | bytes accessed | tf_op | source)
XLA Modules:
  0.0 211.4 jit_solution(1959836013213326521)
XLA Ops:
  0.7 1.8 copy-done.6
  3.2 3.4 %collective-permute-start = (bf16[256,2304]{1,0:T(8,128)(2,1)S(1)}, bf16[256,2304]{1,0:T(8,128)(2,1)S(1)}, u32[]{:S(2)}, u32[]{:S(2)}) collective-permute-start(bf16[256,2304]{1,0:T(8,128)(2,1)S(1)} %shard_map.118), channel_id=1, source_target_pairs={{0,8},{1,9},{2,10},{3,11},{4,12},{5,13},{6,14},{7,15},{8,0},{9,1},... | collective-permute-start | bytes 3538952 | tf_op jit(solution)/shard_map/ppermute | solution.py:27
  9.4 34.4 %collective-permute-done.1.c_far = bf16[256,1024]{1,0:T(8,128)(2,1)S(1)} collective-permute-done((bf16[256,1024]{1,0:T(8,128)(2,1)S(1)}, bf16[256,1024]{1,0:T(8,128)(2,1)S(1)}, u32[]{:S(2)}, u32[]{:S(2)}) %collective-permute-start.1) | collective-permute-done | bytes 524320 | tf_op jit(solution)/shard_map/ppermute | solution.py:27
  43.8 7.2 %shard_map.119 = (bf16[4,288,1024]{2,1,0:T(8,128)(2,1)S(1)}, bf16[4,288,1024]{2,1,0:T(8,128)(2,1)}, bf16[512,1024]{1,0:T(8,128)(2,1)S(1)}) custom-call(s32[4]{0:T(128)S(1)} %pad_add_fusion.place, bf16[256,4608]{1,0:T(8,128)(2,1)} %bitcast.24, bf16[256,2304]{1,0:T(8,128)(2,1)S(1)} %collective-permute-done.a_far, ...), custom_call_target="tpu_custom_call" | custom-call | flops 2415919104 | bytes 12582912 | tf_op jit(solution)/shard_map/pallas_call | solution.py:31
  51.1 3.3 %collective-permute-start.14 = (bf16[256,1024]{1,0:T(8,128)(2,1)S(1)}, bf16[256,1024]{1,0:T(8,128)(2,1)S(1)}, u32[]{:S(2)}, u32[]{:S(2)}) collective-permute-start(bf16[256,1024]{1,0:T(8,128)(2,1)S(1)} %get-tuple-element.68.c_own), channel_id=1, source_target_pairs={{0,8},{1,9},{2,10},{3,11},{4,12},{5,13},{6,14},{7,15},{8,0},{9,1},... | collective-permute-start | bytes 1572872 | tf_op jit(solution)/shard_map/ppermute | solution.py:27
  54.5 12.5 %collective-permute-done.14.c_far = bf16[256,1024]{1,0:T(8,128)(2,1)S(1)} collective-permute-done((bf16[256,1024]{1,0:T(8,128)(2,1)S(1)}, bf16[256,1024]{1,0:T(8,128)(2,1)S(1)}, u32[]{:S(2)}, u32[]{:S(2)}) %collective-permute-start.14) | collective-permute-done | bytes 524320 | tf_op jit(solution)/shard_map/ppermute | solution.py:27
  67.0 7.2 %shard_map.123 = (bf16[4,288,1024]{2,1,0:T(8,128)(2,1)S(1)}, bf16[4,288,1024]{2,1,0:T(8,128)(2,1)}, bf16[512,1024]{1,0:T(8,128)(2,1)}) custom-call(s32[4]{0:T(128)S(1)} %pad_add_fusion.place, bf16[256,4608]{1,0:T(8,128)(2,1)} %bitcast.25, bf16[256,2304]{1,0:T(8,128)(2,1)S(1)} %collective-permute-done.a_far, bf16[256,1024]{1,0:T(8,128)(2,1)S(1)} %get-tuple-element.68.c_own, ...), custom_call_target="tpu_custom_call" | custom-call | flops 2415919104 | bytes 12582912 | tf_op jit(solution)/shard_map/pallas_call | solution.py:31
  74.3 1.6 collective-permute-start.20
  75.9 1.7 collective-permute-start.21
  79.3 2.9 %collective-permute-start.4 = (bf16[144,1024]{1,0:T(8,128)(2,1)S(1)}, bf16[144,1024]{1,0:T(8,128)(2,1)S(1)}, u32[]{:S(2)}, u32[]{:S(2)}) collective-permute-start(bf16[144,1024]{1,0:T(8,128)(2,1)S(1)} %get-tuple-element.41), channel_id=1, source_target_pairs={{0,6},{1,7},{2,0},{3,1},{4,2},{5,3},{6,4},{7,5},{8,14},{9,15},{10,... | collective-permute-start | bytes 884744 | tf_op jit(solution)/shard_map/ppermute | solution.py:27
  82.2 22.1 %collective-permute-done.20.wm = bf16[288,2048]{1,0:T(8,128)(2,1)S(1)} collective-permute-done((bf16[288,2048]{1,0:T(8,128)(2,1)S(1)}, bf16[288,2048]{1,0:T(8,128)(2,1)S(1)}, u32[]{:S(2)}, u32[]{:S(2)}) %collective-permute-start.20) | collective-permute-done | bytes 1179680 | tf_op jit(solution)/shard_map/ppermute | solution.py:27
  104.8 5.9 %collective-permute-done.3.up = bf16[144,1024]{1,0:T(8,128)(2,1)S(1)} collective-permute-done((bf16[144,1024]{1,0:T(8,128)(2,1)S(1)}, bf16[144,1024]{1,0:T(8,128)(2,1)S(1)}, u32[]{:S(2)}, u32[]{:S(2)}) %collective-permute-start.3) | collective-permute-done | bytes 294944 | tf_op jit(solution)/shard_map/ppermute | solution.py:27
  111.2 2.2 %shard_map.121 = (bf16[288,1024]{1,0:T(8,128)(2,1)S(1)}, bf16[288,1024]{1,0:T(8,128)(2,1)S(1)}) custom-call(s32[4]{0:T(128)S(1)} %pad_add_fusion.place, bf16[4,288,1024]{2,1,0:T(8,128)(2,1)S(1)} %get-tuple-element.38.mine.mine_up.mine_down.rest_0_, bf16[4,288,1024]{2,1,0:T(8,128)(2,1)} %copy-done.1, ...), custom_call_target="tpu_custom_call" | custom-call | bytes 4194304 | tf_op jit(solution)/shard_map/pallas_call | solution.py:31
  114.0 9.3 %collective-permute-done.22.w2a = bf16[144,2048]{1,0:T(8,128)(2,1)S(1)} collective-permute-done((bf16[144,2048]{1,0:T(8,128)(2,1)S(1)}, bf16[144,2048]{1,0:T(8,128)(2,1)S(1)}, u32[]{:S(2)}, u32[]{:S(2)}) %collective-permute-start.22) | collective-permute-done | bytes 589856 | tf_op jit(solution)/shard_map/ppermute | solution.py:27
  123.3 1.6 collective-permute-start.6
  127.6 7.8 %collective-permute-done.5.up.rest_2_ = bf16[288,1024]{1,0:T(8,128)(2,1)S(1)} collective-permute-done((bf16[288,1024]{1,0:T(8,128)(2,1)S(1)}, bf16[288,1024]{1,0:T(8,128)(2,1)S(1)}, u32[]{:S(2)}, u32[]{:S(2)}) %collective-permute-start.5) | collective-permute-done | bytes 589856 | tf_op jit(solution)/shard_map/ppermute | solution.py:27
  135.8 3.8 %collective-permute-done.6.down.rest_3_ = bf16[288,1024]{1,0:T(8,128)(2,1)S(1)} collective-permute-done((bf16[288,1024]{1,0:T(8,128)(2,1)S(1)}, bf16[288,1024]{1,0:T(8,128)(2,1)S(1)}, u32[]{:S(2)}, u32[]{:S(2)}) %collective-permute-start.6) | collective-permute-done | bytes 589856 | tf_op jit(solution)/shard_map/ppermute | solution.py:27
  139.6 2.8 %collective-permute-start.17 = (bf16[144,1024]{1,0:T(8,128)(2,1)S(1)}, bf16[144,1024]{1,0:T(8,128)(2,1)S(1)}, u32[]{:S(2)}, u32[]{:S(2)}) collective-permute-start(bf16[144,1024]{1,0:T(8,128)(2,1)S(1)} %get-tuple-element.51), channel_id=1, source_target_pairs={{0,6},{1,7},{2,0},{3,1},{4,2},{5,3},{6,4},{7,5},{8,14},{9,15},{10,... | collective-permute-start | bytes 884744 | tf_op jit(solution)/shard_map/ppermute | solution.py:27
  142.4 5.7 %shard_map.122 = (f32[288,256]{1,0:T(8,128)S(1)}, bf16[288,256]{1,0:T(8,128)(2,1)S(1)}, bf16[288,256]{1,0:T(8,128)(2,1)S(1)}, bf16[288,256]{1,0:T(8,128)(2,1)S(1)}) custom-call(s32[4]{0:T(128)S(1)} %pad_add_fusion.place, f32[288,2,1024]{2,1,0:T(2,128)S(1)} %bitcast.22, f32[288,2,1024]{2,1,0:T(2,128)} %bitcast.27, f32[288,2,1024]{2,1,0:T(2,128)} %bitcast.29, ...), custom_call_target="tpu_custom_call" | custom-call | bytes 10485760 | tf_op jit(solution)/shard_map/pallas_call | solution.py:31
  148.1 4.1 %collective-permute-done.23.w2b = bf16[144,2048]{1,0:T(8,128)(2,1)S(1)} collective-permute-done((bf16[144,2048]{1,0:T(8,128)(2,1)S(1)}, bf16[144,2048]{1,0:T(8,128)(2,1)S(1)}, u32[]{:S(2)}, u32[]{:S(2)}) %collective-permute-start.23) | collective-permute-done | bytes 589856 | tf_op jit(solution)/shard_map/ppermute | solution.py:27
  152.2 2.0 collective-permute-start.7
  154.2 3.6 %collective-permute-start.8 = (bf16[288,256]{1,0:T(8,128)(2,1)S(1)}, bf16[288,256]{1,0:T(8,128)(2,1)S(1)}, u32[]{:S(2)}, u32[]{:S(2)}) collective-permute-start(bf16[288,256]{1,0:T(8,128)(2,1)S(1)} %get-tuple-element.46), channel_id=1, source_target_pairs={{0,32},{1,33},{2,34},{3,35},{4,36},{5,37},{6,38},{7,39},{8,40},{9,... | collective-permute-start | bytes 442376 | tf_op jit(solution)/shard_map/ppermute | solution.py:27
  158.8 7.2 %shard_map.128 = (bf16[256,1152]{1,0:T(8,128)(2,1)S(1)}, bf16[256,1152]{1,0:T(8,128)(2,1)S(1)}) custom-call(s32[4]{0:T(128)S(1)} %pad_add_fusion.place, bf16[288,2048]{1,0:T(8,128)(2,1)} %bitcast.34, bf16[288,2048]{1,0:T(8,128)(2,1)} %copy-done.11, bf16[288,2048]{1,0:T(8,128)(2,1)} %collective-permute-done.21.wp, ...), custom_call_target="tpu_custom_call" | custom-call | flops 2415919104 | bytes 8388608 | tf_op jit(solution)/shard_map/pallas_call | solution.py:31
  166.0 3.3 %collective-permute-start.26 = (bf16[256,1152]{1,0:T(8,128)(2,1)S(1)}, bf16[256,1152]{1,0:T(8,128)(2,1)S(1)}, u32[]{:S(2)}, u32[]{:S(2)}) collective-permute-start(bf16[256,1152]{1,0:T(8,128)(2,1)S(1)} %get-tuple-element.63), channel_id=1, source_target_pairs={{0,8},{1,9},{2,10},{3,11},{4,12},{5,13},{6,14},{7,15},{8,0},{9,1},... | collective-permute-start | bytes 1769480 | tf_op jit(solution)/shard_map/ppermute | solution.py:27
  169.3 2.2 %shard_map.125 = (bf16[288,1024]{1,0:T(8,128)(2,1)S(1)}, bf16[288,1024]{1,0:T(8,128)(2,1)S(1)}) custom-call(s32[4]{0:T(128)S(1)} %pad_add_fusion.place, bf16[4,288,1024]{2,1,0:T(8,128)(2,1)S(1)} %get-tuple-element.48.mine.mine_up.mine_down.rest_4_, bf16[4,288,1024]{2,1,0:T(8,128)(2,1)} %copy-done.3, ...), custom_call_target="tpu_custom_call" | custom-call | bytes 4194304 | tf_op jit(solution)/shard_map/pallas_call | solution.py:31
  171.8 3.0 %collective-permute-start.19 = (bf16[288,1024]{1,0:T(8,128)(2,1)S(1)}, bf16[288,1024]{1,0:T(8,128)(2,1)S(1)}, u32[]{:S(2)}, u32[]{:S(2)}) collective-permute-start(bf16[288,1024]{1,0:T(8,128)(2,1)S(1)} %get-tuple-element.53), channel_id=1, source_target_pairs={{0,6},{1,7},{2,0},{3,1},{4,2},{5,3},{6,4},{7,5},{8,14},{9,15},{10,... | collective-permute-start | bytes 1769480 | tf_op jit(solution)/shard_map/ppermute | solution.py:27
  175.9 7.2 %shard_map.129 = (bf16[256,1152]{1,0:T(8,128)(2,1)S(1)}, bf16[256,1152]{1,0:T(8,128)(2,1)S(1)}) custom-call(s32[4]{0:T(128)S(1)} %pad_add_fusion.place, bf16[288,2048]{1,0:T(8,128)(2,1)} %bitcast.35, bf16[288,2048]{1,0:T(8,128)(2,1)} %copy-done.11, bf16[288,2048]{1,0:T(8,128)(2,1)} %collective-permute-done.21.wp, ...), custom_call_target="tpu_custom_call" | custom-call | flops 2415919104 | bytes 8388608 | tf_op jit(solution)/shard_map/pallas_call | solution.py:31
  183.0 11.4 %collective-permute-done.10 = bf16[288,256]{1,0:T(8,128)(2,1)S(1)} collective-permute-done((bf16[288,256]{1,0:T(8,128)(2,1)S(1)}, bf16[288,256]{1,0:T(8,128)(2,1)S(1)}, u32[]{:S(2)}, u32[]{:S(2)}) %collective-permute-start.10) | collective-permute-done | bytes 147488 | tf_op jit(solution)/shard_map/ppermute | solution.py:27
  195.0 2.8 %collective-permute-start.12 = (bf16[288,256]{1,0:T(8,128)(2,1)S(1)}, bf16[288,256]{1,0:T(8,128)(2,1)S(1)}, u32[]{:S(2)}, u32[]{:S(2)}) collective-permute-start(bf16[288,256]{1,0:T(8,128)(2,1)S(1)} %multiply_convert_fusion.m0), channel_id=1, source_target_pairs={{0,32},{1,33},{2,34},{3,35},{4,36},{5,37},{6,38},{7,39},{8,40},{9,... | collective-permute-start | bytes 442376 | tf_op jit(solution)/shard_map/ppermute | solution.py:27
  197.8 7.3 %shard_map.126 = (f32[288,2,1024]{2,1,0:T(2,128)}, f32[288,2,1024]{2,1,0:T(2,128)}, f32[288,1024]{1,0:T(8,128)S(1)}) custom-call(s32[4]{0:T(128)S(1)} %pad_add_fusion.place, f32[288,2,1024]{2,1,0:T(2,128)S(1)} %bitcast.23, f32[288,2,1024]{2,1,0:T(2,128)} %bitcast.28, f32[288,2,1024]{2,1,0:T(2,128)} %bitcast.30, bf16[4,288,1024]{2,1,0:T(8,128)(2,1)} %copy-done, ...), custom_call_target="tpu_custom_call" | custom-call | bytes 16777216 | tf_op jit(solution)/shard_map/pallas_call | solution.py:31
  205.1 3.2 %shard_map.130 = bf16[256,4608]{1,0:T(8,128)(2,1)} custom-call(s32[4]{0:T(128)S(1)} %pad_add_fusion.place, bf16[256,1152]{1,0:T(8,128)(2,1)S(1)} %get-tuple-element.65.near, bf16[256,1152]{1,0:T(8,128)(2,1)S(1)} %collective-permute-done.26.far, bf16[256,1152]{1,0:T(8,128)(2,1)S(1)} %collective-permute-done.27.near_other, ...), custom_call_target="tpu_custom_call" | custom-call | bytes 5242880 | tf_op jit(solution)/shard_map/pallas_call | solution.py:31
  208.3 3.1 %shard_map.127 = (f32[288,2,1024]{2,1,0:T(2,128)}, f32[288,1024]{1,0:T(8,128)}, f32[288,1024]{1,0:T(8,128)}) custom-call(s32[4]{0:T(128)S(1)} %pad_add_fusion.place, bf16[288,256]{1,0:T(8,128)(2,1)S(1)} %multiply_convert_fusion.m0, bf16[288,256]{1,0:T(8,128)(2,1)S(1)} %collective-permute-done.11.m1, bf16[288,256]{1,0:T(8,128)(2,1)S(1)} %collective-permute-done.12.m2, ...), custom_call_target="tpu_custom_call" | custom-call | bytes 9437184 | tf_op jit(solution)/shard_map/pallas_call | solution.py:31
  (74 shorter events, 13.0 us)
Async XLA Ops:
  3.2 40.6 %collective-permute-start = (bf16[256,2304]{1,0:T(8,128)(2,1)S(1)}, bf16[256,2304]{1,0:T(8,128)(2,1)S(1)}, u32[]{:S(2)}, u32[]{:S(2)}) collective-permute-start(bf16[256,2304]{1,0:T(8,128)(2,1)S(1)} %shard_map.118), channel_id=1, source_target_pairs={{0,8},{1,9},{2,10},{3,11},{4,12},{5,13},{6,14},{7,15},{8,0},{9,1},... | collective-permute-start | bytes 3538952 | tf_op jit(solution)/shard_map/ppermute | solution.py:27
  9.1 34.7 %collective-permute-start.1 = (bf16[256,1024]{1,0:T(8,128)(2,1)S(1)}, bf16[256,1024]{1,0:T(8,128)(2,1)S(1)}, u32[]{:S(2)}, u32[]{:S(2)}) collective-permute-start(bf16[256,1024]{1,0:T(8,128)(2,1)S(1)} %get-tuple-element.69.c_own), channel_id=1, source_target_pairs={{0,8},{1,9},{2,10},{3,11},{4,12},{5,13},{6,14},{7,15},{8,0},{9,1},... | collective-permute-start | bytes 1572872 | tf_op jit(solution)/shard_map/ppermute | solution.py:27
  51.0 60.1 %copy-start = (bf16[4,288,1024]{2,1,0:T(8,128)(2,1)}, bf16[4,288,1024]{2,1,0:T(8,128)(2,1)S(1)}, u32[]{:S(2)}) copy-start(bf16[4,288,1024]{2,1,0:T(8,128)(2,1)S(1)} %get-tuple-element.38.mine.mine_up.mine_down.rest_0_) | copy-start | bytes 7077892
  51.0 26.6 %collective-permute-start.2 = (bf16[4,288,1024]{2,1,0:T(8,128)(2,1)}, bf16[4,288,1024]{2,1,0:T(8,128)(2,1)S(1)}, u32[]{:S(2)}, u32[]{:S(2)}) collective-permute-start(bf16[4,288,1024]{2,1,0:T(8,128)(2,1)} %get-tuple-element.39), channel_id=1, source_target_pairs={{0,1},{1,0},{2,3},{3,2},{4,5},{5,4},{6,7},{7,6},{8,9},{9,8},{10,11... | collective-permute-start | bytes 7077896 | tf_op jit(solution)/shard_map/ppermute | solution.py:27
  51.1 23.1 %copy-start.9 = (bf16[36,8,2,1024]{3,1,2,0:T(8,128)(2,1)S(1)}, bf16[36,8,2,1024]{3,1,2,0:T(8,128)(2,1)}, u32[]{:S(2)}) copy-start(bf16[36,8,2,1024]{3,1,2,0:T(8,128)(2,1)} %copy.14) | copy-start | bytes 3538948
  51.1 15.8 %collective-permute-start.14 = (bf16[256,1024]{1,0:T(8,128)(2,1)S(1)}, bf16[256,1024]{1,0:T(8,128)(2,1)S(1)}, u32[]{:S(2)}, u32[]{:S(2)}) collective-permute-start(bf16[256,1024]{1,0:T(8,128)(2,1)S(1)} %get-tuple-element.68.c_own), channel_id=1, source_target_pairs={{0,8},{1,9},{2,10},{3,11},{4,12},{5,13},{6,14},{7,15},{8,0},{9,1},... | collective-permute-start | bytes 1572872 | tf_op jit(solution)/shard_map/ppermute | solution.py:27
  74.2 95.1 %copy-start.2 = (bf16[4,288,1024]{2,1,0:T(8,128)(2,1)}, bf16[4,288,1024]{2,1,0:T(8,128)(2,1)S(1)}, u32[]{:S(2)}) copy-start(bf16[4,288,1024]{2,1,0:T(8,128)(2,1)S(1)} %get-tuple-element.48.mine.mine_up.mine_down.rest_4_) | copy-start | bytes 7077892
  74.2 51.8 %collective-permute-start.15 = (bf16[4,288,1024]{2,1,0:T(8,128)(2,1)}, bf16[4,288,1024]{2,1,0:T(8,128)(2,1)S(1)}, u32[]{:S(2)}, u32[]{:S(2)}) collective-permute-start(bf16[4,288,1024]{2,1,0:T(8,128)(2,1)} %get-tuple-element.49), channel_id=1, source_target_pairs={{0,1},{1,0},{2,3},{3,2},{4,5},{5,4},{6,7},{7,6},{8,9},{9,8},{10,11... | collective-permute-start | bytes 7077896 | tf_op jit(solution)/shard_map/ppermute | solution.py:27
  74.3 30.1 %collective-permute-start.20 = (bf16[288,2048]{1,0:T(8,128)(2,1)S(1)}, bf16[288,2048]{1,0:T(8,128)(2,1)S(1)}, u32[]{:S(2)}, u32[]{:S(2)}) collective-permute-start(bf16[288,2048]{1,0:T(8,128)(2,1)S(1)} %bitcast.36), channel_id=1, source_target_pairs={{0,2},{1,3},{2,4},{3,5},{4,6},{5,7},{6,0},{7,1},{8,10},{9,11},{10,... | collective-permute-start | bytes 3538952 | tf_op jit(solution)/shard_map/ppermute | solution.py:27
  75.9 37.5 %collective-permute-start.21 = (bf16[288,2048]{1,0:T(8,128)(2,1)S(1)}, bf16[288,2048]{1,0:T(8,128)(2,1)}, u32[]{:S(2)}, u32[]{:S(2)}) collective-permute-start(bf16[288,2048]{1,0:T(8,128)(2,1)S(1)} %bitcast.37), channel_id=1, source_target_pairs={{0,6},{1,7},{2,0},{3,1},{4,2},{5,3},{6,4},{7,5},{8,14},{9,15},{10,... | collective-permute-start | bytes 3538952 | tf_op jit(solution)/shard_map/ppermute | solution.py:27
  79.0 31.7 %collective-permute-start.3 = (bf16[144,1024]{1,0:T(8,128)(2,1)S(1)}, bf16[144,1024]{1,0:T(8,128)(2,1)S(1)}, u32[]{:S(2)}, u32[]{:S(2)}) collective-permute-start(bf16[144,1024]{1,0:T(8,128)(2,1)S(1)} %get-tuple-element.40), channel_id=1, source_target_pairs={{0,2},{1,3},{2,4},{3,5},{4,6},{5,7},{6,0},{7,1},{8,10},{9,11},{10,... | collective-permute-start | bytes 884744 | tf_op jit(solution)/shard_map/ppermute | solution.py:27
  79.3 31.3 %collective-permute-start.4 = (bf16[144,1024]{1,0:T(8,128)(2,1)S(1)}, bf16[144,1024]{1,0:T(8,128)(2,1)S(1)}, u32[]{:S(2)}, u32[]{:S(2)}) collective-permute-start(bf16[144,1024]{1,0:T(8,128)(2,1)S(1)} %get-tuple-element.41), channel_id=1, source_target_pairs={{0,6},{1,7},{2,0},{3,1},{4,2},{5,3},{6,4},{7,5},{8,14},{9,15},{10,... | collective-permute-start | bytes 884744 | tf_op jit(solution)/shard_map/ppermute | solution.py:27
  104.4 18.9 %collective-permute-start.22 = (bf16[144,2048]{1,0:T(8,128)(2,1)S(1)}, bf16[144,2048]{1,0:T(8,128)(2,1)S(1)}, u32[]{:S(2)}, u32[]{:S(2)}) collective-permute-start(bf16[144,2048]{1,0:T(8,128)(2,1)S(1)} %slice.18), channel_id=1, source_target_pairs={{0,2},{1,3},{2,4},{3,5},{4,6},{5,7},{6,0},{7,1},{8,10},{9,11},{10,... | collective-permute-start | bytes 1769480 | tf_op jit(solution)/shard_map/ppermute | solution.py:27
  110.6 43.5 %collective-permute-start.25 = (bf16[512,1024]{1,0:T(8,128)(2,1)}, bf16[512,1024]{1,0:T(8,128)(2,1)S(1)}, u32[]{:S(2)}, u32[]{:S(2)}) collective-permute-start(bf16[512,1024]{1,0:T(8,128)(2,1)} %get-tuple-element.62.v0), channel_id=1, source_target_pairs={{0,1},{1,0},{2,3},{3,2},{4,5},{5,4},{6,7},{7,6},{8,9},{9,8},{10,11... | collective-permute-start | bytes 3145736 | tf_op jit(solution)/shard_map/ppermute | solution.py:27
  110.7 47.1 %collective-permute-start.24 = (bf16[512,1024]{1,0:T(8,128)(2,1)S(1)}, bf16[512,1024]{1,0:T(8,128)(2,1)S(1)}, u32[]{:S(2)}, u32[]{:S(2)}) collective-permute-start(bf16[512,1024]{1,0:T(8,128)(2,1)S(1)} %get-tuple-element.61.k0), channel_id=1, source_target_pairs={{0,1},{1,0},{2,3},{3,2},{4,5},{5,4},{6,7},{7,6},{8,9},{9,8},{10,11... | collective-permute-start | bytes 3145736 | tf_op jit(solution)/shard_map/ppermute | solution.py:27
  113.4 22.1 %collective-permute-start.5 = (bf16[288,1024]{1,0:T(8,128)(2,1)S(1)}, bf16[288,1024]{1,0:T(8,128)(2,1)S(1)}, u32[]{:S(2)}, u32[]{:S(2)}) collective-permute-start(bf16[288,1024]{1,0:T(8,128)(2,1)S(1)} %get-tuple-element.42), channel_id=1, source_target_pairs={{0,2},{1,3},{2,4},{3,5},{4,6},{5,7},{6,0},{7,1},{8,10},{9,11},{10,... | collective-permute-start | bytes 1769480 | tf_op jit(solution)/shard_map/ppermute | solution.py:27
  123.3 16.3 %collective-permute-start.6 = (bf16[288,1024]{1,0:T(8,128)(2,1)S(1)}, bf16[288,1024]{1,0:T(8,128)(2,1)S(1)}, u32[]{:S(2)}, u32[]{:S(2)}) collective-permute-start(bf16[288,1024]{1,0:T(8,128)(2,1)S(1)} %get-tuple-element.43), channel_id=1, source_target_pairs={{0,6},{1,7},{2,0},{3,1},{4,2},{5,3},{6,4},{7,5},{8,14},{9,15},{10,... | collective-permute-start | bytes 1769480 | tf_op jit(solution)/shard_map/ppermute | solution.py:27
  126.0 26.2 %collective-permute-start.23 = (bf16[144,2048]{1,0:T(8,128)(2,1)S(1)}, bf16[144,2048]{1,0:T(8,128)(2,1)S(1)}, u32[]{:S(2)}, u32[]{:S(2)}) collective-permute-start(bf16[144,2048]{1,0:T(8,128)(2,1)S(1)} %slice.19), channel_id=1, source_target_pairs={{0,6},{1,7},{2,0},{3,1},{4,2},{5,3},{6,4},{7,5},{8,14},{9,15},{10,... | collective-permute-start | bytes 1769480 | tf_op jit(solution)/shard_map/ppermute | solution.py:27
  135.5 30.5 %collective-permute-start.16 = (bf16[144,1024]{1,0:T(8,128)(2,1)S(1)}, bf16[144,1024]{1,0:T(8,128)(2,1)S(1)}, u32[]{:S(2)}, u32[]{:S(2)}) collective-permute-start(bf16[144,1024]{1,0:T(8,128)(2,1)S(1)} %get-tuple-element.50), channel_id=1, source_target_pairs={{0,2},{1,3},{2,4},{3,5},{4,6},{5,7},{6,0},{7,1},{8,10},{9,11},{10,... | collective-permute-start | bytes 884744 | tf_op jit(solution)/shard_map/ppermute | solution.py:27
  139.6 29.7 %collective-permute-start.17 = (bf16[144,1024]{1,0:T(8,128)(2,1)S(1)}, bf16[144,1024]{1,0:T(8,128)(2,1)S(1)}, u32[]{:S(2)}, u32[]{:S(2)}) collective-permute-start(bf16[144,1024]{1,0:T(8,128)(2,1)S(1)} %get-tuple-element.51), channel_id=1, source_target_pairs={{0,6},{1,7},{2,0},{3,1},{4,2},{5,3},{6,4},{7,5},{8,14},{9,15},{10,... | collective-permute-start | bytes 884744 | tf_op jit(solution)/shard_map/ppermute | solution.py:27
  152.2 19.3 %collective-permute-start.7 = (bf16[288,256]{1,0:T(8,128)(2,1)S(1)}, bf16[288,256]{1,0:T(8,128)(2,1)S(1)}, u32[]{:S(2)}, u32[]{:S(2)}) collective-permute-start(bf16[288,256]{1,0:T(8,128)(2,1)S(1)} %get-tuple-element.45), channel_id=1, source_target_pairs={{0,16},{1,17},{2,18},{3,19},{4,20},{5,21},{6,22},{7,23},{8,24},{9,... | collective-permute-start | bytes 442376 | tf_op jit(solution)/shard_map/ppermute | solution.py:27
  154.2 17.7 %collective-permute-start.8 = (bf16[288,256]{1,0:T(8,128)(2,1)S(1)}, bf16[288,256]{1,0:T(8,128)(2,1)S(1)}, u32[]{:S(2)}, u32[]{:S(2)}) collective-permute-start(bf16[288,256]{1,0:T(8,128)(2,1)S(1)} %get-tuple-element.46), channel_id=1, source_target_pairs={{0,32},{1,33},{2,34},{3,35},{4,36},{5,37},{6,38},{7,39},{8,40},{9,... | collective-permute-start | bytes 442376 | tf_op jit(solution)/shard_map/ppermute | solution.py:27
  157.8 17.0 %collective-permute-start.9 = (bf16[288,256]{1,0:T(8,128)(2,1)S(1)}, bf16[288,256]{1,0:T(8,128)(2,1)S(1)}, u32[]{:S(2)}, u32[]{:S(2)}) collective-permute-start(bf16[288,256]{1,0:T(8,128)(2,1)S(1)} %get-tuple-element.47), channel_id=1, source_target_pairs={{0,48},{1,49},{2,50},{3,51},{4,52},{5,53},{6,54},{7,55},{8,56},{9,... | collective-permute-start | bytes 442376 | tf_op jit(solution)/shard_map/ppermute | solution.py:27
  166.0 28.6 %collective-permute-start.26 = (bf16[256,1152]{1,0:T(8,128)(2,1)S(1)}, bf16[256,1152]{1,0:T(8,128)(2,1)S(1)}, u32[]{:S(2)}, u32[]{:S(2)}) collective-permute-start(bf16[256,1152]{1,0:T(8,128)(2,1)S(1)} %get-tuple-element.63), channel_id=1, source_target_pairs={{0,8},{1,9},{2,10},{3,11},{4,12},{5,13},{6,14},{7,15},{8,0},{9,1},... | collective-permute-start | bytes 1769480 | tf_op jit(solution)/shard_map/ppermute | solution.py:27
  169.3 35.8 %collective-permute-start.28 = (bf16[256,1152]{1,0:T(8,128)(2,1)S(1)}, bf16[256,1152]{1,0:T(8,128)(2,1)S(1)}, u32[]{:S(2)}, u32[]{:S(2)}) collective-permute-start(bf16[256,1152]{1,0:T(8,128)(2,1)S(1)} %get-tuple-element.67), channel_id=1, source_target_pairs={{0,9},{1,8},{2,11},{3,10},{4,13},{5,12},{6,15},{7,14},{8,1},{9,0},... | collective-permute-start | bytes 1769480 | tf_op jit(solution)/shard_map/ppermute | solution.py:27
  171.5 23.5 %collective-permute-start.18 = (bf16[288,1024]{1,0:T(8,128)(2,1)S(1)}, bf16[288,1024]{1,0:T(8,128)(2,1)S(1)}, u32[]{:S(2)}, u32[]{:S(2)}) collective-permute-start(bf16[288,1024]{1,0:T(8,128)(2,1)S(1)} %get-tuple-element.52), channel_id=1, source_target_pairs={{0,2},{1,3},{2,4},{3,5},{4,6},{5,7},{6,0},{7,1},{8,10},{9,11},{10,... | collective-permute-start | bytes 1769480 | tf_op jit(solution)/shard_map/ppermute | solution.py:27
  171.8 25.9 %collective-permute-start.19 = (bf16[288,1024]{1,0:T(8,128)(2,1)S(1)}, bf16[288,1024]{1,0:T(8,128)(2,1)S(1)}, u32[]{:S(2)}, u32[]{:S(2)}) collective-permute-start(bf16[288,1024]{1,0:T(8,128)(2,1)S(1)} %get-tuple-element.53), channel_id=1, source_target_pairs={{0,6},{1,7},{2,0},{3,1},{4,2},{5,3},{6,4},{7,5},{8,14},{9,15},{10,... | collective-permute-start | bytes 1769480 | tf_op jit(solution)/shard_map/ppermute | solution.py:27
  174.9 19.6 %collective-permute-start.10 = (bf16[288,256]{1,0:T(8,128)(2,1)S(1)}, bf16[288,256]{1,0:T(8,128)(2,1)S(1)}, u32[]{:S(2)}, u32[]{:S(2)}) collective-permute-start(bf16[288,256]{1,0:T(8,128)(2,1)S(1)} %fusion), channel_id=1, source_target_pairs={{0,64},{1,65},{2,66},{3,67},{4,68},{5,69},{6,70},{7,71},{8,72},{9,... | collective-permute-start | bytes 442376 | tf_op jit(solution)/shard_map/ppermute | solution.py:27
  194.5 10.6 %collective-permute-start.27 = (bf16[256,1152]{1,0:T(8,128)(2,1)S(1)}, bf16[256,1152]{1,0:T(8,128)(2,1)S(1)}, u32[]{:S(2)}, u32[]{:S(2)}) collective-permute-start(bf16[256,1152]{1,0:T(8,128)(2,1)S(1)} %get-tuple-element.66), channel_id=1, source_target_pairs={{0,1},{1,0},{2,3},{3,2},{4,5},{5,4},{6,7},{7,6},{8,9},{9,8},{10,11... | collective-permute-start | bytes 1769480 | tf_op jit(solution)/shard_map/ppermute | solution.py:27
  194.6 13.7 %collective-permute-start.11 = (bf16[288,256]{1,0:T(8,128)(2,1)S(1)}, bf16[288,256]{1,0:T(8,128)(2,1)S(1)}, u32[]{:S(2)}, u32[]{:S(2)}) collective-permute-start(bf16[288,256]{1,0:T(8,128)(2,1)S(1)} %multiply_convert_fusion.m0), channel_id=1, source_target_pairs={{0,48},{1,49},{2,50},{3,51},{4,52},{5,53},{6,54},{7,55},{8,56},{9,... | collective-permute-start | bytes 442376 | tf_op jit(solution)/shard_map/ppermute | solution.py:27
  195.0 13.3 %collective-permute-start.12 = (bf16[288,256]{1,0:T(8,128)(2,1)S(1)}, bf16[288,256]{1,0:T(8,128)(2,1)S(1)}, u32[]{:S(2)}, u32[]{:S(2)}) collective-permute-start(bf16[288,256]{1,0:T(8,128)(2,1)S(1)} %multiply_convert_fusion.m0), channel_id=1, source_target_pairs={{0,32},{1,33},{2,34},{3,35},{4,36},{5,37},{6,38},{7,39},{8,40},{9,... | collective-permute-start | bytes 442376 | tf_op jit(solution)/shard_map/ppermute | solution.py:27
  197.8 10.5 %collective-permute-start.13 = (bf16[288,256]{1,0:T(8,128)(2,1)S(1)}, bf16[288,256]{1,0:T(8,128)(2,1)S(1)}, u32[]{:S(2)}, u32[]{:S(2)}) collective-permute-start(bf16[288,256]{1,0:T(8,128)(2,1)S(1)} %multiply_convert_fusion.m0), channel_id=1, source_target_pairs={{0,16},{1,17},{2,18},{3,19},{4,20},{5,21},{6,22},{7,23},{8,24},{9,... | collective-permute-start | bytes 442376 | tf_op jit(solution)/shard_map/ppermute | solution.py:27
  (10 other events, 51.8 us)
where the time goes:
time: 213 us; the launch traced here: 211 us
  waiting for transfers between devices  111 us (52%)
  Pallas kernels  54.6 us (26%)
  starting transfers between devices  38.2 us (18%)
  local copies, waits for them, and re-layouts  5.39 us (3%)
    ppermute x29, waiting for transfers between devices, shift(): return lax.ppermute(value, AXES, pairs)  111 us
    pallas_call x13, Pallas kernels, call(): pl.pallas_call(kernel, out_shape=out_shape, grid_spec=pltpu.PrefetchScala...  54.6 us
    ppermute x29, starting transfers between devices, shift(): return lax.ppermute(value, AXES, pairs)  38.2 us
  transfers between devices with their start and end apart: 29, of which 9 were waited for; matrix products, arithmetic and copies ran while one was open for 2% of the time, Pallas kernels for 21%

commit v1 on v0

v1 whole, which is shorter than its diff:
```python
import jax
import jax.numpy as jnp
import numpy as np
from jax import lax
from jax.experimental import pallas as pl
from jax.experimental.pallas import tpu as pltpu
from jax.sharding import Mesh
from jax.sharding import PartitionSpec as P

CORRECT_FIRST = 1.0 - 0.9**8
CORRECT_SECOND = 1.0 - 0.95**8
AXES = ("ylo", "z", "yhi", "x", "core")
SIZES = (2, 4, 2, 4, 2)
BF16 = jnp.bfloat16
F32 = jnp.float32
ANY = pl.BlockSpec(memory_space=pl.ANY)
HBM = pl.BlockSpec(memory_space=pltpu.HBM)
WEIGHT = 50


def shift(value, **steps):
    pairs = []
    for source in np.ndindex(*SIZES):
        target = [(s + steps.get(a, 0)) % n for s, a, n in zip(source, AXES, SIZES)]
        pairs.append(
            (int(np.ravel_multi_index(source, SIZES)), int(np.ravel_multi_index(target, SIZES)))
        )
    return lax.ppermute(value, AXES, pairs)


def call(
    kernel, out_shape, place, inputs, in_specs, out_specs, scratch=(), grid=(1,), flops=0, moved=0, weight=0, alias=None, vmem=12
):
    return pl.pallas_call(
        kernel,
        out_shape=out_shape,
        grid_spec=pltpu.PrefetchScalarGridSpec(
            num_scalar_prefetch=1,
            grid=grid,
            in_specs=in_specs,
            out_specs=out_specs,
            scratch_shapes=list(scratch),
        ),
        compiler_params=pltpu.CompilerParams(vmem_limit_bytes=vmem * 2**20),
        input_output_aliases=alias or {},
        cost_estimate=pl.CostEstimate(flops=weight * 10**9, bytes_accessed=weight * 10**7, transcendentals=0),
    )(place, *inputs)


def after(value, *others):
    return lax.optimization_barrier((value, *others))[0]


def shape(dims, dtype=BF16):
    return jax.ShapeDtypeStruct(dims, dtype)


def far_half_kernel(place, acts, out, sem):
    n = out.shape[1]
    copy = pltpu.make_async_copy(
        acts.at[:, pl.ds(pl.multiple_of((1 - place[0]) * n, 128), n)], out, sem
    )
    copy.start()
    copy.wait()


def stack_kernel(place, *refs):
    out = refs[-1]
    n = 0
    for ref in refs[:-1]:
        out[n : n + ref.shape[0]] = ref[...]
        n += ref.shape[0]


def gradient_kernel(place, acts, a_far, c_own, c_far, mine, other, a_s, c_s, g_s, in_sem, out_sem):
    h, c = place[0], place[1]
    tok, wide = a_far.shape
    rows = mine.shape[1]
    copies = [
        pltpu.make_async_copy(
            acts.at[:, pl.ds(pl.multiple_of(h * wide, 128), wide)],
            a_s.at[pl.ds(0, tok)],
            in_sem.at[0],
        ),
        pltpu.make_async_copy(a_far, a_s.at[pl.ds(tok, tok)], in_sem.at[1]),
        pltpu.make_async_copy(c_own, c_s.at[pl.ds(0, tok)], in_sem.at[2]),
        pltpu.make_async_copy(c_far, c_s.at[pl.ds(tok, tok)], in_sem.at[3]),
    ]
    for copy in copies:
        copy.start()
    for copy in copies:
        copy.wait()
    tile = 256
    sends = []
    for i in range(wide // tile):
        cols = slice(i * tile, (i + 1) * tile)
        g_s[cols, :] = lax.dot_general(
            a_s[:, cols], c_s[...], (((0,), (0,)), ((), ())), preferred_element_type=F32
        ).astype(BF16)
        ready = {4: (0, 1), 8: (2, 3)}.get(i, ())
        for core, out in ((1 - c, other), (c, mine)):
            for to in ready:
                start = pl.multiple_of((2 * to + core) * rows, 16)
                sends.append(
                    pltpu.make_async_copy(
                        g_s.at[pl.ds(start, rows)], out.at[to], out_sem.at[len(sends)]
                    )
                )
                sends[-1].start()
    for send in sends:
        send.wait()


def rounded_kernel(place, w, w_low, w_key):
    n = w.shape[2]
    key = w[:, 0, :]
    w_key[...] = key
    w_low[:, :n] = key.astype(BF16)
    w_low[:, n:] = w[:, 1, :].astype(BF16)


def planes_kernel(place, m, v, m_key, v_key):
    m_key[...] = m[:, 0, :]
    v_key[...] = v[:, 0, :]


def block_sum(mine, got):
    return mine[0].astype(F32) + got[0].astype(F32)


def first_hop_kernel(place, mine, got, up, down):
    part = block_sum(mine, got).astype(BF16)
    n = up.shape[0]
    up[...] = part[:n]
    down[...] = part[n:]


def second_hop_kernel(place, mine_up, got_up, mine_down, got_down, up, down, to_up, to_down):
    n = up.shape[0]
    part = block_sum(mine_up, got_up)
    to_up[:n] = (part[:n] + up[...].astype(F32)).astype(BF16)
    to_up[n:] = part[n:].astype(BF16)
    part = block_sum(mine_down, got_down)
    to_down[:n] = part[:n].astype(BF16)
    to_down[n:] = (part[n:] + down[...].astype(F32)).astype(BF16)


def owned_sum(mine, got, up, down):
    return block_sum(mine, got) + up[...].astype(F32) + down[...].astype(F32)


def adamw(w, m, v, g):
    m = 0.9 * m + 0.1 * g
    v = 0.95 * v + 0.05 * g * g
    step_dir = m / CORRECT_FIRST / (jnp.sqrt(v / CORRECT_SECOND) + 1e-08)
    return m, v, w - 0.01 * (step_dir + 0.1 * w)


def selected_kernel(place, w, m, v, mine, got, up, down, own, s1, s2, s3, sel):
    g = owned_sum(mine, got, up, down)
    sel[...] = adamw(w[...], m[...], v[...], g)[2]
    n = own.shape[1]
    for step, out in ((0, own), (1, s1), (2, s2), (3, s3)):
        start = pl.multiple_of(lax.rem(place[3] + step, 4) * n, 128)
        out[...] = sel[:, pl.ds(start, n)].astype(out.dtype)


def moments_kernel(place, w, m, v, *rest):
    parts, (first, second, inner) = (rest[:4], rest[4:8]), rest[8:]
    for f in range(2):
        g = owned_sum(*parts[f])
        m_new, v_new, inner_new = adamw(w[:, f, :], m[:, f, :], v[:, f, :], g)
        first[:, f, :] = m_new
        second[:, f, :] = v_new
    inner[...] = inner_new


def outer_kernel(place, m0, m1, m2, m3, anchor, momentum, inner, weights, anchor_new, momentum_new, mean):
    n = m0.shape[1]
    for step, part in enumerate((m0, m1, m2, m3)):
        start = pl.multiple_of(lax.rem(place[3] + step, 4) * n, 128)
        mean[:, pl.ds(start, n)] = part[...].astype(F32)
    delta = anchor[...] - mean[...]
    moved = 0.9 * momentum[...] + delta
    synced = anchor[...] - 0.7 * (delta + 0.9 * moved)
    momentum_new[...] = moved
    anchor_new[...] = synced
    weights[:, 0, :] = synced
    weights[:, 1, :] = inner[...]


def far_columns_kernel(place, far, near, out):
    out[...] = far[...]


def input_kernel(
    place, w013, w2a, w2b, v013, v2, k_near, v_near, k_far, v_far, near, far, w_s, c_s, o_s, sem, out_sem
):
    h, c, x = place[0], place[1], place[2]
    rows, feat = v2.shape[0], k_near.shape[1]
    part = w2a.shape[0]
    tok, wide = far.shape
    pieces = []
    for core, triple in ((c, w013), (1 - c, v013)):
        for n, step in enumerate((0, 1, 3)):
            pieces.append((core, step, 0, triple, n * rows, rows))
    pieces += [(c, 2, 0, w2a, 0, part), (c, 2, part, w2b, 0, part), (1 - c, 2, 0, v2, 0, rows)]
    copies = [[], []]
    for f in range(2):
        for core, step, low, piece, first, n in pieces:
            start = (2 * lax.rem(x + step, 4) + core) * rows + low
            copies[f].append(
                pltpu.make_async_copy(
                    piece.at[pl.ds(first, n), pl.ds(f * feat, feat)],
                    w_s.at[f, pl.ds(pl.multiple_of(start, 16), n)],
                    sem.at[9 * f + len(copies[f])],
                )
            )
    for n, tokens in enumerate((k_far, k_near, v_far, v_near)):
        copies[n // 2].append(
            pltpu.make_async_copy(
                tokens, c_s.at[n // 2, pl.ds(n % 2 * tok, tok)], sem.at[18 + n]
            )
        )
    for copy in copies[0] + copies[1]:
        copy.start()
    for copy in copies[0] + copies[1]:
        copy.wait()
    tile = 384
    dims = (((1,), (1,)), ((), ()))
    sends = []
    for j in range(wide // tile):
        cols = slice(j * tile, (j + 1) * tile)
        acc = lax.dot_general(c_s[0], w_s[0, cols, :], dims, preferred_element_type=F32)
        acc += lax.dot_general(c_s[1], w_s[1, cols, :], dims, preferred_element_type=F32)
        o_s[:, cols] = acc.astype(BF16)
        for b, (out, base) in enumerate(((far, 0), (near, h * wide))):
            sends.append(
                pltpu.make_async_copy(
                    o_s.at[pl.ds(b * tok, tok), pl.ds(j * tile, tile)],
                    out.at[:, pl.ds(pl.multiple_of(base + j * tile, 128), tile)],
                    out_sem.at[len(sends)],
                )
            )
            sends[-1].start()
    for send in sends:
        send.wait()


def shards(activations, cotangent, weights, first_moment, second_moment, anchor, momentum):
    acts = activations[0]
    tok, width = acts.shape
    weight_here = weights[0]
    rows = weight_here.shape[0]
    feat = weight_here.shape[2]
    ylo, z, h, x, c = [lax.axis_index(a) for a in AXES]
    place = jnp.stack([h, c, x, z]).astype(jnp.int32)
    hr = rows // 2

    def whole(*dims):
        return pl.BlockSpec(dims, lambda i, place: (0,) * len(dims))

    half_rows = pl.BlockSpec((hr, feat), lambda i, place: (i, 0))
    half_both = pl.BlockSpec((hr, 2, feat), lambda i, place: (i, 0, 0))
    a_send = call(
        far_half_kernel,
        shape((tok, width // 2)),
        place,
        (acts,),
        [ANY],
        ANY,
        [pltpu.SemaphoreType.DMA],
        moved=2 * tok * width,
    )
    a_far = shift(a_send, yhi=1)
    w0, w_key = call(
        rounded_kernel,
        [shape((rows, 2 * feat)), shape((rows, feat), F32)],
        place,
        (after(weight_here, a_send),),
        [half_both],
        [pl.BlockSpec((hr, 2 * feat), lambda i, place: (i, 0)), half_rows],
        grid=(2,),
        moved=5 * 2**20,
        weight=WEIGHT,
    )
    w1, w3 = shift(w0, x=-1), shift(w0, x=1)
    cot = after(cotangent, w0, a_send)[0]
    key, val = cot[:, 0, :], cot[:, 1, :]
    key_far = shift(key, yhi=1)

    m_key, v_key = call(
        planes_kernel,
        [shape((rows, feat), F32)] * 2,
        place,
        (after(first_moment, key)[0], second_moment[0]),
        [half_both] * 2,
        [half_rows] * 2,
        grid=(2,),
        moved=7 * 2**20,
        weight=WEIGHT,
    )
    planes = (w_key, m_key, v_key)
    val_far = shift(after(val, m_key), yhi=1)

    def partial(a, c_own, c_far):
        return call(
            gradient_kernel,
            [shape((4, rows, feat))] * 2,
            place,
            (acts, a, c_own, c_far),
            [HBM] * 4,
            [HBM] * 2,
            [
                pltpu.VMEM((2 * tok, width // 2), BF16),
                pltpu.VMEM((2 * tok, feat), BF16),
                pltpu.VMEM((width // 2, feat), BF16),
                pltpu.SemaphoreType.DMA((4,)),
                pltpu.SemaphoreType.DMA((8,)),
            ],
            flops=2 * tok * width * feat,
            moved=12 * 2**20,
            weight=WEIGHT,
            vmem=16,
        )

    def block(step):
        return pl.BlockSpec((1, rows, feat), lambda i, place: (lax.rem(place[2] + step, 4), 0, 0))

    def first_hop(mine, got):
        up, down = call(
            first_hop_kernel,
            [shape((hr, feat))] * 2,
            place,
            (mine, got),
            [block(2)] * 2,
            [whole(hr, feat)] * 2,
            moved=2**21,
        )
        return up, down

    def second_hop(mine, got, up, down, weight=0):
        return call(
            second_hop_kernel,
            [shape((rows, feat))] * 2,
            place,
            (mine, got, mine, got, up, down),
            [block(1), block(1), block(3), block(3), whole(hr, feat), whole(hr, feat)],
            [whole(rows, feat)] * 2,
            moved=2**22,
            weight=weight,
        )

    a_far, w1, w3, planes = lax.optimization_barrier((a_far, w1, w3, planes))
    def stack(*parts):
        total = sum(p.shape[0] for p in parts)
        return call(
            stack_kernel,
            shape((total, 2 * feat)),
            place,
            parts,
            [whole(*p.shape) for p in parts],
            whole(total, 2 * feat),
            moved=2 * 4 * total * feat,
            vmem=20,
        )

    w2a, w2b = shift(w3[:hr], x=1), shift(w1[hr:], x=-1)
    w013 = stack(w0, w1, w3)
    v013 = shift(w013, core=1)
    mine0, other0 = partial(a_far, key, key_far)
    got0 = shift(other0, core=1)
    val_far, w2a, w2b, v013 = lax.optimization_barrier((val_far, w2a, w2b, v013))
    v2 = shift(stack(w2a, w2b), core=1)
    mine1, other1 = partial(a_far, val, val_far)
    got1 = shift(other1, core=1)
    up0, down0 = first_hop(mine0, after(got0, other1))
    up0r, down0r = shift(up0, x=1), shift(down0, x=-1)
    to_up0, to_down0 = second_hop(mine0, got0, up0r, after(down0r, other1))
    from_down0, from_up0 = shift(to_up0, x=1), shift(to_down0, x=-1)
    up1, down1 = first_hop(mine1, after(got1, to_up0))
    up1r, down1r = shift(up1, x=1), shift(down1, x=-1)

    near, out_far = call(
        input_kernel,
        [shape((tok, width)), shape((tok, width // 2))],
        place,
        (after(w013, up1), w2a, w2b, v013, v2, key, val, key_far, val_far),
        [ANY] * 9,
        [ANY] * 2,
        [
            pltpu.VMEM((2, width // 2, feat), BF16),
            pltpu.VMEM((2, 2 * tok, feat), BF16),
            pltpu.VMEM((2 * tok, width // 2), BF16),
            pltpu.SemaphoreType.DMA((22,)),
            pltpu.SemaphoreType.DMA((12,)),
        ],
        flops=4 * tok * width * feat,
        moved=16 * 2**20,
        weight=WEIGHT,
        vmem=20,
    )
    far = shift(out_far, yhi=1)
    to_up1, to_down1 = second_hop(mine1, got1, up1r, after(down1r, out_far))
    from_down1, from_up1 = shift(to_up1, x=1), shift(to_down1, x=-1)
    from_up0 = after(from_up0, to_up1)
    input_grad = call(
        far_columns_kernel,
        shape((tok, width)),
        place,
        (far, near),
        [pl.BlockSpec((tok // 2, width // 2), lambda i, place: (i, 0)), ANY],
        pl.BlockSpec((tok // 2, width // 2), lambda i, place: (i, 1 - place[0])),
        grid=(2,),
        moved=2 * tok * width,
        alias={2: 0},
    )

    half_own = pl.BlockSpec((1, hr, feat), lambda i, place: (place[2], i, 0))
    qc = feat // 4
    half_quarter = pl.BlockSpec((hr, qc), lambda i, place: (i, 0))
    sums0 = (mine0, got0, from_down0, from_up0)
    sum_specs = [half_own, half_own, half_rows, half_rows]
    own, s1, s2, s3 = call(
        selected_kernel,
        [shape((rows, qc), F32)] + [shape((rows, qc))] * 3,
        place,
        (*planes, *sums0),
        [half_rows] * 3 + sum_specs,
        [half_quarter] * 4,
        [pltpu.VMEM((hr, feat), F32)],
        grid=(2,),
        moved=10 * 2**20,
        weight=WEIGHT,
    )
    total = own
    for s, part in ((1, s1), (2, s2), (-1, s3)):
        total = total + shift(part, z=s).astype(F32)
    total, from_down1, from_up1 = lax.optimization_barrier((total, from_down1, from_up1))
    total = lax.reduce_precision(total, 8, 7)
    total = total + after(shift(total.astype(BF16), ylo=1), input_grad).astype(F32)
    mean = (total / 8).astype(BF16)
    means = (mean, shift(mean, z=-1), shift(mean, z=2), shift(mean, z=1))
    sums1 = (mine1, got1, from_down1, from_up1)
    first_out, second_out, inner = call(
        moments_kernel,
        [shape((rows, 2, feat), F32)] * 2 + [shape((rows, feat), F32)],
        place,
        (weight_here, first_moment[0], second_moment[0], *sums0, *sums1),
        [half_both] * 3 + sum_specs * 2,
        [half_both] * 2 + [half_rows],
        grid=(2,),
        moved=16 * 2**20,
    )
    weights_out, anchor_out, momentum_out = call(
        outer_kernel,
        [shape((rows, 2, feat), F32)] + [shape((rows, feat), F32)] * 2,
        place,
        (*means, anchor, momentum, inner),
        [half_quarter] * 4 + [half_rows] * 3,
        [half_both] + [half_rows] * 2,
        [pltpu.VMEM((hr, feat), F32)],
        grid=(2,),
        moved=9 * 2**20,
    )

    return (
        weights_out[None],
        first_out[None],
        second_out[None],
        anchor_out,
        momentum_out,
        input_grad[None],
    )


def solution(mesh):
    fine = Mesh(mesh.devices.reshape(SIZES), AXES)
    rep, fs = ("ylo", "z"), ("yhi", "x", "core")
    in_specs = (
        P(rep, fs, None),
        P(rep, fs, None, None),
        P(rep, fs, None, None),
        P(rep, fs, None, None),
        P(rep, fs, None, None),
        P(fs, None),
        P(fs, None),
    )
    out_specs = (
        P(rep, fs, None, None),
        P(rep, fs, None, None),
        P(rep, fs, None, None),
        P(fs, None),
        P(fs, None),
        P(rep, fs, None),
    )
    return jax.shard_map(shards, mesh=fine, in_specs=in_specs, out_specs=out_specs, check_vma=False)
```

time: 213 us -> 138 us (0.65)
  waiting for transfers between devices: 111 us -> 50.3 us
  Pallas kernels: 54.6 us -> 42.2 us
  starting transfers between devices: 38.2 us -> 42 us
  local copies, waits for them, and re-layouts: 5.39 us -> 2.14 us
    ppermute x29 -> x27, waiting for transfers between devices: 111 us -> 50.3 us  [shift(): return lax.ppermute(value, AXES, pairs)]
    pallas_call x13 -> x16, Pallas kernels: 54.6 us -> 42.2 us  [call(): pl.pallas_call(kernel, out_shape=out_shape, grid_spec=pltpu.PrefetchScala...]
    ppermute x29 -> x27, starting transfers between devices: 38.2 us -> 42 us  [shift(): return lax.ppermute(value, AXES, pairs)]
    unnamed x27 -> x22, local copies, waits for them, and re-layouts: 3.91 us -> 1.71 us
  transfers between devices with their start and end apart: 29 -> 27, of which waited for: 9 -> 14; matrix products, arithmetic and copies ran while one was open for 2% -> 0% of each run, Pallas kernels for 21% -> 28%
where the time goes in v1:
time: 138 us
  waiting for transfers between devices  50.3 us (36%)
  Pallas kernels  42.2 us (31%)
  starting transfers between devices  42 us (30%)
  local copies, waits for them, and re-layouts  2.14 us (2%)
    ppermute x27, waiting for transfers between devices, shift(): return lax.ppermute(value, AXES, pairs)  50.3 us
    pallas_call x16, Pallas kernels, call(): pl.pallas_call(kernel, out_shape=out_shape, grid_spec=pltpu.PrefetchScala...  42.2 us
    ppermute x27, starting transfers between devices, shift(): return lax.ppermute(value, AXES, pairs)  42 us
  transfers between devices with their start and end apart: 27, of which 14 were waited for; matrix products, arithmetic and copies ran while one was open for 0% of the time, Pallas kernels for 28%

profile of v1, /device:TPU:0, one launch (start us, length us, event | category | flops | bytes accessed | tf_op | source)
XLA Modules:
  0.0 137.7 jit_solution(9064759464275935486)
XLA Ops:
  0.7 1.7 %copy-done = bf16[1,256,4608]{2,1,0:T(8,128)(2,1)S(1)} copy-done((bf16[1,256,4608]{2,1,0:T(8,128)(2,1)S(1)}, bf16[1,256,4608]{2,1,0:T(8,128)(2,1)}, u32[]{:S(2)}) %copy-start) | copy-done | bytes 2359320
  3.0 3.4 %collective-permute-start = (bf16[256,2304]{1,0:T(8,128)(2,1)S(1)}, bf16[256,2304]{1,0:T(8,128)(2,1)S(1)}, u32[]{:S(2)}, u32[]{:S(2)}) collective-permute-start(bf16[256,2304]{1,0:T(8,128)(2,1)S(1)} %shard_map.118), channel_id=1, source_target_pairs={{0,8},{1,9},{2,10},{3,11},{4,12},{5,13},{6,14},{7,15},{8,0},{9,1},... | collective-permute-start | bytes 3538952 | tf_op jit(solution)/shard_map/ppermute | solution.py:28
  6.4 3.1 %shard_map.119 = (bf16[288,2048]{1,0:T(8,128)(2,1)S(1)}, f32[288,1024]{1,0:T(8,128)S(1)}) custom-call(s32[4]{0:T(128)S(1)} %pad_add_fusion.place, f32[288,2,1024]{2,1,0:T(2,128)S(1)} %bitcast.23), custom_call_target="tpu_custom_call" | custom-call | flops 49999998976 | bytes 500000000 | tf_op jit(solution)/shard_map/pallas_call | solution.py:34
  9.5 1.6 %collective-permute-start.2 = (bf16[288,2048]{1,0:T(8,128)(2,1)S(1)}, bf16[288,2048]{1,0:T(8,128)(2,1)S(1)}, u32[]{:S(2)}, u32[]{:S(2)}) collective-permute-start(bf16[288,2048]{1,0:T(8,128)(2,1)S(1)} %get-tuple-element.59.refs_0_), channel_id=1, source_target_pairs={{0,2},{1,3},{2,4},{3,5},{4,6},{5,7},{6,0},{7,1},{8,10},{9,11},{10,... | collective-permute-start | bytes 3538952 | tf_op jit(solution)/shard_map/ppermute | solution.py:28
  11.1 1.7 %collective-permute-start.1 = (bf16[288,2048]{1,0:T(8,128)(2,1)S(1)}, bf16[288,2048]{1,0:T(8,128)(2,1)S(1)}, u32[]{:S(2)}, u32[]{:S(2)}) collective-permute-start(bf16[288,2048]{1,0:T(8,128)(2,1)S(1)} %get-tuple-element.59.refs_0_), channel_id=1, source_target_pairs={{0,6},{1,7},{2,0},{3,1},{4,2},{5,3},{6,4},{7,5},{8,14},{9,15},{10,... | collective-permute-start | bytes 3538952 | tf_op jit(solution)/shard_map/ppermute | solution.py:28
  15.2 2.7 %collective-permute-start.5 = (bf16[256,1024]{1,0:T(8,128)(2,1)S(1)}, bf16[256,1024]{1,0:T(8,128)(2,1)S(1)}, u32[]{:S(2)}, u32[]{:S(2)}) collective-permute-start(bf16[256,1024]{1,0:T(8,128)(2,1)S(1)} %get-tuple-element.71.c_own.v_near), channel_id=1, source_target_pairs={{0,8},{1,9},{2,10},{3,11},{4,12},{5,13},{6,14},{7,15},{8,0},{9,1},... | collective-permute-start | bytes 1572872 | tf_op jit(solution)/shard_map/ppermute | solution.py:28
  17.9 15.6 %collective-permute-done.a_far = bf16[256,2304]{1,0:T(8,128)(2,1)S(1)} collective-permute-done((bf16[256,2304]{1,0:T(8,128)(2,1)S(1)}, bf16[256,2304]{1,0:T(8,128)(2,1)S(1)}, u32[]{:S(2)}, u32[]{:S(2)}) %collective-permute-start) | collective-permute-done | bytes 1179680 | tf_op jit(solution)/shard_map/ppermute | solution.py:28
  33.5 4.8 %collective-permute-done.2.refs_2_ = bf16[288,2048]{1,0:T(8,128)(2,1)S(1)} collective-permute-done((bf16[288,2048]{1,0:T(8,128)(2,1)S(1)}, bf16[288,2048]{1,0:T(8,128)(2,1)S(1)}, u32[]{:S(2)}, u32[]{:S(2)}) %collective-permute-start.2) | collective-permute-done | bytes 1179680 | tf_op jit(solution)/shard_map/ppermute | solution.py:28
  39.1 3.0 %collective-permute-start.7 = (bf16[144,2048]{1,0:T(8,128)(2,1)S(1)}, bf16[144,2048]{1,0:T(8,128)(2,1)S(1)}, u32[]{:S(2)}, u32[]{:S(2)}) collective-permute-start(bf16[144,2048]{1,0:T(8,128)(2,1)S(1)} %slice.15), channel_id=1, source_target_pairs={{0,6},{1,7},{2,0},{3,1},{4,2},{5,3},{6,4},{7,5},{8,14},{9,15},{10,... | collective-permute-start | bytes 1769480 | tf_op jit(solution)/shard_map/ppermute | solution.py:28
  42.2 2.5 %collective-permute-done.3.c_far.k_far = bf16[256,1024]{1,0:T(8,128)(2,1)S(1)} collective-permute-done((bf16[256,1024]{1,0:T(8,128)(2,1)S(1)}, bf16[256,1024]{1,0:T(8,128)(2,1)S(1)}, u32[]{:S(2)}, u32[]{:S(2)}) %collective-permute-start.3) | collective-permute-done | bytes 524320 | tf_op jit(solution)/shard_map/ppermute | solution.py:28
  44.7 4.9 %shard_map.121 = (bf16[4,288,1024]{2,1,0:T(8,128)(2,1)S(1)}, bf16[4,288,1024]{2,1,0:T(8,128)(2,1)S(1)}) custom-call(s32[4]{0:T(128)S(1)} %pad_add_fusion.place, bf16[256,4608]{1,0:T(8,128)(2,1)S(1)} %bitcast.21, bf16[256,2304]{1,0:T(8,128)(2,1)S(1)} %collective-permute-done.a_far, bf16[256,1024]{1,0:T(8,128)(2,1)S(1)} %get-tuple-element.111.c_own.k_near, ...), custom_call_target="tpu_custom_call" | custom-call | flops 49999998976 | bytes 500000000 | tf_op jit(solution)/shard_map/pallas_call | solution.py:34
  49.7 5.2 %collective-permute-done.5.c_far.v_far = bf16[256,1024]{1,0:T(8,128)(2,1)S(1)} collective-permute-done((bf16[256,1024]{1,0:T(8,128)(2,1)S(1)}, bf16[256,1024]{1,0:T(8,128)(2,1)S(1)}, u32[]{:S(2)}, u32[]{:S(2)}) %collective-permute-start.5) | collective-permute-done | bytes 524320 | tf_op jit(solution)/shard_map/ppermute | solution.py:28
  54.8 1.8 %collective-permute-done.6.refs_0_.w2a = bf16[144,2048]{1,0:T(8,128)(2,1)S(1)} collective-permute-done((bf16[144,2048]{1,0:T(8,128)(2,1)S(1)}, bf16[144,2048]{1,0:T(8,128)(2,1)S(1)}, u32[]{:S(2)}, u32[]{:S(2)}) %collective-permute-start.6) | collective-permute-done | bytes 589856 | tf_op jit(solution)/shard_map/ppermute | solution.py:28
  56.7 4.9 %shard_map.123 = (bf16[4,288,1024]{2,1,0:T(8,128)(2,1)S(1)}, bf16[4,288,1024]{2,1,0:T(8,128)(2,1)S(1)}) custom-call(s32[4]{0:T(128)S(1)} %pad_add_fusion.place, bf16[256,4608]{1,0:T(8,128)(2,1)S(1)} %bitcast.22, bf16[256,2304]{1,0:T(8,128)(2,1)S(1)} %collective-permute-done.a_far, bf16[256,1024]{1,0:T(8,128)(2,1)S(1)} %get-tuple-element.71.c_own.v_near, ...), custom_call_target="tpu_custom_call" | custom-call | flops 49999998976 | bytes 500000000 | tf_op jit(solution)/shard_map/pallas_call | solution.py:34
  65.6 6.9 %collective-permute-done.10.down = bf16[144,1024]{1,0:T(8,128)(2,1)S(1)} collective-permute-done((bf16[144,1024]{1,0:T(8,128)(2,1)S(1)}, bf16[144,1024]{1,0:T(8,128)(2,1)S(1)}, u32[]{:S(2)}, u32[]{:S(2)}) %collective-permute-start.10) | collective-permute-done | bytes 294944 | tf_op jit(solution)/shard_map/ppermute | solution.py:28
  72.5 1.9 %collective-permute-done.9.up = bf16[144,1024]{1,0:T(8,128)(2,1)S(1)} collective-permute-done((bf16[144,1024]{1,0:T(8,128)(2,1)S(1)}, bf16[144,1024]{1,0:T(8,128)(2,1)S(1)}, u32[]{:S(2)}, u32[]{:S(2)}) %collective-permute-start.9) | collective-permute-done | bytes 294944 | tf_op jit(solution)/shard_map/ppermute | solution.py:28
  75.7 1.7 %collective-permute-start.11 = (bf16[288,1024]{1,0:T(8,128)(2,1)S(1)}, bf16[288,1024]{1,0:T(8,128)(2,1)S(1)}, u32[]{:S(2)}, u32[]{:S(2)}) collective-permute-start(bf16[288,1024]{1,0:T(8,128)(2,1)S(1)} %get-tuple-element.80), channel_id=1, source_target_pairs={{0,2},{1,3},{2,4},{3,5},{4,6},{5,7},{6,0},{7,1},{8,10},{9,11},{10,... | collective-permute-start | bytes 1769480 | tf_op jit(solution)/shard_map/ppermute | solution.py:28
  78.2 3.2 %collective-permute-start.15 = (bf16[144,1024]{1,0:T(8,128)(2,1)S(1)}, bf16[144,1024]{1,0:T(8,128)(2,1)S(1)}, u32[]{:S(2)}, u32[]{:S(2)}) collective-permute-start(bf16[144,1024]{1,0:T(8,128)(2,1)S(1)} %get-tuple-element.85), channel_id=1, source_target_pairs={{0,6},{1,7},{2,0},{3,1},{4,2},{5,3},{6,4},{7,5},{8,14},{9,15},{10,... | collective-permute-start | bytes 884744 | tf_op jit(solution)/shard_map/ppermute | solution.py:28
  81.4 10.2 %shard_map.128 = (bf16[256,4608]{1,0:T(8,128)(2,1)}, bf16[256,2304]{1,0:T(8,128)(2,1)S(1)}) custom-call(s32[4]{0:T(128)S(1)} %pad_add_fusion.place, bf16[864,2048]{1,0:T(8,128)(2,1)S(1)} %shard_map.122.w013, bf16[144,2048]{1,0:T(8,128)(2,1)S(1)} %collective-permute-done.6.refs_0_.w2a, bf16[144,2048]{1,0:T(8,128)(2,1)S(1)} %collective-permute-done.7.refs_1_.w2b, ...), custom_call_target="tpu_custom_call" | custom-call | flops 49999998976 | bytes 500000000 | tf_op jit(solution)/shard_map/pallas_call | solution.py:34
  91.7 3.3 %collective-permute-start.23 = (bf16[256,2304]{1,0:T(8,128)(2,1)S(1)}, bf16[256,2304]{1,0:T(8,128)(2,1)S(1)}, u32[]{:S(2)}, u32[]{:S(2)}) collective-permute-start(bf16[256,2304]{1,0:T(8,128)(2,1)S(1)} %get-tuple-element.90), channel_id=1, source_target_pairs={{0,8},{1,9},{2,10},{3,11},{4,12},{5,13},{6,14},{7,15},{8,0},{9,1},... | collective-permute-start | bytes 3538952 | tf_op jit(solution)/shard_map/ppermute | solution.py:28
  98.6 1.7 %collective-permute-start.20 = (bf16[288,1024]{1,0:T(8,128)(2,1)S(1)}, bf16[288,1024]{1,0:T(8,128)(2,1)S(1)}, u32[]{:S(2)}, u32[]{:S(2)}) collective-permute-start(bf16[288,1024]{1,0:T(8,128)(2,1)S(1)} %get-tuple-element.92), channel_id=1, source_target_pairs={{0,2},{1,3},{2,4},{3,5},{4,6},{5,7},{6,0},{7,1},{8,10},{9,11},{10,... | collective-permute-start | bytes 1769480 | tf_op jit(solution)/shard_map/ppermute | solution.py:28
  100.4 2.9 %shard_map.130 = (f32[288,256]{1,0:T(8,128)S(1)}, bf16[288,256]{1,0:T(8,128)(2,1)S(1)}, bf16[288,256]{1,0:T(8,128)(2,1)S(1)}, bf16[288,256]{1,0:T(8,128)(2,1)S(1)}) custom-call(s32[4]{0:T(128)S(1)} %pad_add_fusion.place, f32[288,1024]{1,0:T(8,128)S(1)} %get-tuple-element.65.w, f32[288,1024]{1,0:T(8,128)S(1)} %get-tuple-element.66.m, ...), custom_call_target="tpu_custom_call" | custom-call | flops 49999998976 | bytes 500000000 | tf_op jit(solution)/shard_map/pallas_call | solution.py:34
  103.3 2.0 %collective-permute-start.17 = (bf16[288,256]{1,0:T(8,128)(2,1)S(1)}, bf16[288,256]{1,0:T(8,128)(2,1)S(1)}, u32[]{:S(2)}, u32[]{:S(2)}) collective-permute-start(bf16[288,256]{1,0:T(8,128)(2,1)S(1)} %get-tuple-element.95), channel_id=1, source_target_pairs={{0,16},{1,17},{2,18},{3,19},{4,20},{5,21},{6,22},{7,23},{8,24},{9,... | collective-permute-start | bytes 442376 | tf_op jit(solution)/shard_map/ppermute | solution.py:28
  105.3 3.6 %collective-permute-start.18 = (bf16[288,256]{1,0:T(8,128)(2,1)S(1)}, bf16[288,256]{1,0:T(8,128)(2,1)S(1)}, u32[]{:S(2)}, u32[]{:S(2)}) collective-permute-start(bf16[288,256]{1,0:T(8,128)(2,1)S(1)} %get-tuple-element.96), channel_id=1, source_target_pairs={{0,32},{1,33},{2,34},{3,35},{4,36},{5,37},{6,38},{7,39},{8,40},{9,... | collective-permute-start | bytes 442376 | tf_op jit(solution)/shard_map/ppermute | solution.py:28
  108.9 2.7 %collective-permute-done.17 = bf16[288,256]{1,0:T(8,128)(2,1)S(1)} collective-permute-done((bf16[288,256]{1,0:T(8,128)(2,1)S(1)}, bf16[288,256]{1,0:T(8,128)(2,1)S(1)}, u32[]{:S(2)}, u32[]{:S(2)}) %collective-permute-start.17) | collective-permute-done | bytes 147488 | tf_op jit(solution)/shard_map/ppermute | solution.py:28
  113.6 3.2 %collective-permute-done.19 = bf16[288,256]{1,0:T(8,128)(2,1)S(1)} collective-permute-done((bf16[288,256]{1,0:T(8,128)(2,1)S(1)}, bf16[288,256]{1,0:T(8,128)(2,1)S(1)}, u32[]{:S(2)}, u32[]{:S(2)}) %collective-permute-start.19) | collective-permute-done | bytes 147488 | tf_op jit(solution)/shard_map/ppermute | solution.py:28
  116.9 1.7 %collective-permute-start.22 = (bf16[288,256]{1,0:T(8,128)(2,1)S(1)}, bf16[288,256]{1,0:T(8,128)(2,1)S(1)}, u32[]{:S(2)}, u32[]{:S(2)}) collective-permute-start(bf16[288,256]{1,0:T(8,128)(2,1)S(1)} %reduce-precision_convert_fusion), channel_id=1, source_target_pairs={{0,64},{1,65},{2,66},{3,67},{4,68},{5,69},{6,70},{7,71},{8,72},{9,... | collective-permute-start | bytes 442376 | tf_op jit(solution)/shard_map/ppermute | solution.py:28
  119.7 1.6 %shard_map.131 = bf16[256,4608]{1,0:T(8,128)(2,1)} custom-call(s32[4]{0:T(128)S(1)} %pad_add_fusion.place, bf16[256,2304]{1,0:T(8,128)(2,1)S(1)} %collective-permute-done.23.far, bf16[256,4608]{1,0:T(8,128)(2,1)} %get-tuple-element.100.near), custom_call_target="tpu_custom_call", output_to_operand_aliasing={{}: (2, {})} | custom-call | tf_op jit(solution)/shard_map/pallas_call | solution.py:34
  122.4 2.2 %collective-permute-start.26 = (bf16[288,256]{1,0:T(8,128)(2,1)S(1)}, bf16[288,256]{1,0:T(8,128)(2,1)S(1)}, u32[]{:S(2)}, u32[]{:S(2)}) collective-permute-start(bf16[288,256]{1,0:T(8,128)(2,1)S(1)} %multiply_convert_fusion.m0), channel_id=1, source_target_pairs={{0,16},{1,17},{2,18},{3,19},{4,20},{5,21},{6,22},{7,23},{8,24},{9,... | collective-permute-start | bytes 442376 | tf_op jit(solution)/shard_map/ppermute | solution.py:28
  124.6 3.6 %collective-permute-start.25 = (bf16[288,256]{1,0:T(8,128)(2,1)S(1)}, bf16[288,256]{1,0:T(8,128)(2,1)S(1)}, u32[]{:S(2)}, u32[]{:S(2)}) collective-permute-start(bf16[288,256]{1,0:T(8,128)(2,1)S(1)} %multiply_convert_fusion.m0), channel_id=1, source_target_pairs={{0,32},{1,33},{2,34},{3,35},{4,36},{5,37},{6,38},{7,39},{8,40},{9,... | collective-permute-start | bytes 442376 | tf_op jit(solution)/shard_map/ppermute | solution.py:28
  129.3 5.3 %shard_map.132 = (f32[288,2,1024]{2,1,0:T(2,128)}, f32[288,2,1024]{2,1,0:T(2,128)}, f32[288,1024]{1,0:T(8,128)S(1)}) custom-call(s32[4]{0:T(128)S(1)} %pad_add_fusion.place, f32[288,2,1024]{2,1,0:T(2,128)S(1)} %bitcast.24, f32[288,2,1024]{2,1,0:T(2,128)S(1)} %bitcast.26, f32[288,2,1024]{2,1,0:T(2,128)S(1)} %bitcast.28, ...), custom_call_target="tpu_custom_call" | custom-call | tf_op jit(solution)/shard_map/pallas_call | solution.py:34
  134.6 3.1 %shard_map.133 = (f32[288,2,1024]{2,1,0:T(2,128)}, f32[288,1024]{1,0:T(8,128)}, f32[288,1024]{1,0:T(8,128)}) custom-call(s32[4]{0:T(128)S(1)} %pad_add_fusion.place, bf16[288,256]{1,0:T(8,128)(2,1)S(1)} %multiply_convert_fusion.m0, bf16[288,256]{1,0:T(8,128)(2,1)S(1)} %collective-permute-done.24.m1, bf16[288,256]{1,0:T(8,128)(2,1)S(1)} %collective-permute-done.25.m2, ...), custom_call_target="tpu_custom_call" | custom-call | tf_op jit(solution)/shard_map/pallas_call | solution.py:34
  (68 shorter events, 19.2 us)
Async XLA Ops:
  3.0 30.4 %collective-permute-start = (bf16[256,2304]{1,0:T(8,128)(2,1)S(1)}, bf16[256,2304]{1,0:T(8,128)(2,1)S(1)}, u32[]{:S(2)}, u32[]{:S(2)}) collective-permute-start(bf16[256,2304]{1,0:T(8,128)(2,1)S(1)} %shard_map.118), channel_id=1, source_target_pairs={{0,8},{1,9},{2,10},{3,11},{4,12},{5,13},{6,14},{7,15},{8,0},{9,1},... | collective-permute-start | bytes 3538952 | tf_op jit(solution)/shard_map/ppermute | solution.py:28
  6.4 6.4 %copy-start.10 = (bf16[1,256,2,1024]{3,2,1,0:T(2,128)(2,1)S(1)}, bf16[1,256,2,1024]{3,2,1,0:T(2,128)(2,1)}, u32[]{:S(2)}) copy-start(bf16[1,256,2,1024]{3,2,1,0:T(2,128)(2,1)} %param.8) | copy-start | bytes 3145732
  6.4 7.8 %copy-start.6 = (f32[1,288,2,1024]{3,2,1,0:T(2,128)S(1)}, f32[1,288,2,1024]{3,2,1,0:T(2,128)}, u32[]{:S(2)}) copy-start(f32[1,288,2,1024]{3,2,1,0:T(2,128)} %param.11) | copy-start | bytes 7077892
  9.5 28.7 %collective-permute-start.2 = (bf16[288,2048]{1,0:T(8,128)(2,1)S(1)}, bf16[288,2048]{1,0:T(8,128)(2,1)S(1)}, u32[]{:S(2)}, u32[]{:S(2)}) collective-permute-start(bf16[288,2048]{1,0:T(8,128)(2,1)S(1)} %get-tuple-element.59.refs_0_), channel_id=1, source_target_pairs={{0,2},{1,3},{2,4},{3,5},{4,6},{5,7},{6,0},{7,1},{8,10},{9,11},{10,... | collective-permute-start | bytes 3538952 | tf_op jit(solution)/shard_map/ppermute | solution.py:28
  11.1 27.1 %collective-permute-start.1 = (bf16[288,2048]{1,0:T(8,128)(2,1)S(1)}, bf16[288,2048]{1,0:T(8,128)(2,1)S(1)}, u32[]{:S(2)}, u32[]{:S(2)}) collective-permute-start(bf16[288,2048]{1,0:T(8,128)(2,1)S(1)} %get-tuple-element.59.refs_0_), channel_id=1, source_target_pairs={{0,6},{1,7},{2,0},{3,1},{4,2},{5,3},{6,4},{7,5},{8,14},{9,15},{10,... | collective-permute-start | bytes 3538952 | tf_op jit(solution)/shard_map/ppermute | solution.py:28
  13.2 31.5 %collective-permute-start.3 = (bf16[256,1024]{1,0:T(8,128)(2,1)S(1)}, bf16[256,1024]{1,0:T(8,128)(2,1)S(1)}, u32[]{:S(2)}, u32[]{:S(2)}) collective-permute-start(bf16[256,1024]{1,0:T(8,128)(2,1)S(1)} %get-tuple-element.111.c_own.k_near), channel_id=1, source_target_pairs={{0,8},{1,9},{2,10},{3,11},{4,12},{5,13},{6,14},{7,15},{8,0},{9,1},... | collective-permute-start | bytes 1572872 | tf_op jit(solution)/shard_map/ppermute | solution.py:28
  15.2 39.6 %collective-permute-start.5 = (bf16[256,1024]{1,0:T(8,128)(2,1)S(1)}, bf16[256,1024]{1,0:T(8,128)(2,1)S(1)}, u32[]{:S(2)}, u32[]{:S(2)}) collective-permute-start(bf16[256,1024]{1,0:T(8,128)(2,1)S(1)} %get-tuple-element.71.c_own.v_near), channel_id=1, source_target_pairs={{0,8},{1,9},{2,10},{3,11},{4,12},{5,13},{6,14},{7,15},{8,0},{9,1},... | collective-permute-start | bytes 1572872 | tf_op jit(solution)/shard_map/ppermute | solution.py:28
  39.1 15.7 %collective-permute-start.7 = (bf16[144,2048]{1,0:T(8,128)(2,1)S(1)}, bf16[144,2048]{1,0:T(8,128)(2,1)S(1)}, u32[]{:S(2)}, u32[]{:S(2)}) collective-permute-start(bf16[144,2048]{1,0:T(8,128)(2,1)S(1)} %slice.15), channel_id=1, source_target_pairs={{0,6},{1,7},{2,0},{3,1},{4,2},{5,3},{6,4},{7,5},{8,14},{9,15},{10,... | collective-permute-start | bytes 1769480 | tf_op jit(solution)/shard_map/ppermute | solution.py:28
  42.2 14.5 %collective-permute-start.6 = (bf16[144,2048]{1,0:T(8,128)(2,1)S(1)}, bf16[144,2048]{1,0:T(8,128)(2,1)S(1)}, u32[]{:S(2)}, u32[]{:S(2)}) collective-permute-start(bf16[144,2048]{1,0:T(8,128)(2,1)S(1)} %slice.14), channel_id=1, source_target_pairs={{0,2},{1,3},{2,4},{3,5},{4,6},{5,7},{6,0},{7,1},{8,10},{9,11},{10,... | collective-permute-start | bytes 1769480 | tf_op jit(solution)/shard_map/ppermute | solution.py:28
  42.2 14.5 %collective-permute-start.8 = (bf16[864,2048]{1,0:T(8,128)(2,1)S(1)}, bf16[864,2048]{1,0:T(8,128)(2,1)S(1)}, u32[]{:S(2)}, u32[]{:S(2)}) collective-permute-start(bf16[864,2048]{1,0:T(8,128)(2,1)S(1)} %shard_map.122.w013), channel_id=1, source_target_pairs={{0,1},{1,0},{2,3},{3,2},{4,5},{5,4},{6,7},{7,6},{8,9},{9,8},{10,11... | collective-permute-start | bytes 10616840 | tf_op jit(solution)/shard_map/ppermute | solution.py:28
  49.6 13.3 %collective-permute-start.4 = (bf16[4,288,1024]{2,1,0:T(8,128)(2,1)S(1)}, bf16[4,288,1024]{2,1,0:T(8,128)(2,1)S(1)}, u32[]{:S(2)}, u32[]{:S(2)}) collective-permute-start(bf16[4,288,1024]{2,1,0:T(8,128)(2,1)S(1)} %get-tuple-element.70), channel_id=1, source_target_pairs={{0,1},{1,0},{2,3},{3,2},{4,5},{5,4},{6,7},{7,6},{8,9},{9,8},{10,11... | collective-permute-start | bytes 7077896 | tf_op jit(solution)/shard_map/ppermute | solution.py:28
  61.5 15.9 %collective-permute-start.13 = (bf16[4,288,1024]{2,1,0:T(8,128)(2,1)S(1)}, bf16[4,288,1024]{2,1,0:T(8,128)(2,1)S(1)}, u32[]{:S(2)}, u32[]{:S(2)}) collective-permute-start(bf16[4,288,1024]{2,1,0:T(8,128)(2,1)S(1)} %get-tuple-element.75), channel_id=1, source_target_pairs={{0,1},{1,0},{2,3},{3,2},{4,5},{5,4},{6,7},{7,6},{8,9},{9,8},{10,11... | collective-permute-start | bytes 7077896 | tf_op jit(solution)/shard_map/ppermute | solution.py:28
  62.3 19.2 %collective-permute-start.16 = (bf16[288,2048]{1,0:T(8,128)(2,1)S(1)}, bf16[288,2048]{1,0:T(8,128)(2,1)S(1)}, u32[]{:S(2)}, u32[]{:S(2)}) collective-permute-start(bf16[288,2048]{1,0:T(8,128)(2,1)S(1)} %shard_map.127), channel_id=1, source_target_pairs={{0,1},{1,0},{2,3},{3,2},{4,5},{5,4},{6,7},{7,6},{8,9},{9,8},{10,11... | collective-permute-start | bytes 3538952 | tf_op jit(solution)/shard_map/ppermute | solution.py:28
  63.5 9.0 %collective-permute-start.10 = (bf16[144,1024]{1,0:T(8,128)(2,1)S(1)}, bf16[144,1024]{1,0:T(8,128)(2,1)S(1)}, u32[]{:S(2)}, u32[]{:S(2)}) collective-permute-start(bf16[144,1024]{1,0:T(8,128)(2,1)S(1)} %get-tuple-element.78), channel_id=1, source_target_pairs={{0,6},{1,7},{2,0},{3,1},{4,2},{5,3},{6,4},{7,5},{8,14},{9,15},{10,... | collective-permute-start | bytes 884744 | tf_op jit(solution)/shard_map/ppermute | solution.py:28
  64.6 9.9 %collective-permute-start.9 = (bf16[144,1024]{1,0:T(8,128)(2,1)S(1)}, bf16[144,1024]{1,0:T(8,128)(2,1)S(1)}, u32[]{:S(2)}, u32[]{:S(2)}) collective-permute-start(bf16[144,1024]{1,0:T(8,128)(2,1)S(1)} %get-tuple-element.77), channel_id=1, source_target_pairs={{0,2},{1,3},{2,4},{3,5},{4,6},{5,7},{6,0},{7,1},{8,10},{9,11},{10,... | collective-permute-start | bytes 884744 | tf_op jit(solution)/shard_map/ppermute | solution.py:28
  75.3 25.0 %collective-permute-start.12 = (bf16[288,1024]{1,0:T(8,128)(2,1)S(1)}, bf16[288,1024]{1,0:T(8,128)(2,1)S(1)}, u32[]{:S(2)}, u32[]{:S(2)}) collective-permute-start(bf16[288,1024]{1,0:T(8,128)(2,1)S(1)} %get-tuple-element.81), channel_id=1, source_target_pairs={{0,6},{1,7},{2,0},{3,1},{4,2},{5,3},{6,4},{7,5},{8,14},{9,15},{10,... | collective-permute-start | bytes 1769480 | tf_op jit(solution)/shard_map/ppermute | solution.py:28
  75.7 24.7 %collective-permute-start.11 = (bf16[288,1024]{1,0:T(8,128)(2,1)S(1)}, bf16[288,1024]{1,0:T(8,128)(2,1)S(1)}, u32[]{:S(2)}, u32[]{:S(2)}) collective-permute-start(bf16[288,1024]{1,0:T(8,128)(2,1)S(1)} %get-tuple-element.80), channel_id=1, source_target_pairs={{0,2},{1,3},{2,4},{3,5},{4,6},{5,7},{6,0},{7,1},{8,10},{9,11},{10,... | collective-permute-start | bytes 1769480 | tf_op jit(solution)/shard_map/ppermute | solution.py:28
  78.1 19.2 %collective-permute-start.14 = (bf16[144,1024]{1,0:T(8,128)(2,1)S(1)}, bf16[144,1024]{1,0:T(8,128)(2,1)S(1)}, u32[]{:S(2)}, u32[]{:S(2)}) collective-permute-start(bf16[144,1024]{1,0:T(8,128)(2,1)S(1)} %get-tuple-element.84), channel_id=1, source_target_pairs={{0,2},{1,3},{2,4},{3,5},{4,6},{5,7},{6,0},{7,1},{8,10},{9,11},{10,... | collective-permute-start | bytes 884744 | tf_op jit(solution)/shard_map/ppermute | solution.py:28
  78.2 17.6 %collective-permute-start.15 = (bf16[144,1024]{1,0:T(8,128)(2,1)S(1)}, bf16[144,1024]{1,0:T(8,128)(2,1)S(1)}, u32[]{:S(2)}, u32[]{:S(2)}) collective-permute-start(bf16[144,1024]{1,0:T(8,128)(2,1)S(1)} %get-tuple-element.85), channel_id=1, source_target_pairs={{0,6},{1,7},{2,0},{3,1},{4,2},{5,3},{6,4},{7,5},{8,14},{9,15},{10,... | collective-permute-start | bytes 884744 | tf_op jit(solution)/shard_map/ppermute | solution.py:28
  91.7 28.0 %collective-permute-start.23 = (bf16[256,2304]{1,0:T(8,128)(2,1)S(1)}, bf16[256,2304]{1,0:T(8,128)(2,1)S(1)}, u32[]{:S(2)}, u32[]{:S(2)}) collective-permute-start(bf16[256,2304]{1,0:T(8,128)(2,1)S(1)} %get-tuple-element.90), channel_id=1, source_target_pairs={{0,8},{1,9},{2,10},{3,11},{4,12},{5,13},{6,14},{7,15},{8,0},{9,1},... | collective-permute-start | bytes 3538952 | tf_op jit(solution)/shard_map/ppermute | solution.py:28
  98.3 18.6 %collective-permute-start.21 = (bf16[288,1024]{1,0:T(8,128)(2,1)S(1)}, bf16[288,1024]{1,0:T(8,128)(2,1)S(1)}, u32[]{:S(2)}, u32[]{:S(2)}) collective-permute-start(bf16[288,1024]{1,0:T(8,128)(2,1)S(1)} %get-tuple-element.98), channel_id=1, source_target_pairs={{0,6},{1,7},{2,0},{3,1},{4,2},{5,3},{6,4},{7,5},{8,14},{9,15},{10,... | collective-permute-start | bytes 1769480 | tf_op jit(solution)/shard_map/ppermute | solution.py:28
  98.6 18.2 %collective-permute-start.20 = (bf16[288,1024]{1,0:T(8,128)(2,1)S(1)}, bf16[288,1024]{1,0:T(8,128)(2,1)S(1)}, u32[]{:S(2)}, u32[]{:S(2)}) collective-permute-start(bf16[288,1024]{1,0:T(8,128)(2,1)S(1)} %get-tuple-element.92), channel_id=1, source_target_pairs={{0,2},{1,3},{2,4},{3,5},{4,6},{5,7},{6,0},{7,1},{8,10},{9,11},{10,... | collective-permute-start | bytes 1769480 | tf_op jit(solution)/shard_map/ppermute | solution.py:28
  100.4 28.9 %copy-start.7 = (f32[1,288,2,1024]{3,2,1,0:T(2,128)S(1)}, f32[1,288,2,1024]{3,2,1,0:T(2,128)}, u32[]{:S(2)}) copy-start(f32[1,288,2,1024]{3,2,1,0:T(2,128)} %param.11) | copy-start | bytes 7077892
  103.3 8.3 %collective-permute-start.17 = (bf16[288,256]{1,0:T(8,128)(2,1)S(1)}, bf16[288,256]{1,0:T(8,128)(2,1)S(1)}, u32[]{:S(2)}, u32[]{:S(2)}) collective-permute-start(bf16[288,256]{1,0:T(8,128)(2,1)S(1)} %get-tuple-element.95), channel_id=1, source_target_pairs={{0,16},{1,17},{2,18},{3,19},{4,20},{5,21},{6,22},{7,23},{8,24},{9,... | collective-permute-start | bytes 442376 | tf_op jit(solution)/shard_map/ppermute | solution.py:28
  105.3 8.3 %collective-permute-start.18 = (bf16[288,256]{1,0:T(8,128)(2,1)S(1)}, bf16[288,256]{1,0:T(8,128)(2,1)S(1)}, u32[]{:S(2)}, u32[]{:S(2)}) collective-permute-start(bf16[288,256]{1,0:T(8,128)(2,1)S(1)} %get-tuple-element.96), channel_id=1, source_target_pairs={{0,32},{1,33},{2,34},{3,35},{4,36},{5,37},{6,38},{7,39},{8,40},{9,... | collective-permute-start | bytes 442376 | tf_op jit(solution)/shard_map/ppermute | solution.py:28
  111.6 5.1 %collective-permute-start.19 = (bf16[288,256]{1,0:T(8,128)(2,1)S(1)}, bf16[288,256]{1,0:T(8,128)(2,1)S(1)}, u32[]{:S(2)}, u32[]{:S(2)}) collective-permute-start(bf16[288,256]{1,0:T(8,128)(2,1)S(1)} %get-tuple-element.97), channel_id=1, source_target_pairs={{0,48},{1,49},{2,50},{3,51},{4,52},{5,53},{6,54},{7,55},{8,56},{9,... | collective-permute-start | bytes 442376 | tf_op jit(solution)/shard_map/ppermute | solution.py:28
  116.9 5.5 %collective-permute-start.22 = (bf16[288,256]{1,0:T(8,128)(2,1)S(1)}, bf16[288,256]{1,0:T(8,128)(2,1)S(1)}, u32[]{:S(2)}, u32[]{:S(2)}) collective-permute-start(bf16[288,256]{1,0:T(8,128)(2,1)S(1)} %reduce-precision_convert_fusion), channel_id=1, source_target_pairs={{0,64},{1,65},{2,66},{3,67},{4,68},{5,69},{6,70},{7,71},{8,72},{9,... | collective-permute-start | bytes 442376 | tf_op jit(solution)/shard_map/ppermute | solution.py:28
  119.7 9.6 %copy-start.3 = (f32[1,288,2,1024]{3,2,1,0:T(2,128)S(1)}, f32[1,288,2,1024]{3,2,1,0:T(2,128)}, u32[]{:S(2)}) copy-start(f32[1,288,2,1024]{3,2,1,0:T(2,128)} %param.9) | copy-start | bytes 7077892
  119.7 9.6 %copy-start.5 = (f32[1,288,2,1024]{3,2,1,0:T(2,128)S(1)}, f32[1,288,2,1024]{3,2,1,0:T(2,128)}, u32[]{:S(2)}) copy-start(f32[1,288,2,1024]{3,2,1,0:T(2,128)} %param.10) | copy-start | bytes 7077892
  122.4 12.1 %collective-permute-start.26 = (bf16[288,256]{1,0:T(8,128)(2,1)S(1)}, bf16[288,256]{1,0:T(8,128)(2,1)S(1)}, u32[]{:S(2)}, u32[]{:S(2)}) collective-permute-start(bf16[288,256]{1,0:T(8,128)(2,1)S(1)} %multiply_convert_fusion.m0), channel_id=1, source_target_pairs={{0,16},{1,17},{2,18},{3,19},{4,20},{5,21},{6,22},{7,23},{8,24},{9,... | collective-permute-start | bytes 442376 | tf_op jit(solution)/shard_map/ppermute | solution.py:28
  124.6 9.9 %collective-permute-start.25 = (bf16[288,256]{1,0:T(8,128)(2,1)S(1)}, bf16[288,256]{1,0:T(8,128)(2,1)S(1)}, u32[]{:S(2)}, u32[]{:S(2)}) collective-permute-start(bf16[288,256]{1,0:T(8,128)(2,1)S(1)} %multiply_convert_fusion.m0), channel_id=1, source_target_pairs={{0,32},{1,33},{2,34},{3,35},{4,36},{5,37},{6,38},{7,39},{8,40},{9,... | collective-permute-start | bytes 442376 | tf_op jit(solution)/shard_map/ppermute | solution.py:28
  128.2 6.3 %collective-permute-start.24 = (bf16[288,256]{1,0:T(8,128)(2,1)S(1)}, bf16[288,256]{1,0:T(8,128)(2,1)S(1)}, u32[]{:S(2)}, u32[]{:S(2)}) collective-permute-start(bf16[288,256]{1,0:T(8,128)(2,1)S(1)} %multiply_convert_fusion.m0), channel_id=1, source_target_pairs={{0,48},{1,49},{2,50},{3,51},{4,52},{5,53},{6,54},{7,55},{8,56},{9,... | collective-permute-start | bytes 442376 | tf_op jit(solution)/shard_map/ppermute | solution.py:28
  (6 other events, 27.4 us)

commit v2 on v1

--- a/solution.py
+++ b/solution.py
@@ -72,19 +72,20 @@
         n += ref.shape[0]
 
 
-def gradient_kernel(place, acts, a_far, c_own, c_far, mine, other, a_s, c_s, g_s, in_sem, out_sem):
-    h, c = place[0], place[1]
-    tok, wide = a_far.shape
+def join_kernel(place, own, far, both):
+    n = own.shape[0]
+    both[:n] = own[...]
+    both[n:] = far[...]
+
+
+def gradient_kernel(place, a_both, c_own, c_far, mine, other, a_s, c_s, g_s, in_sem, out_sem):
+    c = place[1]
+    tok, wide = c_own.shape[0], a_both.shape[1]
     rows = mine.shape[1]
     copies = [
-        pltpu.make_async_copy(
-            acts.at[:, pl.ds(pl.multiple_of(h * wide, 128), wide)],
-            a_s.at[pl.ds(0, tok)],
-            in_sem.at[0],
-        ),
-        pltpu.make_async_copy(a_far, a_s.at[pl.ds(tok, tok)], in_sem.at[1]),
-        pltpu.make_async_copy(c_own, c_s.at[pl.ds(0, tok)], in_sem.at[2]),
-        pltpu.make_async_copy(c_far, c_s.at[pl.ds(tok, tok)], in_sem.at[3]),
+        pltpu.make_async_copy(a_both, a_s, in_sem.at[0]),
+        pltpu.make_async_copy(c_own, c_s.at[pl.ds(0, tok)], in_sem.at[1]),
+        pltpu.make_async_copy(c_far, c_s.at[pl.ds(tok, tok)], in_sem.at[2]),
     ]
     for copy in copies:
         copy.start()
@@ -111,17 +112,16 @@
         send.wait()
 
 
-def rounded_kernel(place, w, w_low, w_key):
+def rounded_kernel(place, w, w_low):
     n = w.shape[2]
-    key = w[:, 0, :]
-    w_key[...] = key
-    w_low[:, :n] = key.astype(BF16)
+    w_low[:, :n] = w[:, 0, :].astype(BF16)
     w_low[:, n:] = w[:, 1, :].astype(BF16)
 
 
-def planes_kernel(place, m, v, m_key, v_key):
-    m_key[...] = m[:, 0, :]
-    v_key[...] = v[:, 0, :]
+def planes_kernel(place, w, m, v, *planes):
+    for f in range(2):
+        for whole, plane in zip((w, m, v), planes[3 * f : 3 * f + 3]):
+            plane[...] = whole[:, f, :]
 
 
 def block_sum(mine, got):
@@ -145,8 +145,16 @@
     to_down[n:] = (part[n:] + down[...].astype(F32)).astype(BF16)
 
 
-def owned_sum(mine, got, up, down):
-    return block_sum(mine, got) + up[...].astype(F32) + down[...].astype(F32)
+def blocks_kernel(place, *refs):
+    for n, out in enumerate(refs[6:]):
+        out[...] = block_sum(refs[2 * n], refs[2 * n + 1]).astype(BF16)
+
+
+def owned_sum(mine, got, *others):
+    total = block_sum(mine, got)
+    for other in others:
+        total = total + other[...].astype(F32)
+    return total
 
 
 def adamw(w, m, v, g):
@@ -156,23 +164,22 @@
     return m, v, w - 0.01 * (step_dir + 0.1 * w)
 
 
-def selected_kernel(place, w, m, v, mine, got, up, down, own, s1, s2, s3, sel):
-    g = owned_sum(mine, got, up, down)
-    sel[...] = adamw(w[...], m[...], v[...], g)[2]
+def selected_kernel(place, w, m, v, mine, got, r1, r2, own, s1, s2, s3, m_new, v_new, sel):
+    g = owned_sum(mine, got, r1, r2)
+    m_new[...], v_new[...], sel[...] = adamw(w[...], m[...], v[...], g)
     n = own.shape[1]
     for step, out in ((0, own), (1, s1), (2, s2), (3, s3)):
         start = pl.multiple_of(lax.rem(place[3] + step, 4) * n, 128)
         out[...] = sel[:, pl.ds(start, n)].astype(out.dtype)
 
 
-def moments_kernel(place, w, m, v, *rest):
-    parts, (first, second, inner) = (rest[:4], rest[4:8]), rest[8:]
-    for f in range(2):
-        g = owned_sum(*parts[f])
-        m_new, v_new, inner_new = adamw(w[:, f, :], m[:, f, :], v[:, f, :], g)
-        first[:, f, :] = m_new
-        second[:, f, :] = v_new
-    inner[...] = inner_new
+def moments_kernel(place, m_key, v_key, w, m, v, mine, got, r1, r2, r3, first, second, inner):
+    g = owned_sum(mine, got, r1, r2, r3)
+    m_new, v_new, inner[...] = adamw(w[...], m[...], v[...], g)
+    first[:, 0, :] = m_key[...]
+    first[:, 1, :] = m_new
+    second[:, 0, :] = v_key[...]
+    second[:, 1, :] = v_new
 
 
 def outer_kernel(place, m0, m1, m2, m3, anchor, momentum, inner, weights, anchor_new, momentum_new, mean):
@@ -193,56 +200,52 @@
     out[...] = far[...]
 
 
-def input_kernel(
-    place, w013, w2a, w2b, v013, v2, k_near, v_near, k_far, v_far, near, far, w_s, c_s, o_s, sem, out_sem
-):
+def input_kernel(place, w013, w2, v013, v2, key, val, out, w_s, o_s, sem, out_sem):
     h, c, x = place[0], place[1], place[2]
-    rows, feat = v2.shape[0], k_near.shape[1]
-    part = w2a.shape[0]
-    tok, wide = far.shape
+    rows, feat = v2.shape[0], key.shape[1]
+    wide = o_s.shape[1]
     pieces = []
-    for core, triple in ((c, w013), (1 - c, v013)):
+    for core, triple, last in ((c, w013, w2), (1 - c, v013, v2)):
         for n, step in enumerate((0, 1, 3)):
-            pieces.append((core, step, 0, triple, n * rows, rows))
-    pieces += [(c, 2, 0, w2a, 0, part), (c, 2, part, w2b, 0, part), (1 - c, 2, 0, v2, 0, rows)]
+            pieces.append((core, step, triple, n * rows))
+        pieces.append((core, 2, last, 0))
     copies = [[], []]
     for f in range(2):
-        for core, step, low, piece, first, n in pieces:
-            start = (2 * lax.rem(x + step, 4) + core) * rows + low
+        for core, step, piece, first in pieces:
+            start = pl.multiple_of((2 * lax.rem(x + step, 4) + core) * rows, 16)
             copies[f].append(
                 pltpu.make_async_copy(
-                    piece.at[pl.ds(first, n), pl.ds(f * feat, feat)],
-                    w_s.at[f, pl.ds(pl.multiple_of(start, 16), n)],
-                    sem.at[9 * f + len(copies[f])],
+                    piece.at[pl.ds(first, rows), pl.ds(f * feat, feat)],
+                    w_s.at[f, pl.ds(start, rows)],
+                    sem.at[8 * f + len(copies[f])],
                 )
             )
-    for n, tokens in enumerate((k_far, k_near, v_far, v_near)):
-        copies[n // 2].append(
-            pltpu.make_async_copy(
-                tokens, c_s.at[n // 2, pl.ds(n % 2 * tok, tok)], sem.at[18 + n]
-            )
-        )
     for copy in copies[0] + copies[1]:
         copy.start()
-    for copy in copies[0] + copies[1]:
+    tile = 384
+    tiles = [slice(j * tile, (j + 1) * tile) for j in range(wide // tile)]
+    dims = (((1,), (1,)), ((), ()))
+    for copy in copies[0]:
         copy.wait()
-    tile = 384
-    dims = (((1,), (1,)), ((), ()))
+    accs = [
+        lax.dot_general(key[...], w_s[0, cols, :], dims, preferred_element_type=F32)
+        for cols in tiles
+    ]
+    for copy in copies[1]:
+        copy.wait()
+    base = h * wide if out.shape[1] > wide else 0
     sends = []
-    for j in range(wide // tile):
-        cols = slice(j * tile, (j + 1) * tile)
-        acc = lax.dot_general(c_s[0], w_s[0, cols, :], dims, preferred_element_type=F32)
-        acc += lax.dot_general(c_s[1], w_s[1, cols, :], dims, preferred_element_type=F32)
-        o_s[:, cols] = acc.astype(BF16)
-        for b, (out, base) in enumerate(((far, 0), (near, h * wide))):
-            sends.append(
-                pltpu.make_async_copy(
-                    o_s.at[pl.ds(b * tok, tok), pl.ds(j * tile, tile)],
-                    out.at[:, pl.ds(pl.multiple_of(base + j * tile, 128), tile)],
-                    out_sem.at[len(sends)],
-                )
+    for j, cols in enumerate(tiles):
+        acc = lax.dot_general(val[...], w_s[1, cols, :], dims, preferred_element_type=F32)
+        o_s[:, cols] = (accs[j] + acc).astype(BF16)
+        sends.append(
+            pltpu.make_async_copy(
+                o_s.at[:, pl.ds(j * tile, tile)],
+                out.at[:, pl.ds(pl.multiple_of(base + j * tile, 128), tile)],
+                out_sem.at[j],
             )
-            sends[-1].start()
+        )
+        sends[-1].start()
     for send in sends:
         send.wait()
 
@@ -272,50 +275,49 @@
         [pltpu.SemaphoreType.DMA],
         moved=2 * tok * width,
     )
-    a_far = shift(a_send, yhi=1)
-    w0, w_key = call(
+    w0 = call(
         rounded_kernel,
-        [shape((rows, 2 * feat)), shape((rows, feat), F32)],
+        shape((rows, 2 * feat)),
         place,
         (after(weight_here, a_send),),
         [half_both],
-        [pl.BlockSpec((hr, 2 * feat), lambda i, place: (i, 0)), half_rows],
+        pl.BlockSpec((hr, 2 * feat), lambda i, place: (i, 0)),
         grid=(2,),
         moved=5 * 2**20,
         weight=WEIGHT,
     )
     w1, w3 = shift(w0, x=-1), shift(w0, x=1)
+    a_far = shift(a_send, yhi=1)
     cot = after(cotangent, w0, a_send)[0]
     key, val = cot[:, 0, :], cot[:, 1, :]
     key_far = shift(key, yhi=1)
 
-    m_key, v_key = call(
+    planes = call(
         planes_kernel,
-        [shape((rows, feat), F32)] * 2,
-        place,
-        (after(first_moment, key)[0], second_moment[0]),
-        [half_both] * 2,
-        [half_rows] * 2,
+        [shape((rows, feat), F32)] * 6,
+        place,
+        (after(weight_here, key), first_moment[0], second_moment[0]),
+        [half_both] * 3,
+        [half_rows] * 6,
         grid=(2,),
-        moved=7 * 2**20,
-        weight=WEIGHT,
-    )
-    planes = (w_key, m_key, v_key)
-    val_far = shift(after(val, m_key), yhi=1)
+        moved=14 * 2**20,
+        vmem=20,
+    )
+    val_far = shift(after(val, planes[0]), yhi=1)
 
     def partial(a, c_own, c_far):
         return call(
             gradient_kernel,
             [shape((4, rows, feat))] * 2,
             place,
-            (acts, a, c_own, c_far),
-            [HBM] * 4,
-            [HBM] * 2,
+            (a, c_own, c_far),
+            [ANY] * 3,
+            [ANY] * 2,
             [
                 pltpu.VMEM((2 * tok, width // 2), BF16),
                 pltpu.VMEM((2 * tok, feat), BF16),
                 pltpu.VMEM((width // 2, feat), BF16),
-                pltpu.SemaphoreType.DMA((4,)),
+                pltpu.SemaphoreType.DMA((3,)),
                 pltpu.SemaphoreType.DMA((8,)),
             ],
             flops=2 * tok * width * feat,
@@ -351,8 +353,33 @@
             weight=weight,
         )
 
-    a_far, w1, w3, planes = lax.optimization_barrier((a_far, w1, w3, planes))
-    def stack(*parts):
+    def blocks(mine, got):
+        return call(
+            blocks_kernel,
+            [shape((rows, feat))] * 3,
+            place,
+            (mine, got) * 3,
+            [block(1), block(1), block(2), block(2), block(3), block(3)],
+            [whole(rows, feat)] * 3,
+            moved=2**22,
+        )
+
+    a_both = call(
+        join_kernel,
+        shape((2 * tok, width // 2)),
+        place,
+        (acts, after(a_far, planes[0])),
+        [
+            pl.BlockSpec((tok, width // 2), lambda i, place: (0, place[0])),
+            whole(tok, width // 2),
+        ],
+        whole(2 * tok, width // 2),
+        moved=5 * 2**20,
+        weight=WEIGHT,
+        vmem=16,
+    )
+    a_both, w1, w3, planes = lax.optimization_barrier((a_both, w1, w3, planes))
+    def stack(*parts, weight=0):
         total = sum(p.shape[0] for p in parts)
         return call(
             stack_kernel,
@@ -362,48 +389,74 @@
             [whole(*p.shape) for p in parts],
             whole(total, 2 * feat),
             moved=2 * 4 * total * feat,
+            weight=weight,
             vmem=20,
         )
 
     w2a, w2b = shift(w3[:hr], x=1), shift(w1[hr:], x=-1)
     w013 = stack(w0, w1, w3)
     v013 = shift(w013, core=1)
-    mine0, other0 = partial(a_far, key, key_far)
+    mine0, other0 = partial(a_both, key, key_far)
     got0 = shift(other0, core=1)
     val_far, w2a, w2b, v013 = lax.optimization_barrier((val_far, w2a, w2b, v013))
-    v2 = shift(stack(w2a, w2b), core=1)
-    mine1, other1 = partial(a_far, val, val_far)
+    w2 = stack(w2a, w2b, weight=WEIGHT)
+    v2 = shift(w2, core=1)
+    up0, down0 = first_hop(mine0, after(got0, w2))
+    up0r, down0r = shift(up0, x=1), shift(down0, x=-1)
+    mine1, other1 = partial(a_both, val, after(val_far, up0))
     got1 = shift(other1, core=1)
-    up0, down0 = first_hop(mine0, after(got0, other1))
-    up0r, down0r = shift(up0, x=1), shift(down0, x=-1)
     to_up0, to_down0 = second_hop(mine0, got0, up0r, after(down0r, other1))
-    from_down0, from_up0 = shift(to_up0, x=1), shift(to_down0, x=-1)
-    up1, down1 = first_hop(mine1, after(got1, to_up0))
-    up1r, down1r = shift(up1, x=1), shift(down1, x=-1)
-
-    near, out_far = call(
-        input_kernel,
-        [shape((tok, width)), shape((tok, width // 2))],
-        place,
-        (after(w013, up1), w2a, w2b, v013, v2, key, val, key_far, val_far),
-        [ANY] * 9,
-        [ANY] * 2,
-        [
-            pltpu.VMEM((2, width // 2, feat), BF16),
-            pltpu.VMEM((2, 2 * tok, feat), BF16),
-            pltpu.VMEM((2 * tok, width // 2), BF16),
-            pltpu.SemaphoreType.DMA((22,)),
-            pltpu.SemaphoreType.DMA((12,)),
-        ],
-        flops=4 * tok * width * feat,
-        moved=16 * 2**20,
+    key_parts = (shift(to_up0, x=1), shift(to_down0, x=-1))
+
+    def input_part(first, key, val, columns, weight=0):
+        return call(
+            input_kernel,
+            shape((tok, columns)),
+            place,
+            (first, w2, v013, v2, key, val),
+            [ANY] * 4 + [whole(tok, feat)] * 2,
+            ANY,
+            [
+                pltpu.VMEM((2, width // 2, feat), BF16),
+                pltpu.VMEM((tok, width // 2), BF16),
+                pltpu.SemaphoreType.DMA((16,)),
+                pltpu.SemaphoreType.DMA((6,)),
+            ],
+            flops=2 * tok * width * feat,
+            moved=12 * 2**20,
+            weight=weight,
+            vmem=20,
+        )
+
+    out_far = input_part(after(w013, to_up0), key_far, val_far, width // 2, WEIGHT)
+    far = shift(out_far, yhi=1)
+    u1, u2, u3 = blocks(mine1, after(got1, out_far))
+    val_parts = (shift(u1, x=1), shift(u3, x=-1))
+    key_parts = after(key_parts, u1)
+
+    half_own = pl.BlockSpec((1, hr, feat), lambda i, place: (place[2], i, 0))
+    qc = feat // 4
+    half_quarter = pl.BlockSpec((hr, qc), lambda i, place: (i, 0))
+    sums0 = (mine0, got0, *key_parts)
+    sum_specs = [half_own] * 2 + [half_rows] * 2
+    own, s1, s2, s3, m_key, v_key = call(
+        selected_kernel,
+        [shape((rows, qc), F32)] + [shape((rows, qc))] * 3 + [shape((rows, feat), F32)] * 2,
+        place,
+        (*planes[:3], *sums0),
+        [half_rows] * 3 + sum_specs,
+        [half_quarter] * 4 + [half_rows] * 2,
+        [pltpu.VMEM((hr, feat), F32)],
+        grid=(2,),
+        moved=10 * 2**20,
         weight=WEIGHT,
-        vmem=20,
-    )
-    far = shift(out_far, yhi=1)
-    to_up1, to_down1 = second_hop(mine1, got1, up1r, after(down1r, out_far))
-    from_down1, from_up1 = shift(to_up1, x=1), shift(to_down1, x=-1)
-    from_up0 = after(from_up0, to_up1)
+    )
+    parts = [shift(part, z=step) for step, part in ((1, s1), (2, s2), (-1, s3))]
+    val_parts = (*val_parts, shift(after(u2, *parts), x=2))
+    total = own
+    for part in parts:
+        total = total + part.astype(F32)
+    near = input_part(after(w013, total), key, val, width)
     input_grad = call(
         far_columns_kernel,
         shape((tok, width)),
@@ -416,38 +469,19 @@
         alias={2: 0},
     )
 
-    half_own = pl.BlockSpec((1, hr, feat), lambda i, place: (place[2], i, 0))
-    qc = feat // 4
-    half_quarter = pl.BlockSpec((hr, qc), lambda i, place: (i, 0))
-    sums0 = (mine0, got0, from_down0, from_up0)
-    sum_specs = [half_own, half_own, half_rows, half_rows]
-    own, s1, s2, s3 = call(
-        selected_kernel,
-        [shape((rows, qc), F32)] + [shape((rows, qc))] * 3,
-        place,
-        (*planes, *sums0),
-        [half_rows] * 3 + sum_specs,
-        [half_quarter] * 4,
-        [pltpu.VMEM((hr, feat), F32)],
-        grid=(2,),
-        moved=10 * 2**20,
-        weight=WEIGHT,
-    )
-    total = own
-    for s, part in ((1, s1), (2, s2), (-1, s3)):
-        total = total + shift(part, z=s).astype(F32)
-    total, from_down1, from_up1 = lax.optimization_barrier((total, from_down1, from_up1))
+    total, r1, r3 = lax.optimization_barrier((total, *val_parts[:2]))
+    val_parts = (r1, r3, val_parts[2])
     total = lax.reduce_precision(total, 8, 7)
     total = total + after(shift(total.astype(BF16), ylo=1), input_grad).astype(F32)
     mean = (total / 8).astype(BF16)
     means = (mean, shift(mean, z=-1), shift(mean, z=2), shift(mean, z=1))
-    sums1 = (mine1, got1, from_down1, from_up1)
+    sums1 = (mine1, got1, *val_parts)
     first_out, second_out, inner = call(
         moments_kernel,
         [shape((rows, 2, feat), F32)] * 2 + [shape((rows, feat), F32)],
         place,
-        (weight_here, first_moment[0], second_moment[0], *sums0, *sums1),
-        [half_both] * 3 + sum_specs * 2,
+        (m_key, v_key, *planes[3:], *sums1),
+        [half_rows] * 5 + sum_specs + [half_rows],
         [half_both] * 2 + [half_rows],
         grid=(2,),
         moved=16 * 2**20,

time: 138 us -> 127 us (0.920)
  waiting for transfers between devices: 50.3 us -> 43.2 us
  starting transfers between devices: 42 us -> 36.1 us
  Pallas kernels: 42.2 us -> 43.7 us
    ppermute x27 -> x26, waiting for transfers between devices: 50.3 us -> 43.2 us  [shift(): return lax.ppermute(value, AXES, pairs)]
    ppermute x27 -> x26, starting transfers between devices: 42 us -> 36.1 us  [shift(): return lax.ppermute(value, AXES, pairs)]
    pallas_call x16 -> x17, Pallas kernels: 42.2 us -> 43.7 us  [call(): pl.pallas_call(kernel, out_shape=out_shape, grid_spec=pltpu.PrefetchScala...]
  transfers between devices with their start and end apart: 27 -> 26, of which waited for: 14 -> 13; matrix products, arithmetic and copies ran while one was open for 0% -> 0% of each run, Pallas kernels for 28% -> 32%
where the time goes in v2:
time: 127 us
  Pallas kernels  43.7 us (34%)
  waiting for transfers between devices  43.2 us (34%)
  starting transfers between devices  36.1 us (28%)
  local copies, waits for them, and re-layouts  2.6 us (2%)
    pallas_call x17, Pallas kernels, call(): pl.pallas_call(kernel, out_shape=out_shape, grid_spec=pltpu.PrefetchScala...  43.7 us
    ppermute x26, waiting for transfers between devices, shift(): return lax.ppermute(value, AXES, pairs)  43.2 us
    ppermute x26, starting transfers between devices, shift(): return lax.ppermute(value, AXES, pairs)  36.1 us
  transfers between devices with their start and end apart: 26, of which 13 were waited for; matrix products, arithmetic and copies ran while one was open for 0% of the time, Pallas kernels for 32%

profile of v2, /device:TPU:0, one launch (start us, length us, event | category | flops | bytes accessed | tf_op | source)
XLA Modules:
  0.0 126.7 jit_solution(6960547372149963370)
XLA Ops:
  0.7 1.7 %copy-done.3 = bf16[1,256,4608]{2,1,0:T(8,128)(2,1)S(1)} copy-done((bf16[1,256,4608]{2,1,0:T(8,128)(2,1)S(1)}, bf16[1,256,4608]{2,1,0:T(8,128)(2,1)}, u32[]{:S(2)}) %copy-start.3) | copy-done | bytes 2359320
  3.0 3.4 %collective-permute-start = (bf16[256,2304]{1,0:T(8,128)(2,1)S(1)}, bf16[256,2304]{1,0:T(8,128)(2,1)S(1)}, u32[]{:S(2)}, u32[]{:S(2)}) collective-permute-start(bf16[256,2304]{1,0:T(8,128)(2,1)S(1)} %shard_map.118), channel_id=1, source_target_pairs={{0,8},{1,9},{2,10},{3,11},{4,12},{5,13},{6,14},{7,15},{8,0},{9,1},... | collective-permute-start | bytes 3538952 | tf_op jit(solution)/shard_map/ppermute | solution.py:28
  6.4 2.9 %shard_map.119.refs_0_ = bf16[288,2048]{1,0:T(8,128)(2,1)S(1)} custom-call(s32[4]{0:T(128)S(1)} %pad_add_fusion.place, f32[288,2,1024]{2,1,0:T(2,128)S(1)} %bitcast.19), custom_call_target="tpu_custom_call" | custom-call | flops 49999998976 | bytes 500000000 | tf_op jit(solution)/shard_map/pallas_call | solution.py:34
  10.9 1.7 %collective-permute-start.1 = (bf16[288,2048]{1,0:T(8,128)(2,1)S(1)}, bf16[288,2048]{1,0:T(8,128)(2,1)S(1)}, u32[]{:S(2)}, u32[]{:S(2)}) collective-permute-start(bf16[288,2048]{1,0:T(8,128)(2,1)S(1)} %shard_map.119.refs_0_), channel_id=1, source_target_pairs={{0,6},{1,7},{2,0},{3,1},{4,2},{5,3},{6,4},{7,5},{8,14},{9,15},{10,... | collective-permute-start | bytes 3538952 | tf_op jit(solution)/shard_map/ppermute | solution.py:28
  14.5 1.8 %shard_map.120 = (f32[288,1024]{1,0:T(8,128)S(1)}, f32[288,1024]{1,0:T(8,128)S(1)}, f32[288,1024]{1,0:T(8,128)S(1)}, f32[288,1024]{1,0:T(8,128)S(1)}, f32[288,1024]{1,0:T(8,128)S(1)}, /*index=5*/f32[288,1024]{1,0:T(8,128)S(1)}) custom-call(s32[4]{0:T(128)S(1)} %pad_add_fusion.place, f32[288,2,1024]{2,1,0:T(2,128)S(1)} %bitcast.20, ...), custom_call_target="tpu_custom_call" | custom-call | tf_op jit(solution)/shard_map/pallas_call | solution.py:34
  16.3 2.2 %collective-permute-start.5 = (bf16[256,1024]{1,0:T(8,128)(2,1)S(1)}, bf16[256,1024]{1,0:T(8,128)(2,1)S(1)}, u32[]{:S(2)}, u32[]{:S(2)}) collective-permute-start(bf16[256,1024]{1,0:T(8,128)(2,1)S(1)} %get-tuple-element.82.c_own.val), channel_id=1, source_target_pairs={{0,8},{1,9},{2,10},{3,11},{4,12},{5,13},{6,14},{7,15},{8,0},{9,1},... | collective-permute-start | bytes 1572872 | tf_op jit(solution)/shard_map/ppermute | solution.py:28
  18.5 14.9 %collective-permute-done.far = bf16[256,2304]{1,0:T(8,128)(2,1)S(1)} collective-permute-done((bf16[256,2304]{1,0:T(8,128)(2,1)S(1)}, bf16[256,2304]{1,0:T(8,128)(2,1)S(1)}, u32[]{:S(2)}, u32[]{:S(2)}) %collective-permute-start) | collective-permute-done | bytes 1179680 | tf_op jit(solution)/shard_map/ppermute | solution.py:28
  34.2 3.8 %collective-permute-done.2.refs_2_ = bf16[288,2048]{1,0:T(8,128)(2,1)S(1)} collective-permute-done((bf16[288,2048]{1,0:T(8,128)(2,1)S(1)}, bf16[288,2048]{1,0:T(8,128)(2,1)S(1)}, u32[]{:S(2)}, u32[]{:S(2)}) %collective-permute-start.2) | collective-permute-done | bytes 1179680 | tf_op jit(solution)/shard_map/ppermute | solution.py:28
  38.9 3.0 %collective-permute-start.7 = (bf16[144,2048]{1,0:T(8,128)(2,1)S(1)}, bf16[144,2048]{1,0:T(8,128)(2,1)S(1)}, u32[]{:S(2)}, u32[]{:S(2)}) collective-permute-start(bf16[144,2048]{1,0:T(8,128)(2,1)S(1)} %slice.15), channel_id=1, source_target_pairs={{0,6},{1,7},{2,0},{3,1},{4,2},{5,3},{6,4},{7,5},{8,14},{9,15},{10,... | collective-permute-start | bytes 1769480 | tf_op jit(solution)/shard_map/ppermute | solution.py:28
  41.9 2.8 %collective-permute-done.3.c_far.key = bf16[256,1024]{1,0:T(8,128)(2,1)S(1)} collective-permute-done((bf16[256,1024]{1,0:T(8,128)(2,1)S(1)}, bf16[256,1024]{1,0:T(8,128)(2,1)S(1)}, u32[]{:S(2)}, u32[]{:S(2)}) %collective-permute-start.3) | collective-permute-done | bytes 524320 | tf_op jit(solution)/shard_map/ppermute | solution.py:28
  44.7 4.7 %shard_map.122 = (bf16[4,288,1024]{2,1,0:T(8,128)(2,1)S(1)}, bf16[4,288,1024]{2,1,0:T(8,128)(2,1)S(1)}) custom-call(s32[4]{0:T(128)S(1)} %pad_add_fusion.place, bf16[512,2304]{1,0:T(8,128)(2,1)S(1)} %shard_map.121.a_both, bf16[256,1024]{1,0:T(8,128)(2,1)S(1)} %get-tuple-element.127.c_own.key, bf16[256,1024]{1,0:T(8,128)(2,1)S(1)} %collective-permute-done.3.c_far.key), custom_call_target="tpu_custom_call" | custom-call | flops 49999998976 | bytes 500000000 | tf_op jit(solution)/shard_map/pallas_call | solution.py:34
  49.5 5.3 %collective-permute-done.5.c_far.val = bf16[256,1024]{1,0:T(8,128)(2,1)S(1)} collective-permute-done((bf16[256,1024]{1,0:T(8,128)(2,1)S(1)}, bf16[256,1024]{1,0:T(8,128)(2,1)S(1)}, u32[]{:S(2)}, u32[]{:S(2)}) %collective-permute-start.5) | collective-permute-done | bytes 524320 | tf_op jit(solution)/shard_map/ppermute | solution.py:28
  54.8 1.6 %collective-permute-done.6.refs_0_ = bf16[144,2048]{1,0:T(8,128)(2,1)S(1)} collective-permute-done((bf16[144,2048]{1,0:T(8,128)(2,1)S(1)}, bf16[144,2048]{1,0:T(8,128)(2,1)S(1)}, u32[]{:S(2)}, u32[]{:S(2)}) %collective-permute-start.6) | collective-permute-done | bytes 589856 | tf_op jit(solution)/shard_map/ppermute | solution.py:28
  57.9 3.2 %collective-permute-start.10 = (bf16[144,1024]{1,0:T(8,128)(2,1)S(1)}, bf16[144,1024]{1,0:T(8,128)(2,1)S(1)}, u32[]{:S(2)}, u32[]{:S(2)}) collective-permute-start(bf16[144,1024]{1,0:T(8,128)(2,1)S(1)} %get-tuple-element.89), channel_id=1, source_target_pairs={{0,6},{1,7},{2,0},{3,1},{4,2},{5,3},{6,4},{7,5},{8,14},{9,15},{10,... | collective-permute-start | bytes 884744 | tf_op jit(solution)/shard_map/ppermute | solution.py:28
  61.2 4.7 %shard_map.126 = (bf16[4,288,1024]{2,1,0:T(8,128)(2,1)S(1)}, bf16[4,288,1024]{2,1,0:T(8,128)(2,1)S(1)}) custom-call(s32[4]{0:T(128)S(1)} %pad_add_fusion.place, bf16[512,2304]{1,0:T(8,128)(2,1)S(1)} %shard_map.121.a_both, bf16[256,1024]{1,0:T(8,128)(2,1)S(1)} %get-tuple-element.82.c_own.val, bf16[256,1024]{1,0:T(8,128)(2,1)S(1)} %collective-permute-done.5.c_far.val), custom_call_target="tpu_custom_call" | custom-call | flops 49999998976 | bytes 500000000 | tf_op jit(solution)/shard_map/pallas_call | solution.py:34
  66.0 1.9 %collective-permute-done.10.down = bf16[144,1024]{1,0:T(8,128)(2,1)S(1)} collective-permute-done((bf16[144,1024]{1,0:T(8,128)(2,1)S(1)}, bf16[144,1024]{1,0:T(8,128)(2,1)S(1)}, u32[]{:S(2)}, u32[]{:S(2)}) %collective-permute-start.10) | collective-permute-done | bytes 294944 | tf_op jit(solution)/shard_map/ppermute | solution.py:28
  69.5 3.2 %collective-permute-start.12 = (bf16[288,1024]{1,0:T(8,128)(2,1)S(1)}, bf16[288,1024]{1,0:T(8,128)(2,1)S(1)}, u32[]{:S(2)}, u32[]{:S(2)}) collective-permute-start(bf16[288,1024]{1,0:T(8,128)(2,1)S(1)} %get-tuple-element.95), channel_id=1, source_target_pairs={{0,6},{1,7},{2,0},{3,1},{4,2},{5,3},{6,4},{7,5},{8,14},{9,15},{10,... | collective-permute-start | bytes 1769480 | tf_op jit(solution)/shard_map/ppermute | solution.py:28
  72.8 6.5 %shard_map.128 = bf16[256,2304]{1,0:T(8,128)(2,1)S(1)} custom-call(s32[4]{0:T(128)S(1)} %pad_add_fusion.place, bf16[864,2048]{1,0:T(8,128)(2,1)S(1)} %shard_map.123.w013, bf16[288,2048]{1,0:T(8,128)(2,1)S(1)} %shard_map.124.w2, bf16[864,2048]{1,0:T(8,128)(2,1)S(1)} %collective-permute-done.8.v013, bf16[288,2048]{1,0:T(8,128)(2,1)S(1)} %collective-permute-done.14.v2, ...), custom_call_target="tpu_custom_call" | custom-call | flops 49999998976 | bytes 500000000 | tf_op jit(solution)/shard_map/pallas_call | solution.py:34
  79.2 1.7 %collective-permute-start.21 = (bf16[256,2304]{1,0:T(8,128)(2,1)S(1)}, bf16[256,2304]{1,0:T(8,128)(2,1)S(1)}, u32[]{:S(2)}, u32[]{:S(2)}) collective-permute-start(bf16[256,2304]{1,0:T(8,128)(2,1)S(1)} %shard_map.128), channel_id=1, source_target_pairs={{0,8},{1,9},{2,10},{3,11},{4,12},{5,13},{6,14},{7,15},{8,0},{9,1},... | collective-permute-start | bytes 3538952 | tf_op jit(solution)/shard_map/ppermute | solution.py:28
  82.3 2.6 %collective-permute-done.12.r2 = bf16[288,1024]{1,0:T(8,128)(2,1)S(1)} collective-permute-done((bf16[288,1024]{1,0:T(8,128)(2,1)S(1)}, bf16[288,1024]{1,0:T(8,128)(2,1)S(1)}, u32[]{:S(2)}, u32[]{:S(2)}) %collective-permute-start.12) | collective-permute-done | bytes 589856 | tf_op jit(solution)/shard_map/ppermute | solution.py:28
  84.9 1.7 %collective-permute-done.11.r1 = bf16[288,1024]{1,0:T(8,128)(2,1)S(1)} collective-permute-done((bf16[288,1024]{1,0:T(8,128)(2,1)S(1)}, bf16[288,1024]{1,0:T(8,128)(2,1)S(1)}, u32[]{:S(2)}, u32[]{:S(2)}) %collective-permute-start.11) | collective-permute-done | bytes 589856 | tf_op jit(solution)/shard_map/ppermute | solution.py:28
  86.6 2.1 %collective-permute-start.19 = (bf16[288,1024]{1,0:T(8,128)(2,1)S(1)}, bf16[288,1024]{1,0:T(8,128)(2,1)S(1)}, u32[]{:S(2)}, u32[]{:S(2)}) collective-permute-start(bf16[288,1024]{1,0:T(8,128)(2,1)S(1)} %get-tuple-element.107), channel_id=1, source_target_pairs={{0,6},{1,7},{2,0},{3,1},{4,2},{5,3},{6,4},{7,5},{8,14},{9,15},{10,... | collective-permute-start | bytes 1769480 | tf_op jit(solution)/shard_map/ppermute | solution.py:28
  88.7 3.1 %shard_map.130 = (f32[288,256]{1,0:T(8,128)S(1)}, bf16[288,256]{1,0:T(8,128)(2,1)S(1)}, bf16[288,256]{1,0:T(8,128)(2,1)S(1)}, bf16[288,256]{1,0:T(8,128)(2,1)S(1...) custom-call(s32[4]{0:T(128)S(1)} %pad_add_fusion.place, f32[288,1024]{1,0:T(8,128)S(1)} %get-tuple-element.76.w, ...), custom_call_target="tpu_custom_call" | custom-call | flops 49999998976 | bytes 500000000 | tf_op jit(solution)/shard_map/pallas_call | solution.py:34
  91.9 2.0 %collective-permute-start.15 = (bf16[288,256]{1,0:T(8,128)(2,1)S(1)}, bf16[288,256]{1,0:T(8,128)(2,1)S(1)}, u32[]{:S(2)}, u32[]{:S(2)}) collective-permute-start(bf16[288,256]{1,0:T(8,128)(2,1)S(1)} %get-tuple-element.104), channel_id=1, source_target_pairs={{0,16},{1,17},{2,18},{3,19},{4,20},{5,21},{6,22},{7,23},{8,24},{9,... | collective-permute-start | bytes 442376 | tf_op jit(solution)/shard_map/ppermute | solution.py:28
  93.9 3.6 %collective-permute-start.16 = (bf16[288,256]{1,0:T(8,128)(2,1)S(1)}, bf16[288,256]{1,0:T(8,128)(2,1)S(1)}, u32[]{:S(2)}, u32[]{:S(2)}) collective-permute-start(bf16[288,256]{1,0:T(8,128)(2,1)S(1)} %get-tuple-element.105), channel_id=1, source_target_pairs={{0,32},{1,33},{2,34},{3,35},{4,36},{5,37},{6,38},{7,39},{8,40},{9,... | collective-permute-start | bytes 442376 | tf_op jit(solution)/shard_map/ppermute | solution.py:28
  97.5 3.2 %collective-permute-done.15 = bf16[288,256]{1,0:T(8,128)(2,1)S(1)} collective-permute-done((bf16[288,256]{1,0:T(8,128)(2,1)S(1)}, bf16[288,256]{1,0:T(8,128)(2,1)S(1)}, u32[]{:S(2)}, u32[]{:S(2)}) %collective-permute-start.15) | collective-permute-done | bytes 147488 | tf_op jit(solution)/shard_map/ppermute | solution.py:28
  102.5 3.3 %collective-permute-done.17 = bf16[288,256]{1,0:T(8,128)(2,1)S(1)} collective-permute-done((bf16[288,256]{1,0:T(8,128)(2,1)S(1)}, bf16[288,256]{1,0:T(8,128)(2,1)S(1)}, u32[]{:S(2)}, u32[]{:S(2)}) %collective-permute-start.17) | collective-permute-done | bytes 147488 | tf_op jit(solution)/shard_map/ppermute | solution.py:28
  106.9 6.1 %shard_map.131.near = bf16[256,4608]{1,0:T(8,128)(2,1)} custom-call(s32[4]{0:T(128)S(1)} %pad_add_fusion.place, bf16[864,2048]{1,0:T(8,128)(2,1)S(1)} %shard_map.123.w013, bf16[288,2048]{1,0:T(8,128)(2,1)S(1)} %shard_map.124.w2, bf16[864,2048]{1,0:T(8,128)(2,1)S(1)} %collective-permute-done.8.v013, bf16[288,2048]{1,0:T(8,128)(2,1)S(1)} %collective-permute-done.14.v2, ...), custom_call_target="tpu_custom_call" | custom-call | tf_op jit(solution)/shard_map/pallas_call | solution.py:34
  113.1 1.6 %shard_map.132 = bf16[256,4608]{1,0:T(8,128)(2,1)} custom-call(s32[4]{0:T(128)S(1)} %pad_add_fusion.place, bf16[256,2304]{1,0:T(8,128)(2,1)S(1)} %collective-permute-done.21.far, bf16[256,4608]{1,0:T(8,128)(2,1)} %shard_map.131.near), custom_call_target="tpu_custom_call", output_to_operand_aliasing={{}: (2, {})} | custom-call | tf_op jit(solution)/shard_map/pallas_call | solution.py:34
  114.8 3.5 %collective-permute-start.23 = (bf16[288,256]{1,0:T(8,128)(2,1)S(1)}, bf16[288,256]{1,0:T(8,128)(2,1)S(1)}, u32[]{:S(2)}, u32[]{:S(2)}) collective-permute-start(bf16[288,256]{1,0:T(8,128)(2,1)S(1)} %multiply_convert_fusion.m0), channel_id=1, source_target_pairs={{0,32},{1,33},{2,34},{3,35},{4,36},{5,37},{6,38},{7,39},{8,40},{9,... | collective-permute-start | bytes 442376 | tf_op jit(solution)/shard_map/ppermute | solution.py:28
  119.5 3.9 %shard_map.133 = (f32[288,2,1024]{2,1,0:T(2,128)}, f32[288,2,1024]{2,1,0:T(2,128)}, f32[288,1024]{1,0:T(8,128)S(1)}) custom-call(s32[4]{0:T(128)S(1)} %pad_add_fusion.place, f32[288,1024]{1,0:T(8,128)S(1)} %get-tuple-element.111.m_key, f32[288,1024]{1,0:T(8,128)S(1)} %get-tuple-element.112.v_key, f32[288,1024]{1,0:T(8,128)S(1)} %get-tuple-element.113.w, ...), custom_call_target="tpu_custom_call" | custom-call | tf_op jit(solution)/shard_map/pallas_call | solution.py:34
  123.6 3.1 %shard_map.134 = (f32[288,2,1024]{2,1,0:T(2,128)}, f32[288,1024]{1,0:T(8,128)}, f32[288,1024]{1,0:T(8,128)}) custom-call(s32[4]{0:T(128)S(1)} %pad_add_fusion.place, bf16[288,256]{1,0:T(8,128)(2,1)S(1)} %multiply_convert_fusion.m0, bf16[288,256]{1,0:T(8,128)(2,1)S(1)} %collective-permute-done.22.m1, bf16[288,256]{1,0:T(8,128)(2,1)S(1)} %collective-permute-done.23.m2, ...), custom_call_target="tpu_custom_call" | custom-call | tf_op jit(solution)/shard_map/pallas_call | solution.py:34
  (65 shorter events, 14.8 us)
Async XLA Ops:
  3.0 30.4 %collective-permute-start = (bf16[256,2304]{1,0:T(8,128)(2,1)S(1)}, bf16[256,2304]{1,0:T(8,128)(2,1)S(1)}, u32[]{:S(2)}, u32[]{:S(2)}) collective-permute-start(bf16[256,2304]{1,0:T(8,128)(2,1)S(1)} %shard_map.118), channel_id=1, source_target_pairs={{0,8},{1,9},{2,10},{3,11},{4,12},{5,13},{6,14},{7,15},{8,0},{9,1},... | collective-permute-start | bytes 3538952 | tf_op jit(solution)/shard_map/ppermute | solution.py:28
  6.4 6.2 %copy-start.9 = (bf16[1,256,2,1024]{3,2,1,0:T(2,128)(2,1)S(1)}, bf16[1,256,2,1024]{3,2,1,0:T(2,128)(2,1)}, u32[]{:S(2)}) copy-start(bf16[1,256,2,1024]{3,2,1,0:T(2,128)(2,1)} %param.8) | copy-start | bytes 3145732
  6.4 7.6 %copy-start.2 = (f32[1,288,2,1024]{3,2,1,0:T(2,128)S(1)}, f32[1,288,2,1024]{3,2,1,0:T(2,128)}, u32[]{:S(2)}) copy-start(f32[1,288,2,1024]{3,2,1,0:T(2,128)} %param.11) | copy-start | bytes 7077892
  9.3 28.7 %collective-permute-start.2 = (bf16[288,2048]{1,0:T(8,128)(2,1)S(1)}, bf16[288,2048]{1,0:T(8,128)(2,1)S(1)}, u32[]{:S(2)}, u32[]{:S(2)}) collective-permute-start(bf16[288,2048]{1,0:T(8,128)(2,1)S(1)} %shard_map.119.refs_0_), channel_id=1, source_target_pairs={{0,2},{1,3},{2,4},{3,5},{4,6},{5,7},{6,0},{7,1},{8,10},{9,11},{10,... | collective-permute-start | bytes 3538952 | tf_op jit(solution)/shard_map/ppermute | solution.py:28
  10.9 27.1 %collective-permute-start.1 = (bf16[288,2048]{1,0:T(8,128)(2,1)S(1)}, bf16[288,2048]{1,0:T(8,128)(2,1)S(1)}, u32[]{:S(2)}, u32[]{:S(2)}) collective-permute-start(bf16[288,2048]{1,0:T(8,128)(2,1)S(1)} %shard_map.119.refs_0_), channel_id=1, source_target_pairs={{0,6},{1,7},{2,0},{3,1},{4,2},{5,3},{6,4},{7,5},{8,14},{9,15},{10,... | collective-permute-start | bytes 3538952 | tf_op jit(solution)/shard_map/ppermute | solution.py:28
  13.0 31.7 %copy-start.5 = (bf16[256,1024]{1,0:T(8,128)(2,1)}, bf16[256,1024]{1,0:T(8,128)(2,1)S(1)}, u32[]{:S(2)}) copy-start(bf16[256,1024]{1,0:T(8,128)(2,1)S(1)} %get-tuple-element.127.c_own.key) | copy-start | bytes 1572868
  13.0 31.7 %collective-permute-start.3 = (bf16[256,1024]{1,0:T(8,128)(2,1)S(1)}, bf16[256,1024]{1,0:T(8,128)(2,1)S(1)}, u32[]{:S(2)}, u32[]{:S(2)}) collective-permute-start(bf16[256,1024]{1,0:T(8,128)(2,1)S(1)} %get-tuple-element.127.c_own.key), channel_id=1, source_target_pairs={{0,8},{1,9},{2,10},{3,11},{4,12},{5,13},{6,14},{7,15},{8,0},{9,1},... | collective-permute-start | bytes 1572872 | tf_op jit(solution)/shard_map/ppermute | solution.py:28
  14.5 19.0 %copy-start.4 = (bf16[1,256,4608]{2,1,0:T(8,128)(2,1)S(1)}, bf16[1,256,4608]{2,1,0:T(8,128)(2,1)}, u32[]{:S(2)}) copy-start(bf16[1,256,4608]{2,1,0:T(8,128)(2,1)} %param.7) | copy-start | bytes 7077892
  16.3 38.5 %collective-permute-start.5 = (bf16[256,1024]{1,0:T(8,128)(2,1)S(1)}, bf16[256,1024]{1,0:T(8,128)(2,1)S(1)}, u32[]{:S(2)}, u32[]{:S(2)}) collective-permute-start(bf16[256,1024]{1,0:T(8,128)(2,1)S(1)} %get-tuple-element.82.c_own.val), channel_id=1, source_target_pairs={{0,8},{1,9},{2,10},{3,11},{4,12},{5,13},{6,14},{7,15},{8,0},{9,1},... | collective-permute-start | bytes 1572872 | tf_op jit(solution)/shard_map/ppermute | solution.py:28
  38.9 15.9 %collective-permute-start.7 = (bf16[144,2048]{1,0:T(8,128)(2,1)S(1)}, bf16[144,2048]{1,0:T(8,128)(2,1)S(1)}, u32[]{:S(2)}, u32[]{:S(2)}) collective-permute-start(bf16[144,2048]{1,0:T(8,128)(2,1)S(1)} %slice.15), channel_id=1, source_target_pairs={{0,6},{1,7},{2,0},{3,1},{4,2},{5,3},{6,4},{7,5},{8,14},{9,15},{10,... | collective-permute-start | bytes 1769480 | tf_op jit(solution)/shard_map/ppermute | solution.py:28
  41.9 14.5 %collective-permute-start.6 = (bf16[144,2048]{1,0:T(8,128)(2,1)S(1)}, bf16[144,2048]{1,0:T(8,128)(2,1)S(1)}, u32[]{:S(2)}, u32[]{:S(2)}) collective-permute-start(bf16[144,2048]{1,0:T(8,128)(2,1)S(1)} %slice.14), channel_id=1, source_target_pairs={{0,2},{1,3},{2,4},{3,5},{4,6},{5,7},{6,0},{7,1},{8,10},{9,11},{10,... | collective-permute-start | bytes 1769480 | tf_op jit(solution)/shard_map/ppermute | solution.py:28
  41.9 14.5 %collective-permute-start.8 = (bf16[864,2048]{1,0:T(8,128)(2,1)S(1)}, bf16[864,2048]{1,0:T(8,128)(2,1)S(1)}, u32[]{:S(2)}, u32[]{:S(2)}) collective-permute-start(bf16[864,2048]{1,0:T(8,128)(2,1)S(1)} %shard_map.123.w013), channel_id=1, source_target_pairs={{0,1},{1,0},{2,3},{3,2},{4,5},{5,4},{6,7},{7,6},{8,9},{9,8},{10,11... | collective-permute-start | bytes 10616840 | tf_op jit(solution)/shard_map/ppermute | solution.py:28
  49.4 7.8 %collective-permute-start.4 = (bf16[4,288,1024]{2,1,0:T(8,128)(2,1)S(1)}, bf16[4,288,1024]{2,1,0:T(8,128)(2,1)S(1)}, u32[]{:S(2)}, u32[]{:S(2)}) collective-permute-start(bf16[4,288,1024]{2,1,0:T(8,128)(2,1)S(1)} %get-tuple-element.81), channel_id=1, source_target_pairs={{0,1},{1,0},{2,3},{3,2},{4,5},{5,4},{6,7},{7,6},{8,9},{9,8},{10,11... | collective-permute-start | bytes 7077896 | tf_op jit(solution)/shard_map/ppermute | solution.py:28
  57.1 15.7 %collective-permute-start.14 = (bf16[288,2048]{1,0:T(8,128)(2,1)S(1)}, bf16[288,2048]{1,0:T(8,128)(2,1)S(1)}, u32[]{:S(2)}, u32[]{:S(2)}) collective-permute-start(bf16[288,2048]{1,0:T(8,128)(2,1)S(1)} %shard_map.124.w2), channel_id=1, source_target_pairs={{0,1},{1,0},{2,3},{3,2},{4,5},{5,4},{6,7},{7,6},{8,9},{9,8},{10,11... | collective-permute-start | bytes 3538952 | tf_op jit(solution)/shard_map/ppermute | solution.py:28
  57.9 10.7 %collective-permute-start.9 = (bf16[144,1024]{1,0:T(8,128)(2,1)S(1)}, bf16[144,1024]{1,0:T(8,128)(2,1)S(1)}, u32[]{:S(2)}, u32[]{:S(2)}) collective-permute-start(bf16[144,1024]{1,0:T(8,128)(2,1)S(1)} %get-tuple-element.88), channel_id=1, source_target_pairs={{0,2},{1,3},{2,4},{3,5},{4,6},{5,7},{6,0},{7,1},{8,10},{9,11},{10,... | collective-permute-start | bytes 884744 | tf_op jit(solution)/shard_map/ppermute | solution.py:28
  57.9 9.9 %collective-permute-start.10 = (bf16[144,1024]{1,0:T(8,128)(2,1)S(1)}, bf16[144,1024]{1,0:T(8,128)(2,1)S(1)}, u32[]{:S(2)}, u32[]{:S(2)}) collective-permute-start(bf16[144,1024]{1,0:T(8,128)(2,1)S(1)} %get-tuple-element.89), channel_id=1, source_target_pairs={{0,6},{1,7},{2,0},{3,1},{4,2},{5,3},{6,4},{7,5},{8,14},{9,15},{10,... | collective-permute-start | bytes 884744 | tf_op jit(solution)/shard_map/ppermute | solution.py:28
  65.9 15.1 %collective-permute-start.13 = (bf16[4,288,1024]{2,1,0:T(8,128)(2,1)S(1)}, bf16[4,288,1024]{2,1,0:T(8,128)(2,1)S(1)}, u32[]{:S(2)}, u32[]{:S(2)}) collective-permute-start(bf16[4,288,1024]{2,1,0:T(8,128)(2,1)S(1)} %get-tuple-element.92), channel_id=1, source_target_pairs={{0,1},{1,0},{2,3},{3,2},{4,5},{5,4},{6,7},{7,6},{8,9},{9,8},{10,11... | collective-permute-start | bytes 7077896 | tf_op jit(solution)/shard_map/ppermute | solution.py:28
  69.4 17.1 %collective-permute-start.11 = (bf16[288,1024]{1,0:T(8,128)(2,1)S(1)}, bf16[288,1024]{1,0:T(8,128)(2,1)S(1)}, u32[]{:S(2)}, u32[]{:S(2)}) collective-permute-start(bf16[288,1024]{1,0:T(8,128)(2,1)S(1)} %get-tuple-element.94), channel_id=1, source_target_pairs={{0,2},{1,3},{2,4},{3,5},{4,6},{5,7},{6,0},{7,1},{8,10},{9,11},{10,... | collective-permute-start | bytes 1769480 | tf_op jit(solution)/shard_map/ppermute | solution.py:28
  69.5 15.4 %collective-permute-start.12 = (bf16[288,1024]{1,0:T(8,128)(2,1)S(1)}, bf16[288,1024]{1,0:T(8,128)(2,1)S(1)}, u32[]{:S(2)}, u32[]{:S(2)}) collective-permute-start(bf16[288,1024]{1,0:T(8,128)(2,1)S(1)} %get-tuple-element.95), channel_id=1, source_target_pairs={{0,6},{1,7},{2,0},{3,1},{4,2},{5,3},{6,4},{7,5},{8,14},{9,15},{10,... | collective-permute-start | bytes 1769480 | tf_op jit(solution)/shard_map/ppermute | solution.py:28
  79.2 33.8 %collective-permute-start.21 = (bf16[256,2304]{1,0:T(8,128)(2,1)S(1)}, bf16[256,2304]{1,0:T(8,128)(2,1)S(1)}, u32[]{:S(2)}, u32[]{:S(2)}) collective-permute-start(bf16[256,2304]{1,0:T(8,128)(2,1)S(1)} %shard_map.128), channel_id=1, source_target_pairs={{0,8},{1,9},{2,10},{3,11},{4,12},{5,13},{6,14},{7,15},{8,0},{9,1},... | collective-permute-start | bytes 3538952 | tf_op jit(solution)/shard_map/ppermute | solution.py:28
  81.9 24.0 %collective-permute-start.18 = (bf16[288,1024]{1,0:T(8,128)(2,1)S(1)}, bf16[288,1024]{1,0:T(8,128)(2,1)S(1)}, u32[]{:S(2)}, u32[]{:S(2)}) collective-permute-start(bf16[288,1024]{1,0:T(8,128)(2,1)S(1)} %get-tuple-element.100), channel_id=1, source_target_pairs={{0,2},{1,3},{2,4},{3,5},{4,6},{5,7},{6,0},{7,1},{8,10},{9,11},{10,... | collective-permute-start | bytes 1769480 | tf_op jit(solution)/shard_map/ppermute | solution.py:28
  86.6 19.3 %collective-permute-start.19 = (bf16[288,1024]{1,0:T(8,128)(2,1)S(1)}, bf16[288,1024]{1,0:T(8,128)(2,1)S(1)}, u32[]{:S(2)}, u32[]{:S(2)}) collective-permute-start(bf16[288,1024]{1,0:T(8,128)(2,1)S(1)} %get-tuple-element.107), channel_id=1, source_target_pairs={{0,6},{1,7},{2,0},{3,1},{4,2},{5,3},{6,4},{7,5},{8,14},{9,15},{10,... | collective-permute-start | bytes 1769480 | tf_op jit(solution)/shard_map/ppermute | solution.py:28
  91.9 15.1 %copy-start.6 = (bf16[256,1024]{1,0:T(8,128)(2,1)S(1)}, bf16[256,1024]{1,0:T(8,128)(2,1)}, u32[]{:S(2)}) copy-start(bf16[256,1024]{1,0:T(8,128)(2,1)} %copy-done.5) | copy-start | bytes 1572868
  91.9 8.8 %collective-permute-start.15 = (bf16[288,256]{1,0:T(8,128)(2,1)S(1)}, bf16[288,256]{1,0:T(8,128)(2,1)S(1)}, u32[]{:S(2)}, u32[]{:S(2)}) collective-permute-start(bf16[288,256]{1,0:T(8,128)(2,1)S(1)} %get-tuple-element.104), channel_id=1, source_target_pairs={{0,16},{1,17},{2,18},{3,19},{4,20},{5,21},{6,22},{7,23},{8,24},{9,... | collective-permute-start | bytes 442376 | tf_op jit(solution)/shard_map/ppermute | solution.py:28
  93.9 8.6 %collective-permute-start.16 = (bf16[288,256]{1,0:T(8,128)(2,1)S(1)}, bf16[288,256]{1,0:T(8,128)(2,1)S(1)}, u32[]{:S(2)}, u32[]{:S(2)}) collective-permute-start(bf16[288,256]{1,0:T(8,128)(2,1)S(1)} %get-tuple-element.105), channel_id=1, source_target_pairs={{0,32},{1,33},{2,34},{3,35},{4,36},{5,37},{6,38},{7,39},{8,40},{9,... | collective-permute-start | bytes 442376 | tf_op jit(solution)/shard_map/ppermute | solution.py:28
  100.7 5.1 %collective-permute-start.17 = (bf16[288,256]{1,0:T(8,128)(2,1)S(1)}, bf16[288,256]{1,0:T(8,128)(2,1)S(1)}, u32[]{:S(2)}, u32[]{:S(2)}) collective-permute-start(bf16[288,256]{1,0:T(8,128)(2,1)S(1)} %get-tuple-element.106), channel_id=1, source_target_pairs={{0,48},{1,49},{2,50},{3,51},{4,52},{5,53},{6,54},{7,55},{8,56},{9,... | collective-permute-start | bytes 442376 | tf_op jit(solution)/shard_map/ppermute | solution.py:28
  105.8 13.6 %collective-permute-start.25 = (bf16[288,1024]{1,0:T(8,128)(2,1)S(1)}, bf16[288,1024]{1,0:T(8,128)(2,1)S(1)}, u32[]{:S(2)}, u32[]{:S(2)}) collective-permute-start(bf16[288,1024]{1,0:T(8,128)(2,1)S(1)} %get-tuple-element.119), channel_id=1, source_target_pairs={{0,4},{1,5},{2,6},{3,7},{4,0},{5,1},{6,2},{7,3},{8,12},{9,13},{10,... | collective-permute-start | bytes 1769480 | tf_op jit(solution)/shard_map/ppermute | solution.py:28
  106.0 8.7 %collective-permute-start.20 = (bf16[288,256]{1,0:T(8,128)(2,1)S(1)}, bf16[288,256]{1,0:T(8,128)(2,1)S(1)}, u32[]{:S(2)}, u32[]{:S(2)}) collective-permute-start(bf16[288,256]{1,0:T(8,128)(2,1)S(1)} %reduce-precision_convert_fusion), channel_id=1, source_target_pairs={{0,64},{1,65},{2,66},{3,67},{4,68},{5,69},{6,70},{7,71},{8,72},{9,... | collective-permute-start | bytes 442376 | tf_op jit(solution)/shard_map/ppermute | solution.py:28
  114.7 8.6 %collective-permute-start.24 = (bf16[288,256]{1,0:T(8,128)(2,1)S(1)}, bf16[288,256]{1,0:T(8,128)(2,1)S(1)}, u32[]{:S(2)}, u32[]{:S(2)}) collective-permute-start(bf16[288,256]{1,0:T(8,128)(2,1)S(1)} %multiply_convert_fusion.m0), channel_id=1, source_target_pairs={{0,16},{1,17},{2,18},{3,19},{4,20},{5,21},{6,22},{7,23},{8,24},{9,... | collective-permute-start | bytes 442376 | tf_op jit(solution)/shard_map/ppermute | solution.py:28
  114.8 8.6 %collective-permute-start.23 = (bf16[288,256]{1,0:T(8,128)(2,1)S(1)}, bf16[288,256]{1,0:T(8,128)(2,1)S(1)}, u32[]{:S(2)}, u32[]{:S(2)}) collective-permute-start(bf16[288,256]{1,0:T(8,128)(2,1)S(1)} %multiply_convert_fusion.m0), channel_id=1, source_target_pairs={{0,32},{1,33},{2,34},{3,35},{4,36},{5,37},{6,38},{7,39},{8,40},{9,... | collective-permute-start | bytes 442376 | tf_op jit(solution)/shard_map/ppermute | solution.py:28
  118.3 5.3 %collective-permute-start.22 = (bf16[288,256]{1,0:T(8,128)(2,1)S(1)}, bf16[288,256]{1,0:T(8,128)(2,1)S(1)}, u32[]{:S(2)}, u32[]{:S(2)}) collective-permute-start(bf16[288,256]{1,0:T(8,128)(2,1)S(1)} %multiply_convert_fusion.m0), channel_id=1, source_target_pairs={{0,48},{1,49},{2,50},{3,51},{4,52},{5,53},{6,54},{7,55},{8,56},{9,... | collective-permute-start | bytes 442376 | tf_op jit(solution)/shard_map/ppermute | solution.py:28
  119.5 4.1 %copy-start.8 = (f32[288,1024]{1,0:T(8,128)S(1)}, f32[288,1024]{1,0:T(8,128)}, u32[]{:S(2)}) copy-start(f32[288,1024]{1,0:T(8,128)} %momentum.1) | copy-start | bytes 3538948
  (4 other events, 11.6 us)

commit v3 on v2

--- a/solution.py
+++ b/solution.py
@@ -145,11 +145,6 @@
     to_down[n:] = (part[n:] + down[...].astype(F32)).astype(BF16)
 
 
-def blocks_kernel(place, *refs):
-    for n, out in enumerate(refs[6:]):
-        out[...] = block_sum(refs[2 * n], refs[2 * n + 1]).astype(BF16)
-
-
 def owned_sum(mine, got, *others):
     total = block_sum(mine, got)
     for other in others:
@@ -173,8 +168,8 @@
         out[...] = sel[:, pl.ds(start, n)].astype(out.dtype)
 
 
-def moments_kernel(place, m_key, v_key, w, m, v, mine, got, r1, r2, r3, first, second, inner):
-    g = owned_sum(mine, got, r1, r2, r3)
+def moments_kernel(place, m_key, v_key, w, m, v, mine, got, r1, r2, first, second, inner):
+    g = owned_sum(mine, got, r1, r2)
     m_new, v_new, inner[...] = adamw(w[...], m[...], v[...], g)
     first[:, 0, :] = m_key[...]
     first[:, 1, :] = m_new
@@ -353,17 +348,6 @@
             weight=weight,
         )
 
-    def blocks(mine, got):
-        return call(
-            blocks_kernel,
-            [shape((rows, feat))] * 3,
-            place,
-            (mine, got) * 3,
-            [block(1), block(1), block(2), block(2), block(3), block(3)],
-            [whole(rows, feat)] * 3,
-            moved=2**22,
-        )
-
     a_both = call(
         join_kernel,
         shape((2 * tok, width // 2)),
@@ -430,9 +414,9 @@
 
     out_far = input_part(after(w013, to_up0), key_far, val_far, width // 2, WEIGHT)
     far = shift(out_far, yhi=1)
-    u1, u2, u3 = blocks(mine1, after(got1, out_far))
-    val_parts = (shift(u1, x=1), shift(u3, x=-1))
-    key_parts = after(key_parts, u1)
+    up1, down1 = first_hop(mine1, after(got1, out_far))
+    up1r, down1r = shift(up1, x=1), shift(down1, x=-1)
+    key_parts = after(key_parts, up1)
 
     half_own = pl.BlockSpec((1, hr, feat), lambda i, place: (place[2], i, 0))
     qc = feat // 4
@@ -451,8 +435,9 @@
         moved=10 * 2**20,
         weight=WEIGHT,
     )
+    to_up1, to_down1 = second_hop(mine1, got1, up1r, after(down1r, own))
+    val_parts = (shift(to_up1, x=1), shift(to_down1, x=-1))
     parts = [shift(part, z=step) for step, part in ((1, s1), (2, s2), (-1, s3))]
-    val_parts = (*val_parts, shift(after(u2, *parts), x=2))
     total = own
     for part in parts:
         total = total + part.astype(F32)
@@ -469,8 +454,6 @@
         alias={2: 0},
     )
 
-    total, r1, r3 = lax.optimization_barrier((total, *val_parts[:2]))
-    val_parts = (r1, r3, val_parts[2])
     total = lax.reduce_precision(total, 8, 7)
     total = total + after(shift(total.astype(BF16), ylo=1), input_grad).astype(F32)
     mean = (total / 8).astype(BF16)
@@ -481,7 +464,7 @@
         [shape((rows, 2, feat), F32)] * 2 + [shape((rows, feat), F32)],
         place,
         (m_key, v_key, *planes[3:], *sums1),
-        [half_rows] * 5 + sum_specs + [half_rows],
+        [half_rows] * 5 + sum_specs,
         [half_both] * 2 + [half_rows],
         grid=(2,),
         moved=16 * 2**20,

time: 127 us -> 125 us (0.984)
  waiting for transfers between devices: 43.2 us -> 37.4 us
  starting transfers between devices: 36.1 us -> 39.6 us
    ppermute x26 -> x27, waiting for transfers between devices: 43.2 us -> 37.4 us  [shift(): return lax.ppermute(value, AXES, pairs)]
    ppermute x26 -> x27, starting transfers between devices: 36.1 us -> 39.6 us  [shift(): return lax.ppermute(value, AXES, pairs)]
    pallas_call x17 -> x18, Pallas kernels: 43.7 us -> 44.2 us  [call(): pl.pallas_call(kernel, out_shape=out_shape, grid_spec=pltpu.PrefetchScala...]
  transfers between devices with their start and end apart: 26 -> 27, of which waited for: 13 -> 11; matrix products, arithmetic and copies ran while one was open for 0% -> 0% of each run, Pallas kernels for 32% -> 32%
where the time goes in v3:
time: 125 us
  Pallas kernels  44.2 us (35%)
  starting transfers between devices  39.6 us (32%)
  waiting for transfers between devices  37.4 us (30%)
  local copies, waits for them, and re-layouts  2.61 us (2%)
    pallas_call x18, Pallas kernels, call(): pl.pallas_call(kernel, out_shape=out_shape, grid_spec=pltpu.PrefetchScala...  44.2 us
    ppermute x27, starting transfers between devices, shift(): return lax.ppermute(value, AXES, pairs)  39.6 us
    ppermute x27, waiting for transfers between devices, shift(): return lax.ppermute(value, AXES, pairs)  37.4 us
  transfers between devices with their start and end apart: 27, of which 11 were waited for; matrix products, arithmetic and copies ran while one was open for 0% of the time, Pallas kernels for 32%

profile of v3, /device:TPU:0, one launch (start us, length us, event | category | flops | bytes accessed | tf_op | source)
XLA Modules:
  0.0 124.9 jit_solution(6031288493508196097)
XLA Ops:
  0.7 1.7 %copy-done.3 = bf16[1,256,4608]{2,1,0:T(8,128)(2,1)S(1)} copy-done((bf16[1,256,4608]{2,1,0:T(8,128)(2,1)S(1)}, bf16[1,256,4608]{2,1,0:T(8,128)(2,1)}, u32[]{:S(2)}) %copy-start.3) | copy-done | bytes 2359320
  3.0 3.4 %collective-permute-start = (bf16[256,2304]{1,0:T(8,128)(2,1)S(1)}, bf16[256,2304]{1,0:T(8,128)(2,1)S(1)}, u32[]{:S(2)}, u32[]{:S(2)}) collective-permute-start(bf16[256,2304]{1,0:T(8,128)(2,1)S(1)} %shard_map.118), channel_id=1, source_target_pairs={{0,8},{1,9},{2,10},{3,11},{4,12},{5,13},{6,14},{7,15},{8,0},{9,1},... | collective-permute-start | bytes 3538952 | tf_op jit(solution)/shard_map/ppermute | solution.py:28
  6.4 2.9 %shard_map.119.refs_0_ = bf16[288,2048]{1,0:T(8,128)(2,1)S(1)} custom-call(s32[4]{0:T(128)S(1)} %pad_add_fusion.place, f32[288,2,1024]{2,1,0:T(2,128)S(1)} %bitcast.19), custom_call_target="tpu_custom_call" | custom-call | flops 49999998976 | bytes 500000000 | tf_op jit(solution)/shard_map/pallas_call | solution.py:34
  10.9 1.7 %collective-permute-start.1 = (bf16[288,2048]{1,0:T(8,128)(2,1)S(1)}, bf16[288,2048]{1,0:T(8,128)(2,1)S(1)}, u32[]{:S(2)}, u32[]{:S(2)}) collective-permute-start(bf16[288,2048]{1,0:T(8,128)(2,1)S(1)} %shard_map.119.refs_0_), channel_id=1, source_target_pairs={{0,6},{1,7},{2,0},{3,1},{4,2},{5,3},{6,4},{7,5},{8,14},{9,15},{10,... | collective-permute-start | bytes 3538952 | tf_op jit(solution)/shard_map/ppermute | solution.py:28
  14.5 1.8 %shard_map.120 = (f32[288,1024]{1,0:T(8,128)S(1)}, f32[288,1024]{1,0:T(8,128)S(1)}, f32[288,1024]{1,0:T(8,128)S(1)}, f32[288,1024]{1,0:T(8,128)S(1)}, f32[288,1024]{1,0:T(8,128)S(1)}, /*index=5*/f32[288,1024]{1,0:T(8,128)S(1)}) custom-call(s32[4]{0:T(128)S(1)} %pad_add_fusion.place, f32[288,2,1024]{2,1,0:T(2,128)S(1)} %bitcast.20, ...), custom_call_target="tpu_custom_call" | custom-call | tf_op jit(solution)/shard_map/pallas_call | solution.py:34
  16.3 2.2 %collective-permute-start.5 = (bf16[256,1024]{1,0:T(8,128)(2,1)S(1)}, bf16[256,1024]{1,0:T(8,128)(2,1)S(1)}, u32[]{:S(2)}, u32[]{:S(2)}) collective-permute-start(bf16[256,1024]{1,0:T(8,128)(2,1)S(1)} %get-tuple-element.80.c_own.val), channel_id=1, source_target_pairs={{0,8},{1,9},{2,10},{3,11},{4,12},{5,13},{6,14},{7,15},{8,0},{9,1},... | collective-permute-start | bytes 1572872 | tf_op jit(solution)/shard_map/ppermute | solution.py:28
  18.5 14.9 %collective-permute-done.far = bf16[256,2304]{1,0:T(8,128)(2,1)S(1)} collective-permute-done((bf16[256,2304]{1,0:T(8,128)(2,1)S(1)}, bf16[256,2304]{1,0:T(8,128)(2,1)S(1)}, u32[]{:S(2)}, u32[]{:S(2)}) %collective-permute-start) | collective-permute-done | bytes 1179680 | tf_op jit(solution)/shard_map/ppermute | solution.py:28
  34.2 3.8 %collective-permute-done.2.refs_2_ = bf16[288,2048]{1,0:T(8,128)(2,1)S(1)} collective-permute-done((bf16[288,2048]{1,0:T(8,128)(2,1)S(1)}, bf16[288,2048]{1,0:T(8,128)(2,1)S(1)}, u32[]{:S(2)}, u32[]{:S(2)}) %collective-permute-start.2) | collective-permute-done | bytes 1179680 | tf_op jit(solution)/shard_map/ppermute | solution.py:28
  38.9 3.0 %collective-permute-start.7 = (bf16[144,2048]{1,0:T(8,128)(2,1)S(1)}, bf16[144,2048]{1,0:T(8,128)(2,1)S(1)}, u32[]{:S(2)}, u32[]{:S(2)}) collective-permute-start(bf16[144,2048]{1,0:T(8,128)(2,1)S(1)} %slice.15), channel_id=1, source_target_pairs={{0,6},{1,7},{2,0},{3,1},{4,2},{5,3},{6,4},{7,5},{8,14},{9,15},{10,... | collective-permute-start | bytes 1769480 | tf_op jit(solution)/shard_map/ppermute | solution.py:28
  41.9 2.8 %collective-permute-done.3.c_far.key = bf16[256,1024]{1,0:T(8,128)(2,1)S(1)} collective-permute-done((bf16[256,1024]{1,0:T(8,128)(2,1)S(1)}, bf16[256,1024]{1,0:T(8,128)(2,1)S(1)}, u32[]{:S(2)}, u32[]{:S(2)}) %collective-permute-start.3) | collective-permute-done | bytes 524320 | tf_op jit(solution)/shard_map/ppermute | solution.py:28
  44.7 4.7 %shard_map.122 = (bf16[4,288,1024]{2,1,0:T(8,128)(2,1)S(1)}, bf16[4,288,1024]{2,1,0:T(8,128)(2,1)S(1)}) custom-call(s32[4]{0:T(128)S(1)} %pad_add_fusion.place, bf16[512,2304]{1,0:T(8,128)(2,1)S(1)} %shard_map.121.a_both, bf16[256,1024]{1,0:T(8,128)(2,1)S(1)} %get-tuple-element.125.c_own.key, bf16[256,1024]{1,0:T(8,128)(2,1)S(1)} %collective-permute-done.3.c_far.key), custom_call_target="tpu_custom_call" | custom-call | flops 49999998976 | bytes 500000000 | tf_op jit(solution)/shard_map/pallas_call | solution.py:34
  49.5 5.3 %collective-permute-done.5.c_far.val = bf16[256,1024]{1,0:T(8,128)(2,1)S(1)} collective-permute-done((bf16[256,1024]{1,0:T(8,128)(2,1)S(1)}, bf16[256,1024]{1,0:T(8,128)(2,1)S(1)}, u32[]{:S(2)}, u32[]{:S(2)}) %collective-permute-start.5) | collective-permute-done | bytes 524320 | tf_op jit(solution)/shard_map/ppermute | solution.py:28
  54.8 1.6 %collective-permute-done.6.refs_0_ = bf16[144,2048]{1,0:T(8,128)(2,1)S(1)} collective-permute-done((bf16[144,2048]{1,0:T(8,128)(2,1)S(1)}, bf16[144,2048]{1,0:T(8,128)(2,1)S(1)}, u32[]{:S(2)}, u32[]{:S(2)}) %collective-permute-start.6) | collective-permute-done | bytes 589856 | tf_op jit(solution)/shard_map/ppermute | solution.py:28
  57.9 3.2 %collective-permute-start.10 = (bf16[144,1024]{1,0:T(8,128)(2,1)S(1)}, bf16[144,1024]{1,0:T(8,128)(2,1)S(1)}, u32[]{:S(2)}, u32[]{:S(2)}) collective-permute-start(bf16[144,1024]{1,0:T(8,128)(2,1)S(1)} %get-tuple-element.87), channel_id=1, source_target_pairs={{0,6},{1,7},{2,0},{3,1},{4,2},{5,3},{6,4},{7,5},{8,14},{9,15},{10,... | collective-permute-start | bytes 884744 | tf_op jit(solution)/shard_map/ppermute | solution.py:28
  61.2 4.7 %shard_map.126 = (bf16[4,288,1024]{2,1,0:T(8,128)(2,1)S(1)}, bf16[4,288,1024]{2,1,0:T(8,128)(2,1)S(1)}) custom-call(s32[4]{0:T(128)S(1)} %pad_add_fusion.place, bf16[512,2304]{1,0:T(8,128)(2,1)S(1)} %shard_map.121.a_both, bf16[256,1024]{1,0:T(8,128)(2,1)S(1)} %get-tuple-element.80.c_own.val, bf16[256,1024]{1,0:T(8,128)(2,1)S(1)} %collective-permute-done.5.c_far.val), custom_call_target="tpu_custom_call" | custom-call | flops 49999998976 | bytes 500000000 | tf_op jit(solution)/shard_map/pallas_call | solution.py:34
  66.0 1.9 %collective-permute-done.10.down = bf16[144,1024]{1,0:T(8,128)(2,1)S(1)} collective-permute-done((bf16[144,1024]{1,0:T(8,128)(2,1)S(1)}, bf16[144,1024]{1,0:T(8,128)(2,1)S(1)}, u32[]{:S(2)}, u32[]{:S(2)}) %collective-permute-start.10) | collective-permute-done | bytes 294944 | tf_op jit(solution)/shard_map/ppermute | solution.py:28
  69.5 3.2 %collective-permute-start.12 = (bf16[288,1024]{1,0:T(8,128)(2,1)S(1)}, bf16[288,1024]{1,0:T(8,128)(2,1)S(1)}, u32[]{:S(2)}, u32[]{:S(2)}) collective-permute-start(bf16[288,1024]{1,0:T(8,128)(2,1)S(1)} %get-tuple-element.93), channel_id=1, source_target_pairs={{0,6},{1,7},{2,0},{3,1},{4,2},{5,3},{6,4},{7,5},{8,14},{9,15},{10,... | collective-permute-start | bytes 1769480 | tf_op jit(solution)/shard_map/ppermute | solution.py:28
  72.8 6.5 %shard_map.128 = bf16[256,2304]{1,0:T(8,128)(2,1)S(1)} custom-call(s32[4]{0:T(128)S(1)} %pad_add_fusion.place, bf16[864,2048]{1,0:T(8,128)(2,1)S(1)} %shard_map.123.w013, bf16[288,2048]{1,0:T(8,128)(2,1)S(1)} %shard_map.124.w2, bf16[864,2048]{1,0:T(8,128)(2,1)S(1)} %collective-permute-done.8.v013, bf16[288,2048]{1,0:T(8,128)(2,1)S(1)} %collective-permute-done.14.v2, ...), custom_call_target="tpu_custom_call" | custom-call | flops 49999998976 | bytes 500000000 | tf_op jit(solution)/shard_map/pallas_call | solution.py:34
  79.2 1.7 %collective-permute-start.19 = (bf16[256,2304]{1,0:T(8,128)(2,1)S(1)}, bf16[256,2304]{1,0:T(8,128)(2,1)S(1)}, u32[]{:S(2)}, u32[]{:S(2)}) collective-permute-start(bf16[256,2304]{1,0:T(8,128)(2,1)S(1)} %shard_map.128), channel_id=1, source_target_pairs={{0,8},{1,9},{2,10},{3,11},{4,12},{5,13},{6,14},{7,15},{8,0},{9,1},... | collective-permute-start | bytes 3538952 | tf_op jit(solution)/shard_map/ppermute | solution.py:28
  82.0 2.9 %collective-permute-done.12.r2 = bf16[288,1024]{1,0:T(8,128)(2,1)S(1)} collective-permute-done((bf16[288,1024]{1,0:T(8,128)(2,1)S(1)}, bf16[288,1024]{1,0:T(8,128)(2,1)S(1)}, u32[]{:S(2)}, u32[]{:S(2)}) %collective-permute-start.12) | collective-permute-done | bytes 589856 | tf_op jit(solution)/shard_map/ppermute | solution.py:28
  84.9 1.9 %collective-permute-done.11.r1 = bf16[288,1024]{1,0:T(8,128)(2,1)S(1)} collective-permute-done((bf16[288,1024]{1,0:T(8,128)(2,1)S(1)}, bf16[288,1024]{1,0:T(8,128)(2,1)S(1)}, u32[]{:S(2)}, u32[]{:S(2)}) %collective-permute-start.11) | collective-permute-done | bytes 589856 | tf_op jit(solution)/shard_map/ppermute | solution.py:28
  86.9 1.9 %collective-permute-start.24 = (bf16[144,1024]{1,0:T(8,128)(2,1)S(1)}, bf16[144,1024]{1,0:T(8,128)(2,1)S(1)}, u32[]{:S(2)}, u32[]{:S(2)}) collective-permute-start(bf16[144,1024]{1,0:T(8,128)(2,1)S(1)} %get-tuple-element.112), channel_id=1, source_target_pairs={{0,6},{1,7},{2,0},{3,1},{4,2},{5,3},{6,4},{7,5},{8,14},{9,15},{10,... | collective-permute-start | bytes 884744 | tf_op jit(solution)/shard_map/ppermute | solution.py:28
  88.7 3.1 %shard_map.130 = (f32[288,256]{1,0:T(8,128)S(1)}, bf16[288,256]{1,0:T(8,128)(2,1)S(1)}, bf16[288,256]{1,0:T(8,128)(2,1)S(1)}, bf16[288,256]{1,0:T(8,128)(2,1)S(1...) custom-call(s32[4]{0:T(128)S(1)} %pad_add_fusion.place, f32[288,1024]{1,0:T(8,128)S(1)} %get-tuple-element.74.w, ...), custom_call_target="tpu_custom_call" | custom-call | flops 49999998976 | bytes 500000000 | tf_op jit(solution)/shard_map/pallas_call | solution.py:34
  91.9 2.0 %collective-permute-start.15 = (bf16[288,256]{1,0:T(8,128)(2,1)S(1)}, bf16[288,256]{1,0:T(8,128)(2,1)S(1)}, u32[]{:S(2)}, u32[]{:S(2)}) collective-permute-start(bf16[288,256]{1,0:T(8,128)(2,1)S(1)} %get-tuple-element.102), channel_id=1, source_target_pairs={{0,16},{1,17},{2,18},{3,19},{4,20},{5,21},{6,22},{7,23},{8,24},{9,... | collective-permute-start | bytes 442376 | tf_op jit(solution)/shard_map/ppermute | solution.py:28
  93.9 3.6 %collective-permute-start.16 = (bf16[288,256]{1,0:T(8,128)(2,1)S(1)}, bf16[288,256]{1,0:T(8,128)(2,1)S(1)}, u32[]{:S(2)}, u32[]{:S(2)}) collective-permute-start(bf16[288,256]{1,0:T(8,128)(2,1)S(1)} %get-tuple-element.103), channel_id=1, source_target_pairs={{0,32},{1,33},{2,34},{3,35},{4,36},{5,37},{6,38},{7,39},{8,40},{9,... | collective-permute-start | bytes 442376 | tf_op jit(solution)/shard_map/ppermute | solution.py:28
  100.7 2.0 %collective-permute-start.26 = (bf16[288,1024]{1,0:T(8,128)(2,1)S(1)}, bf16[288,1024]{1,0:T(8,128)(2,1)S(1)}, u32[]{:S(2)}, u32[]{:S(2)}) collective-permute-start(bf16[288,1024]{1,0:T(8,128)(2,1)S(1)} %get-tuple-element.115), channel_id=1, source_target_pairs={{0,6},{1,7},{2,0},{3,1},{4,2},{5,3},{6,4},{7,5},{8,14},{9,15},{10,... | collective-permute-start | bytes 1769480 | tf_op jit(solution)/shard_map/ppermute | solution.py:28
  103.5 6.1 %shard_map.131.near = bf16[256,4608]{1,0:T(8,128)(2,1)} custom-call(s32[4]{0:T(128)S(1)} %pad_add_fusion.place, bf16[864,2048]{1,0:T(8,128)(2,1)S(1)} %shard_map.123.w013, bf16[288,2048]{1,0:T(8,128)(2,1)S(1)} %shard_map.124.w2, bf16[864,2048]{1,0:T(8,128)(2,1)S(1)} %collective-permute-done.8.v013, bf16[288,2048]{1,0:T(8,128)(2,1)S(1)} %collective-permute-done.14.v2, ...), custom_call_target="tpu_custom_call" | custom-call | tf_op jit(solution)/shard_map/pallas_call | solution.py:34
  109.6 1.6 %shard_map.132 = bf16[256,4608]{1,0:T(8,128)(2,1)} custom-call(s32[4]{0:T(128)S(1)} %pad_add_fusion.place, bf16[256,2304]{1,0:T(8,128)(2,1)S(1)} %collective-permute-done.19.far, bf16[256,4608]{1,0:T(8,128)(2,1)} %shard_map.131.near), custom_call_target="tpu_custom_call", output_to_operand_aliasing={{}: (2, {})} | custom-call | tf_op jit(solution)/shard_map/pallas_call | solution.py:34
  111.3 1.8 %collective-permute-start.22 = (bf16[288,256]{1,0:T(8,128)(2,1)S(1)}, bf16[288,256]{1,0:T(8,128)(2,1)S(1)}, u32[]{:S(2)}, u32[]{:S(2)}) collective-permute-start(bf16[288,256]{1,0:T(8,128)(2,1)S(1)} %multiply_convert_fusion.m0), channel_id=1, source_target_pairs={{0,16},{1,17},{2,18},{3,19},{4,20},{5,21},{6,22},{7,23},{8,24},{9,... | collective-permute-start | bytes 442376 | tf_op jit(solution)/shard_map/ppermute | solution.py:28
  113.1 3.6 %collective-permute-start.21 = (bf16[288,256]{1,0:T(8,128)(2,1)S(1)}, bf16[288,256]{1,0:T(8,128)(2,1)S(1)}, u32[]{:S(2)}, u32[]{:S(2)}) collective-permute-start(bf16[288,256]{1,0:T(8,128)(2,1)S(1)} %multiply_convert_fusion.m0), channel_id=1, source_target_pairs={{0,32},{1,33},{2,34},{3,35},{4,36},{5,37},{6,38},{7,39},{8,40},{9,... | collective-permute-start | bytes 442376 | tf_op jit(solution)/shard_map/ppermute | solution.py:28
  117.7 3.8 %shard_map.134 = (f32[288,2,1024]{2,1,0:T(2,128)}, f32[288,2,1024]{2,1,0:T(2,128)}, f32[288,1024]{1,0:T(8,128)S(1)}) custom-call(s32[4]{0:T(128)S(1)} %pad_add_fusion.place, f32[288,1024]{1,0:T(8,128)S(1)} %get-tuple-element.107.m_key, f32[288,1024]{1,0:T(8,128)S(1)} %get-tuple-element.108.v_key, f32[288,1024]{1,0:T(8,128)S(1)} %get-tuple-element.109.w, ...), custom_call_target="tpu_custom_call" | custom-call | tf_op jit(solution)/shard_map/pallas_call | solution.py:34
  121.8 3.1 %shard_map.135 = (f32[288,2,1024]{2,1,0:T(2,128)}, f32[288,1024]{1,0:T(8,128)}, f32[288,1024]{1,0:T(8,128)}) custom-call(s32[4]{0:T(128)S(1)} %pad_add_fusion.place, bf16[288,256]{1,0:T(8,128)(2,1)S(1)} %multiply_convert_fusion.m0, bf16[288,256]{1,0:T(8,128)(2,1)S(1)} %collective-permute-done.20.m1, bf16[288,256]{1,0:T(8,128)(2,1)S(1)} %collective-permute-done.21.m2, ...), custom_call_target="tpu_custom_call" | custom-call | tf_op jit(solution)/shard_map/pallas_call | solution.py:34
  (67 shorter events, 15.5 us)
Async XLA Ops:
  3.0 30.4 %collective-permute-start = (bf16[256,2304]{1,0:T(8,128)(2,1)S(1)}, bf16[256,2304]{1,0:T(8,128)(2,1)S(1)}, u32[]{:S(2)}, u32[]{:S(2)}) collective-permute-start(bf16[256,2304]{1,0:T(8,128)(2,1)S(1)} %shard_map.118), channel_id=1, source_target_pairs={{0,8},{1,9},{2,10},{3,11},{4,12},{5,13},{6,14},{7,15},{8,0},{9,1},... | collective-permute-start | bytes 3538952 | tf_op jit(solution)/shard_map/ppermute | solution.py:28
  6.4 6.2 %copy-start.9 = (bf16[1,256,2,1024]{3,2,1,0:T(2,128)(2,1)S(1)}, bf16[1,256,2,1024]{3,2,1,0:T(2,128)(2,1)}, u32[]{:S(2)}) copy-start(bf16[1,256,2,1024]{3,2,1,0:T(2,128)(2,1)} %param.8) | copy-start | bytes 3145732
  6.4 7.6 %copy-start.2 = (f32[1,288,2,1024]{3,2,1,0:T(2,128)S(1)}, f32[1,288,2,1024]{3,2,1,0:T(2,128)}, u32[]{:S(2)}) copy-start(f32[1,288,2,1024]{3,2,1,0:T(2,128)} %param.11) | copy-start | bytes 7077892
  9.3 28.7 %collective-permute-start.2 = (bf16[288,2048]{1,0:T(8,128)(2,1)S(1)}, bf16[288,2048]{1,0:T(8,128)(2,1)S(1)}, u32[]{:S(2)}, u32[]{:S(2)}) collective-permute-start(bf16[288,2048]{1,0:T(8,128)(2,1)S(1)} %shard_map.119.refs_0_), channel_id=1, source_target_pairs={{0,2},{1,3},{2,4},{3,5},{4,6},{5,7},{6,0},{7,1},{8,10},{9,11},{10,... | collective-permute-start | bytes 3538952 | tf_op jit(solution)/shard_map/ppermute | solution.py:28
  10.9 27.1 %collective-permute-start.1 = (bf16[288,2048]{1,0:T(8,128)(2,1)S(1)}, bf16[288,2048]{1,0:T(8,128)(2,1)S(1)}, u32[]{:S(2)}, u32[]{:S(2)}) collective-permute-start(bf16[288,2048]{1,0:T(8,128)(2,1)S(1)} %shard_map.119.refs_0_), channel_id=1, source_target_pairs={{0,6},{1,7},{2,0},{3,1},{4,2},{5,3},{6,4},{7,5},{8,14},{9,15},{10,... | collective-permute-start | bytes 3538952 | tf_op jit(solution)/shard_map/ppermute | solution.py:28
  13.0 31.7 %copy-start.5 = (bf16[256,1024]{1,0:T(8,128)(2,1)}, bf16[256,1024]{1,0:T(8,128)(2,1)S(1)}, u32[]{:S(2)}) copy-start(bf16[256,1024]{1,0:T(8,128)(2,1)S(1)} %get-tuple-element.125.c_own.key) | copy-start | bytes 1572868
  13.0 31.7 %collective-permute-start.3 = (bf16[256,1024]{1,0:T(8,128)(2,1)S(1)}, bf16[256,1024]{1,0:T(8,128)(2,1)S(1)}, u32[]{:S(2)}, u32[]{:S(2)}) collective-permute-start(bf16[256,1024]{1,0:T(8,128)(2,1)S(1)} %get-tuple-element.125.c_own.key), channel_id=1, source_target_pairs={{0,8},{1,9},{2,10},{3,11},{4,12},{5,13},{6,14},{7,15},{8,0},{9,1},... | collective-permute-start | bytes 1572872 | tf_op jit(solution)/shard_map/ppermute | solution.py:28
  14.5 19.0 %copy-start.4 = (bf16[1,256,4608]{2,1,0:T(8,128)(2,1)S(1)}, bf16[1,256,4608]{2,1,0:T(8,128)(2,1)}, u32[]{:S(2)}) copy-start(bf16[1,256,4608]{2,1,0:T(8,128)(2,1)} %param.7) | copy-start | bytes 7077892
  16.3 38.5 %collective-permute-start.5 = (bf16[256,1024]{1,0:T(8,128)(2,1)S(1)}, bf16[256,1024]{1,0:T(8,128)(2,1)S(1)}, u32[]{:S(2)}, u32[]{:S(2)}) collective-permute-start(bf16[256,1024]{1,0:T(8,128)(2,1)S(1)} %get-tuple-element.80.c_own.val), channel_id=1, source_target_pairs={{0,8},{1,9},{2,10},{3,11},{4,12},{5,13},{6,14},{7,15},{8,0},{9,1},... | collective-permute-start | bytes 1572872 | tf_op jit(solution)/shard_map/ppermute | solution.py:28
  38.9 15.9 %collective-permute-start.7 = (bf16[144,2048]{1,0:T(8,128)(2,1)S(1)}, bf16[144,2048]{1,0:T(8,128)(2,1)S(1)}, u32[]{:S(2)}, u32[]{:S(2)}) collective-permute-start(bf16[144,2048]{1,0:T(8,128)(2,1)S(1)} %slice.15), channel_id=1, source_target_pairs={{0,6},{1,7},{2,0},{3,1},{4,2},{5,3},{6,4},{7,5},{8,14},{9,15},{10,... | collective-permute-start | bytes 1769480 | tf_op jit(solution)/shard_map/ppermute | solution.py:28
  41.9 14.5 %collective-permute-start.6 = (bf16[144,2048]{1,0:T(8,128)(2,1)S(1)}, bf16[144,2048]{1,0:T(8,128)(2,1)S(1)}, u32[]{:S(2)}, u32[]{:S(2)}) collective-permute-start(bf16[144,2048]{1,0:T(8,128)(2,1)S(1)} %slice.14), channel_id=1, source_target_pairs={{0,2},{1,3},{2,4},{3,5},{4,6},{5,7},{6,0},{7,1},{8,10},{9,11},{10,... | collective-permute-start | bytes 1769480 | tf_op jit(solution)/shard_map/ppermute | solution.py:28
  41.9 14.5 %collective-permute-start.8 = (bf16[864,2048]{1,0:T(8,128)(2,1)S(1)}, bf16[864,2048]{1,0:T(8,128)(2,1)S(1)}, u32[]{:S(2)}, u32[]{:S(2)}) collective-permute-start(bf16[864,2048]{1,0:T(8,128)(2,1)S(1)} %shard_map.123.w013), channel_id=1, source_target_pairs={{0,1},{1,0},{2,3},{3,2},{4,5},{5,4},{6,7},{7,6},{8,9},{9,8},{10,11... | collective-permute-start | bytes 10616840 | tf_op jit(solution)/shard_map/ppermute | solution.py:28
  49.4 7.8 %collective-permute-start.4 = (bf16[4,288,1024]{2,1,0:T(8,128)(2,1)S(1)}, bf16[4,288,1024]{2,1,0:T(8,128)(2,1)S(1)}, u32[]{:S(2)}, u32[]{:S(2)}) collective-permute-start(bf16[4,288,1024]{2,1,0:T(8,128)(2,1)S(1)} %get-tuple-element.79), channel_id=1, source_target_pairs={{0,1},{1,0},{2,3},{3,2},{4,5},{5,4},{6,7},{7,6},{8,9},{9,8},{10,11... | collective-permute-start | bytes 7077896 | tf_op jit(solution)/shard_map/ppermute | solution.py:28
  57.1 15.7 %collective-permute-start.14 = (bf16[288,2048]{1,0:T(8,128)(2,1)S(1)}, bf16[288,2048]{1,0:T(8,128)(2,1)S(1)}, u32[]{:S(2)}, u32[]{:S(2)}) collective-permute-start(bf16[288,2048]{1,0:T(8,128)(2,1)S(1)} %shard_map.124.w2), channel_id=1, source_target_pairs={{0,1},{1,0},{2,3},{3,2},{4,5},{5,4},{6,7},{7,6},{8,9},{9,8},{10,11... | collective-permute-start | bytes 3538952 | tf_op jit(solution)/shard_map/ppermute | solution.py:28
  57.9 10.7 %collective-permute-start.9 = (bf16[144,1024]{1,0:T(8,128)(2,1)S(1)}, bf16[144,1024]{1,0:T(8,128)(2,1)S(1)}, u32[]{:S(2)}, u32[]{:S(2)}) collective-permute-start(bf16[144,1024]{1,0:T(8,128)(2,1)S(1)} %get-tuple-element.86), channel_id=1, source_target_pairs={{0,2},{1,3},{2,4},{3,5},{4,6},{5,7},{6,0},{7,1},{8,10},{9,11},{10,... | collective-permute-start | bytes 884744 | tf_op jit(solution)/shard_map/ppermute | solution.py:28
  57.9 9.9 %collective-permute-start.10 = (bf16[144,1024]{1,0:T(8,128)(2,1)S(1)}, bf16[144,1024]{1,0:T(8,128)(2,1)S(1)}, u32[]{:S(2)}, u32[]{:S(2)}) collective-permute-start(bf16[144,1024]{1,0:T(8,128)(2,1)S(1)} %get-tuple-element.87), channel_id=1, source_target_pairs={{0,6},{1,7},{2,0},{3,1},{4,2},{5,3},{6,4},{7,5},{8,14},{9,15},{10,... | collective-permute-start | bytes 884744 | tf_op jit(solution)/shard_map/ppermute | solution.py:28
  65.9 15.1 %collective-permute-start.13 = (bf16[4,288,1024]{2,1,0:T(8,128)(2,1)S(1)}, bf16[4,288,1024]{2,1,0:T(8,128)(2,1)S(1)}, u32[]{:S(2)}, u32[]{:S(2)}) collective-permute-start(bf16[4,288,1024]{2,1,0:T(8,128)(2,1)S(1)} %get-tuple-element.90), channel_id=1, source_target_pairs={{0,1},{1,0},{2,3},{3,2},{4,5},{5,4},{6,7},{7,6},{8,9},{9,8},{10,11... | collective-permute-start | bytes 7077896 | tf_op jit(solution)/shard_map/ppermute | solution.py:28
  69.4 17.4 %collective-permute-start.11 = (bf16[288,1024]{1,0:T(8,128)(2,1)S(1)}, bf16[288,1024]{1,0:T(8,128)(2,1)S(1)}, u32[]{:S(2)}, u32[]{:S(2)}) collective-permute-start(bf16[288,1024]{1,0:T(8,128)(2,1)S(1)} %get-tuple-element.92), channel_id=1, source_target_pairs={{0,2},{1,3},{2,4},{3,5},{4,6},{5,7},{6,0},{7,1},{8,10},{9,11},{10,... | collective-permute-start | bytes 1769480 | tf_op jit(solution)/shard_map/ppermute | solution.py:28
  69.5 15.4 %collective-permute-start.12 = (bf16[288,1024]{1,0:T(8,128)(2,1)S(1)}, bf16[288,1024]{1,0:T(8,128)(2,1)S(1)}, u32[]{:S(2)}, u32[]{:S(2)}) collective-permute-start(bf16[288,1024]{1,0:T(8,128)(2,1)S(1)} %get-tuple-element.93), channel_id=1, source_target_pairs={{0,6},{1,7},{2,0},{3,1},{4,2},{5,3},{6,4},{7,5},{8,14},{9,15},{10,... | collective-permute-start | bytes 1769480 | tf_op jit(solution)/shard_map/ppermute | solution.py:28
  79.2 30.4 %collective-permute-start.19 = (bf16[256,2304]{1,0:T(8,128)(2,1)S(1)}, bf16[256,2304]{1,0:T(8,128)(2,1)S(1)}, u32[]{:S(2)}, u32[]{:S(2)}) collective-permute-start(bf16[256,2304]{1,0:T(8,128)(2,1)S(1)} %shard_map.128), channel_id=1, source_target_pairs={{0,8},{1,9},{2,10},{3,11},{4,12},{5,13},{6,14},{7,15},{8,0},{9,1},... | collective-permute-start | bytes 3538952 | tf_op jit(solution)/shard_map/ppermute | solution.py:28
  81.7 16.8 %collective-permute-start.23 = (bf16[144,1024]{1,0:T(8,128)(2,1)S(1)}, bf16[144,1024]{1,0:T(8,128)(2,1)S(1)}, u32[]{:S(2)}, u32[]{:S(2)}) collective-permute-start(bf16[144,1024]{1,0:T(8,128)(2,1)S(1)} %get-tuple-element.98), channel_id=1, source_target_pairs={{0,2},{1,3},{2,4},{3,5},{4,6},{5,7},{6,0},{7,1},{8,10},{9,11},{10,... | collective-permute-start | bytes 884744 | tf_op jit(solution)/shard_map/ppermute | solution.py:28
  86.9 10.6 %collective-permute-start.24 = (bf16[144,1024]{1,0:T(8,128)(2,1)S(1)}, bf16[144,1024]{1,0:T(8,128)(2,1)S(1)}, u32[]{:S(2)}, u32[]{:S(2)}) collective-permute-start(bf16[144,1024]{1,0:T(8,128)(2,1)S(1)} %get-tuple-element.112), channel_id=1, source_target_pairs={{0,6},{1,7},{2,0},{3,1},{4,2},{5,3},{6,4},{7,5},{8,14},{9,15},{10,... | collective-permute-start | bytes 884744 | tf_op jit(solution)/shard_map/ppermute | solution.py:28
  91.9 8.8 %collective-permute-start.15 = (bf16[288,256]{1,0:T(8,128)(2,1)S(1)}, bf16[288,256]{1,0:T(8,128)(2,1)S(1)}, u32[]{:S(2)}, u32[]{:S(2)}) collective-permute-start(bf16[288,256]{1,0:T(8,128)(2,1)S(1)} %get-tuple-element.102), channel_id=1, source_target_pairs={{0,16},{1,17},{2,18},{3,19},{4,20},{5,21},{6,22},{7,23},{8,24},{9,... | collective-permute-start | bytes 442376 | tf_op jit(solution)/shard_map/ppermute | solution.py:28
  93.9 8.8 %collective-permute-start.16 = (bf16[288,256]{1,0:T(8,128)(2,1)S(1)}, bf16[288,256]{1,0:T(8,128)(2,1)S(1)}, u32[]{:S(2)}, u32[]{:S(2)}) collective-permute-start(bf16[288,256]{1,0:T(8,128)(2,1)S(1)} %get-tuple-element.103), channel_id=1, source_target_pairs={{0,32},{1,33},{2,34},{3,35},{4,36},{5,37},{6,38},{7,39},{8,40},{9,... | collective-permute-start | bytes 442376 | tf_op jit(solution)/shard_map/ppermute | solution.py:28
  97.4 5.2 %collective-permute-start.17 = (bf16[288,256]{1,0:T(8,128)(2,1)S(1)}, bf16[288,256]{1,0:T(8,128)(2,1)S(1)}, u32[]{:S(2)}, u32[]{:S(2)}) collective-permute-start(bf16[288,256]{1,0:T(8,128)(2,1)S(1)} %get-tuple-element.104), channel_id=1, source_target_pairs={{0,48},{1,49},{2,50},{3,51},{4,52},{5,53},{6,54},{7,55},{8,56},{9,... | collective-permute-start | bytes 442376 | tf_op jit(solution)/shard_map/ppermute | solution.py:28
  99.4 4.2 %copy-start.6 = (bf16[256,1024]{1,0:T(8,128)(2,1)S(1)}, bf16[256,1024]{1,0:T(8,128)(2,1)}, u32[]{:S(2)}) copy-start(bf16[256,1024]{1,0:T(8,128)(2,1)} %copy-done.5) | copy-start | bytes 1572868
  99.4 18.3 %collective-permute-start.25 = (bf16[288,1024]{1,0:T(8,128)(2,1)S(1)}, bf16[288,1024]{1,0:T(8,128)(2,1)S(1)}, u32[]{:S(2)}, u32[]{:S(2)}) collective-permute-start(bf16[288,1024]{1,0:T(8,128)(2,1)S(1)} %get-tuple-element.114), channel_id=1, source_target_pairs={{0,2},{1,3},{2,4},{3,5},{4,6},{5,7},{6,0},{7,1},{8,10},{9,11},{10,... | collective-permute-start | bytes 1769480 | tf_op jit(solution)/shard_map/ppermute | solution.py:28
  100.7 17.0 %collective-permute-start.26 = (bf16[288,1024]{1,0:T(8,128)(2,1)S(1)}, bf16[288,1024]{1,0:T(8,128)(2,1)S(1)}, u32[]{:S(2)}, u32[]{:S(2)}) collective-permute-start(bf16[288,1024]{1,0:T(8,128)(2,1)S(1)} %get-tuple-element.115), channel_id=1, source_target_pairs={{0,6},{1,7},{2,0},{3,1},{4,2},{5,3},{6,4},{7,5},{8,14},{9,15},{10,... | collective-permute-start | bytes 1769480 | tf_op jit(solution)/shard_map/ppermute | solution.py:28
  102.8 8.5 %collective-permute-start.18 = (bf16[288,256]{1,0:T(8,128)(2,1)S(1)}, bf16[288,256]{1,0:T(8,128)(2,1)S(1)}, u32[]{:S(2)}, u32[]{:S(2)}) collective-permute-start(bf16[288,256]{1,0:T(8,128)(2,1)S(1)} %get-tuple-element.122), channel_id=1, source_target_pairs={{0,64},{1,65},{2,66},{3,67},{4,68},{5,69},{6,70},{7,71},{8,72},{9,... | collective-permute-start | bytes 442376 | tf_op jit(solution)/shard_map/ppermute | solution.py:28
  111.3 10.2 %collective-permute-start.22 = (bf16[288,256]{1,0:T(8,128)(2,1)S(1)}, bf16[288,256]{1,0:T(8,128)(2,1)S(1)}, u32[]{:S(2)}, u32[]{:S(2)}) collective-permute-start(bf16[288,256]{1,0:T(8,128)(2,1)S(1)} %multiply_convert_fusion.m0), channel_id=1, source_target_pairs={{0,16},{1,17},{2,18},{3,19},{4,20},{5,21},{6,22},{7,23},{8,24},{9,... | collective-permute-start | bytes 442376 | tf_op jit(solution)/shard_map/ppermute | solution.py:28
  113.1 8.4 %collective-permute-start.21 = (bf16[288,256]{1,0:T(8,128)(2,1)S(1)}, bf16[288,256]{1,0:T(8,128)(2,1)S(1)}, u32[]{:S(2)}, u32[]{:S(2)}) collective-permute-start(bf16[288,256]{1,0:T(8,128)(2,1)S(1)} %multiply_convert_fusion.m0), channel_id=1, source_target_pairs={{0,32},{1,33},{2,34},{3,35},{4,36},{5,37},{6,38},{7,39},{8,40},{9,... | collective-permute-start | bytes 442376 | tf_op jit(solution)/shard_map/ppermute | solution.py:28
  116.7 5.1 %collective-permute-start.20 = (bf16[288,256]{1,0:T(8,128)(2,1)S(1)}, bf16[288,256]{1,0:T(8,128)(2,1)S(1)}, u32[]{:S(2)}, u32[]{:S(2)}) collective-permute-start(bf16[288,256]{1,0:T(8,128)(2,1)S(1)} %multiply_convert_fusion.m0), channel_id=1, source_target_pairs={{0,48},{1,49},{2,50},{3,51},{4,52},{5,53},{6,54},{7,55},{8,56},{9,... | collective-permute-start | bytes 442376 | tf_op jit(solution)/shard_map/ppermute | solution.py:28
  (5 other events, 15.8 us)

commit v4 on v3

--- a/solution.py
+++ b/solution.py
@@ -1,3 +1,5 @@
+import functools
+
 import jax
 import jax.numpy as jnp
 import numpy as np
@@ -195,44 +197,38 @@
     out[...] = far[...]
 
 
-def input_kernel(place, w013, w2, v013, v2, key, val, out, w_s, o_s, sem, out_sem):
+def input_kernel(f, place, w013, w2, v013, v2, tokens, *rest):
+    out, w_s, sem = (rest[0], rest[1], rest[2]) if f == 0 else (rest[1], rest[2], rest[4])
     h, c, x = place[0], place[1], place[2]
-    rows, feat = v2.shape[0], key.shape[1]
-    wide = o_s.shape[1]
-    pieces = []
+    wide, feat = w_s.shape
+    rows = wide // 8
+    base = h * wide if out.shape[1] > wide else 0
+    copies = []
     for core, triple, last in ((c, w013, w2), (1 - c, v013, v2)):
-        for n, step in enumerate((0, 1, 3)):
-            pieces.append((core, step, triple, n * rows))
-        pieces.append((core, 2, last, 0))
-    copies = [[], []]
-    for f in range(2):
-        for core, step, piece, first in pieces:
+        for step, piece, first in ((0, triple, 0), (1, triple, 1), (3, triple, 2), (2, last, 0)):
             start = pl.multiple_of((2 * lax.rem(x + step, 4) + core) * rows, 16)
-            copies[f].append(
+            copies.append(
                 pltpu.make_async_copy(
-                    piece.at[pl.ds(first, rows), pl.ds(f * feat, feat)],
-                    w_s.at[f, pl.ds(start, rows)],
-                    sem.at[8 * f + len(copies[f])],
+                    piece.at[pl.ds(first * rows, rows), pl.ds(f * feat, feat)],
+                    w_s.at[pl.ds(start, rows)],
+                    sem.at[len(copies)],
                 )
             )
-    for copy in copies[0] + copies[1]:
+    for copy in copies:
         copy.start()
+    for copy in copies:
+        copy.wait()
     tile = 384
-    tiles = [slice(j * tile, (j + 1) * tile) for j in range(wide // tile)]
     dims = (((1,), (1,)), ((), ()))
-    for copy in copies[0]:
-        copy.wait()
-    accs = [
-        lax.dot_general(key[...], w_s[0, cols, :], dims, preferred_element_type=F32)
-        for cols in tiles
-    ]
-    for copy in copies[1]:
-        copy.wait()
-    base = h * wide if out.shape[1] > wide else 0
     sends = []
-    for j, cols in enumerate(tiles):
-        acc = lax.dot_general(val[...], w_s[1, cols, :], dims, preferred_element_type=F32)
-        o_s[:, cols] = (accs[j] + acc).astype(BF16)
+    for j in range(wide // tile):
+        cols = slice(j * tile, (j + 1) * tile)
+        acc = lax.dot_general(tokens[...], w_s[cols, :], dims, preferred_element_type=F32)
+        if f == 0:
+            out[:, cols] = acc
+            continue
+        o_s, out_sem = rest[3], rest[5]
+        o_s[:, cols] = (rest[0][:, cols] + acc).astype(BF16)
         sends.append(
             pltpu.make_async_copy(
                 o_s.at[:, pl.ds(j * tile, tile)],
@@ -389,34 +385,48 @@
     up0r, down0r = shift(up0, x=1), shift(down0, x=-1)
     mine1, other1 = partial(a_both, val, after(val_far, up0))
     got1 = shift(other1, core=1)
-    to_up0, to_down0 = second_hop(mine0, got0, up0r, after(down0r, other1))
-    key_parts = (shift(to_up0, x=1), shift(to_down0, x=-1))
-
-    def input_part(first, key, val, columns, weight=0):
+    weights_s = pltpu.VMEM((width // 2, feat), BF16)
+
+    def input_key(first, tokens):
         return call(
-            input_kernel,
+            functools.partial(input_kernel, 0),
+            shape((tok, width // 2), F32),
+            place,
+            (first, w2, v013, v2, tokens),
+            [ANY] * 4 + [whole(tok, feat)],
+            whole(tok, width // 2),
+            [weights_s, pltpu.SemaphoreType.DMA((8,))],
+            vmem=16,
+        )
+
+    def input_val(first, tokens, key_part, columns, weight=0):
+        return call(
+            functools.partial(input_kernel, 1),
             shape((tok, columns)),
             place,
-            (first, w2, v013, v2, key, val),
-            [ANY] * 4 + [whole(tok, feat)] * 2,
+            (first, w2, v013, v2, tokens, key_part),
+            [ANY] * 4 + [whole(tok, feat), whole(tok, width // 2)],
             ANY,
             [
-                pltpu.VMEM((2, width // 2, feat), BF16),
+                weights_s,
                 pltpu.VMEM((tok, width // 2), BF16),
-                pltpu.SemaphoreType.DMA((16,)),
+                pltpu.SemaphoreType.DMA((8,)),
                 pltpu.SemaphoreType.DMA((6,)),
             ],
-            flops=2 * tok * width * feat,
-            moved=12 * 2**20,
             weight=weight,
-            vmem=20,
-        )
-
-    out_far = input_part(after(w013, to_up0), key_far, val_far, width // 2, WEIGHT)
+            vmem=16,
+        )
+
+    far_key = input_key(after(w013, other1), key_far)
+    to_up0, to_down0 = second_hop(mine0, got0, up0r, after(down0r, far_key))
+    key_parts = (shift(to_up0, x=1), shift(to_down0, x=-1))
+
+    out_far = input_val(after(w013, to_up0), val_far, far_key, width // 2, WEIGHT)
     far = shift(out_far, yhi=1)
     up1, down1 = first_hop(mine1, after(got1, out_far))
     up1r, down1r = shift(up1, x=1), shift(down1, x=-1)
-    key_parts = after(key_parts, up1)
+    near_key = input_key(after(w013, up1), key)
+    key_parts = after(key_parts, near_key)
 
     half_own = pl.BlockSpec((1, hr, feat), lambda i, place: (place[2], i, 0))
     qc = feat // 4
@@ -441,24 +451,23 @@
     total = own
     for part in parts:
         total = total + part.astype(F32)
-    near = input_part(after(w013, total), key, val, width)
+    near = input_val(after(w013, total), val, near_key, width)
+    total = lax.reduce_precision(total, 8, 7)
+    total = total + after(shift(total.astype(BF16), ylo=1), near).astype(F32)
+    mean = (total / 8).astype(BF16)
+    means = (mean, shift(mean, z=-1), shift(mean, z=2), shift(mean, z=1))
     input_grad = call(
         far_columns_kernel,
         shape((tok, width)),
         place,
-        (far, near),
+        (after(far, mean), near),
         [pl.BlockSpec((tok // 2, width // 2), lambda i, place: (i, 0)), ANY],
         pl.BlockSpec((tok // 2, width // 2), lambda i, place: (i, 1 - place[0])),
         grid=(2,),
         moved=2 * tok * width,
         alias={2: 0},
     )
-
-    total = lax.reduce_precision(total, 8, 7)
-    total = total + after(shift(total.astype(BF16), ylo=1), input_grad).astype(F32)
-    mean = (total / 8).astype(BF16)
-    means = (mean, shift(mean, z=-1), shift(mean, z=2), shift(mean, z=1))
-    sums1 = (mine1, got1, *val_parts)
+    sums1 = (after(mine1, input_grad), got1, *val_parts)
     first_out, second_out, inner = call(
         moments_kernel,
         [shape((rows, 2, feat), F32)] * 2 + [shape((rows, feat), F32)],

time: 125 us -> 124 us (level)
  waiting for transfers between devices: 37.4 us -> 31.4 us
  starting transfers between devices: 39.6 us -> 43.3 us
    ppermute x27, waiting for transfers between devices: 37.4 us -> 31.4 us  [shift(): return lax.ppermute(value, AXES, pairs)]
    ppermute x27, starting transfers between devices: 39.6 us -> 43.3 us  [shift(): return lax.ppermute(value, AXES, pairs)]
    pallas_call x18 -> x20, Pallas kernels: 44.2 us -> 45.3 us  [call(): pl.pallas_call(kernel, out_shape=out_shape, grid_spec=pltpu.PrefetchScala...]
  transfers between devices with their start and end apart: 27 -> 27, of which waited for: 11 -> 8; matrix products, arithmetic and copies ran while one was open for 0% -> 0% of each run, Pallas kernels for 32% -> 34%
where the time goes in v4:
time: 124 us
  Pallas kernels  45.3 us (37%)
  starting transfers between devices  43.3 us (35%)
  waiting for transfers between devices  31.4 us (25%)
  local copies, waits for them, and re-layouts  2.6 us (2%)
    pallas_call x20, Pallas kernels, call(): pl.pallas_call(kernel, out_shape=out_shape, grid_spec=pltpu.PrefetchScala...  45.3 us
    ppermute x27, starting transfers between devices, shift(): return lax.ppermute(value, AXES, pairs)  43.3 us
    ppermute x27, waiting for transfers between devices, shift(): return lax.ppermute(value, AXES, pairs)  31.4 us
  transfers between devices with their start and end apart: 27, of which 8 were waited for; matrix products, arithmetic and copies ran while one was open for 0% of the time, Pallas kernels for 34%

profile of v4, /device:TPU:0, one launch (start us, length us, event | category | flops | bytes accessed | tf_op | source)
XLA Modules:
  0.0 123.8 jit_solution(5615959113120955775)
XLA Ops:
  0.7 1.7 %copy-done.3 = bf16[1,256,4608]{2,1,0:T(8,128)(2,1)S(1)} copy-done((bf16[1,256,4608]{2,1,0:T(8,128)(2,1)S(1)}, bf16[1,256,4608]{2,1,0:T(8,128)(2,1)}, u32[]{:S(2)}) %copy-start.3) | copy-done | bytes 2359320
  3.0 3.4 %collective-permute-start = (bf16[256,2304]{1,0:T(8,128)(2,1)S(1)}, bf16[256,2304]{1,0:T(8,128)(2,1)S(1)}, u32[]{:S(2)}, u32[]{:S(2)}) collective-permute-start(bf16[256,2304]{1,0:T(8,128)(2,1)S(1)} %shard_map.118), channel_id=1, source_target_pairs={{0,8},{1,9},{2,10},{3,11},{4,12},{5,13},{6,14},{7,15},{8,0},{9,1},... | collective-permute-start | bytes 3538952 | tf_op jit(solution)/shard_map/ppermute | solution.py:30
  6.4 2.9 %shard_map.119.refs_0_ = bf16[288,2048]{1,0:T(8,128)(2,1)S(1)} custom-call(s32[4]{0:T(128)S(1)} %pad_add_fusion.place, f32[288,2,1024]{2,1,0:T(2,128)S(1)} %bitcast.19), custom_call_target="tpu_custom_call" | custom-call | flops 49999998976 | bytes 500000000 | tf_op jit(solution)/shard_map/pallas_call | solution.py:36
  9.3 1.6 %collective-permute-start.2 = (bf16[288,2048]{1,0:T(8,128)(2,1)S(1)}, bf16[288,2048]{1,0:T(8,128)(2,1)S(1)}, u32[]{:S(2)}, u32[]{:S(2)}) collective-permute-start(bf16[288,2048]{1,0:T(8,128)(2,1)S(1)} %shard_map.119.refs_0_), channel_id=1, source_target_pairs={{0,2},{1,3},{2,4},{3,5},{4,6},{5,7},{6,0},{7,1},{8,10},{9,11},{10,... | collective-permute-start | bytes 3538952 | tf_op jit(solution)/shard_map/ppermute | solution.py:30
  10.9 1.7 %collective-permute-start.1 = (bf16[288,2048]{1,0:T(8,128)(2,1)S(1)}, bf16[288,2048]{1,0:T(8,128)(2,1)S(1)}, u32[]{:S(2)}, u32[]{:S(2)}) collective-permute-start(bf16[288,2048]{1,0:T(8,128)(2,1)S(1)} %shard_map.119.refs_0_), channel_id=1, source_target_pairs={{0,6},{1,7},{2,0},{3,1},{4,2},{5,3},{6,4},{7,5},{8,14},{9,15},{10,... | collective-permute-start | bytes 3538952 | tf_op jit(solution)/shard_map/ppermute | solution.py:30
  14.5 1.8 %shard_map.120 = (f32[288,1024]{1,0:T(8,128)S(1)}, f32[288,1024]{1,0:T(8,128)S(1)}, f32[288,1024]{1,0:T(8,128)S(1)}, f32[288,1024]{1,0:T(8,128)S(1)}, f32[288,1024]{1,0:T(8,128)S(1)}, /*index=5*/f32[288,1024]{1,0:T(8,128)S(1)}) custom-call(s32[4]{0:T(128)S(1)} %pad_add_fusion.place, f32[288,2,1024]{2,1,0:T(2,128)S(1)} %bitcast.20, ...), custom_call_target="tpu_custom_call" | custom-call | tf_op jit(solution)/shard_map/pallas_call | solution.py:36
  16.3 2.2 %collective-permute-start.5 = (bf16[256,1024]{1,0:T(8,128)(2,1)S(1)}, bf16[256,1024]{1,0:T(8,128)(2,1)S(1)}, u32[]{:S(2)}, u32[]{:S(2)}) collective-permute-start(bf16[256,1024]{1,0:T(8,128)(2,1)S(1)} %get-tuple-element.84.c_own.tokens), channel_id=1, source_target_pairs={{0,8},{1,9},{2,10},{3,11},{4,12},{5,13},{6,14},{7,15},{8,0},{9,1},... | collective-permute-start | bytes 1572872 | tf_op jit(solution)/shard_map/ppermute | solution.py:30
  18.5 14.9 %collective-permute-done.far = bf16[256,2304]{1,0:T(8,128)(2,1)S(1)} collective-permute-done((bf16[256,2304]{1,0:T(8,128)(2,1)S(1)}, bf16[256,2304]{1,0:T(8,128)(2,1)S(1)}, u32[]{:S(2)}, u32[]{:S(2)}) %collective-permute-start) | collective-permute-done | bytes 1179680 | tf_op jit(solution)/shard_map/ppermute | solution.py:30
  34.2 3.8 %collective-permute-done.2.refs_2_ = bf16[288,2048]{1,0:T(8,128)(2,1)S(1)} collective-permute-done((bf16[288,2048]{1,0:T(8,128)(2,1)S(1)}, bf16[288,2048]{1,0:T(8,128)(2,1)S(1)}, u32[]{:S(2)}, u32[]{:S(2)}) %collective-permute-start.2) | collective-permute-done | bytes 1179680 | tf_op jit(solution)/shard_map/ppermute | solution.py:30
  38.9 3.0 %collective-permute-start.7 = (bf16[144,2048]{1,0:T(8,128)(2,1)S(1)}, bf16[144,2048]{1,0:T(8,128)(2,1)S(1)}, u32[]{:S(2)}, u32[]{:S(2)}) collective-permute-start(bf16[144,2048]{1,0:T(8,128)(2,1)S(1)} %slice.15), channel_id=1, source_target_pairs={{0,6},{1,7},{2,0},{3,1},{4,2},{5,3},{6,4},{7,5},{8,14},{9,15},{10,... | collective-permute-start | bytes 1769480 | tf_op jit(solution)/shard_map/ppermute | solution.py:30
  41.9 2.8 %collective-permute-done.3.c_far.tokens = bf16[256,1024]{1,0:T(8,128)(2,1)S(1)} collective-permute-done((bf16[256,1024]{1,0:T(8,128)(2,1)S(1)}, bf16[256,1024]{1,0:T(8,128)(2,1)S(1)}, u32[]{:S(2)}, u32[]{:S(2)}) %collective-permute-start.3) | collective-permute-done | bytes 524320 | tf_op jit(solution)/shard_map/ppermute | solution.py:30
  44.7 4.7 %shard_map.122 = (bf16[4,288,1024]{2,1,0:T(8,128)(2,1)S(1)}, bf16[4,288,1024]{2,1,0:T(8,128)(2,1)S(1)}) custom-call(s32[4]{0:T(128)S(1)} %pad_add_fusion.place, bf16[512,2304]{1,0:T(8,128)(2,1)S(1)} %shard_map.121.a_both, bf16[256,1024]{1,0:T(8,128)(2,1)S(1)} %get-tuple-element.133.c_own.tokens, bf16[256,1024]{1,0:T(8,128)(2,1)S(1)} %collective-permute-done.3.c_far.tokens), custom_call_target="tpu_custom_call" | custom-call | flops 49999998976 | bytes 500000000 | tf_op jit(solution)/shard_map/pallas_call | solution.py:36
  49.5 5.3 %collective-permute-done.5.c_far.tokens = bf16[256,1024]{1,0:T(8,128)(2,1)S(1)} collective-permute-done((bf16[256,1024]{1,0:T(8,128)(2,1)S(1)}, bf16[256,1024]{1,0:T(8,128)(2,1)S(1)}, u32[]{:S(2)}, u32[]{:S(2)}) %collective-permute-start.5) | collective-permute-done | bytes 524320 | tf_op jit(solution)/shard_map/ppermute | solution.py:30
  54.8 1.6 %collective-permute-done.6.refs_0_ = bf16[144,2048]{1,0:T(8,128)(2,1)S(1)} collective-permute-done((bf16[144,2048]{1,0:T(8,128)(2,1)S(1)}, bf16[144,2048]{1,0:T(8,128)(2,1)S(1)}, u32[]{:S(2)}, u32[]{:S(2)}) %collective-permute-start.6) | collective-permute-done | bytes 589856 | tf_op jit(solution)/shard_map/ppermute | solution.py:30
  57.9 3.2 %collective-permute-start.10 = (bf16[144,1024]{1,0:T(8,128)(2,1)S(1)}, bf16[144,1024]{1,0:T(8,128)(2,1)S(1)}, u32[]{:S(2)}, u32[]{:S(2)}) collective-permute-start(bf16[144,1024]{1,0:T(8,128)(2,1)S(1)} %get-tuple-element.91), channel_id=1, source_target_pairs={{0,6},{1,7},{2,0},{3,1},{4,2},{5,3},{6,4},{7,5},{8,14},{9,15},{10,... | collective-permute-start | bytes 884744 | tf_op jit(solution)/shard_map/ppermute | solution.py:30
  61.2 4.7 %shard_map.126 = (bf16[4,288,1024]{2,1,0:T(8,128)(2,1)S(1)}, bf16[4,288,1024]{2,1,0:T(8,128)(2,1)S(1)}) custom-call(s32[4]{0:T(128)S(1)} %pad_add_fusion.place, bf16[512,2304]{1,0:T(8,128)(2,1)S(1)} %shard_map.121.a_both, bf16[256,1024]{1,0:T(8,128)(2,1)S(1)} %get-tuple-element.84.c_own.tokens, bf16[256,1024]{1,0:T(8,128)(2,1)S(1)} %collective-permute-done.5.c_far.tokens), custom_call_target="tpu_custom_call" | custom-call | flops 49999998976 | bytes 500000000 | tf_op jit(solution)/shard_map/pallas_call | solution.py:36
  66.0 2.9 %shard_map.127.rest_0_ = f32[256,2304]{1,0:T(8,128)S(1)} custom-call(s32[4]{0:T(128)S(1)} %pad_add_fusion.place, bf16[864,2048]{1,0:T(8,128)(2,1)S(1)} %shard_map.123.w013, bf16[288,2048]{1,0:T(8,128)(2,1)S(1)} %shard_map.124.w2, bf16[864,2048]{1,0:T(8,128)(2,1)S(1)} %collective-permute-done.8.v013, bf16[288,2048]{1,0:T(8,128)(2,1)S(1)} %collective-permute-done.11.v2, ...), custom_call_target="tpu_custom_call" | custom-call | tf_op jit(solution)/shard_map/pallas_call | solution.py:36
  69.9 3.2 %collective-permute-start.13 = (bf16[288,1024]{1,0:T(8,128)(2,1)S(1)}, bf16[288,1024]{1,0:T(8,128)(2,1)S(1)}, u32[]{:S(2)}, u32[]{:S(2)}) collective-permute-start(bf16[288,1024]{1,0:T(8,128)(2,1)S(1)} %get-tuple-element.99), channel_id=1, source_target_pairs={{0,6},{1,7},{2,0},{3,1},{4,2},{5,3},{6,4},{7,5},{8,14},{9,15},{10,... | collective-permute-start | bytes 1769480 | tf_op jit(solution)/shard_map/ppermute | solution.py:30
  73.1 4.1 %shard_map.129 = bf16[256,2304]{1,0:T(8,128)(2,1)S(1)} custom-call(s32[4]{0:T(128)S(1)} %pad_add_fusion.place, bf16[864,2048]{1,0:T(8,128)(2,1)S(1)} %shard_map.123.w013, bf16[288,2048]{1,0:T(8,128)(2,1)S(1)} %shard_map.124.w2, bf16[864,2048]{1,0:T(8,128)(2,1)S(1)} %collective-permute-done.8.v013, bf16[288,2048]{1,0:T(8,128)(2,1)S(1)} %collective-permute-done.11.v2, ...), custom_call_target="tpu_custom_call" | custom-call | flops 49999998976 | bytes 500000000 | tf_op jit(solution)/shard_map/pallas_call | solution.py:36
  77.2 1.7 %collective-permute-start.22 = (bf16[256,2304]{1,0:T(8,128)(2,1)S(1)}, bf16[256,2304]{1,0:T(8,128)(2,1)S(1)}, u32[]{:S(2)}, u32[]{:S(2)}) collective-permute-start(bf16[256,2304]{1,0:T(8,128)(2,1)S(1)} %shard_map.129), channel_id=1, source_target_pairs={{0,8},{1,9},{2,10},{3,11},{4,12},{5,13},{6,14},{7,15},{8,0},{9,1},... | collective-permute-start | bytes 3538952 | tf_op jit(solution)/shard_map/ppermute | solution.py:30
  79.7 3.2 %collective-permute-start.24 = (bf16[144,1024]{1,0:T(8,128)(2,1)S(1)}, bf16[144,1024]{1,0:T(8,128)(2,1)S(1)}, u32[]{:S(2)}, u32[]{:S(2)}) collective-permute-start(bf16[144,1024]{1,0:T(8,128)(2,1)S(1)} %get-tuple-element.120), channel_id=1, source_target_pairs={{0,6},{1,7},{2,0},{3,1},{4,2},{5,3},{6,4},{7,5},{8,14},{9,15},{10,... | collective-permute-start | bytes 884744 | tf_op jit(solution)/shard_map/ppermute | solution.py:30
  82.9 2.9 %shard_map.131.rest_0_ = f32[256,2304]{1,0:T(8,128)S(1)} custom-call(s32[4]{0:T(128)S(1)} %pad_add_fusion.place, bf16[864,2048]{1,0:T(8,128)(2,1)S(1)} %shard_map.123.w013, bf16[288,2048]{1,0:T(8,128)(2,1)S(1)} %shard_map.124.w2, bf16[864,2048]{1,0:T(8,128)(2,1)S(1)} %collective-permute-done.8.v013, bf16[288,2048]{1,0:T(8,128)(2,1)S(1)} %collective-permute-done.11.v2, ...), custom_call_target="tpu_custom_call" | custom-call | tf_op jit(solution)/shard_map/pallas_call | solution.py:36
  87.2 3.1 %shard_map.132 = (f32[288,256]{1,0:T(8,128)S(1)}, bf16[288,256]{1,0:T(8,128)(2,1)S(1)}, bf16[288,256]{1,0:T(8,128)(2,1)S(1)}, bf16[288,256]{1,0:T(8,128)(2,1)S(1...) custom-call(s32[4]{0:T(128)S(1)} %pad_add_fusion.place, f32[288,1024]{1,0:T(8,128)S(1)} %get-tuple-element.78.w, ...), custom_call_target="tpu_custom_call" | custom-call | flops 49999998976 | bytes 500000000 | tf_op jit(solution)/shard_map/pallas_call | solution.py:36
  90.4 2.0 %collective-permute-start.15 = (bf16[288,256]{1,0:T(8,128)(2,1)S(1)}, bf16[288,256]{1,0:T(8,128)(2,1)S(1)}, u32[]{:S(2)}, u32[]{:S(2)}) collective-permute-start(bf16[288,256]{1,0:T(8,128)(2,1)S(1)} %get-tuple-element.108), channel_id=1, source_target_pairs={{0,16},{1,17},{2,18},{3,19},{4,20},{5,21},{6,22},{7,23},{8,24},{9,... | collective-permute-start | bytes 442376 | tf_op jit(solution)/shard_map/ppermute | solution.py:30
  92.3 3.6 %collective-permute-start.16 = (bf16[288,256]{1,0:T(8,128)(2,1)S(1)}, bf16[288,256]{1,0:T(8,128)(2,1)S(1)}, u32[]{:S(2)}, u32[]{:S(2)}) collective-permute-start(bf16[288,256]{1,0:T(8,128)(2,1)S(1)} %get-tuple-element.109), channel_id=1, source_target_pairs={{0,32},{1,33},{2,34},{3,35},{4,36},{5,37},{6,38},{7,39},{8,40},{9,... | collective-permute-start | bytes 442376 | tf_op jit(solution)/shard_map/ppermute | solution.py:30
  98.8 3.6 %collective-permute-start.26 = (bf16[288,1024]{1,0:T(8,128)(2,1)S(1)}, bf16[288,1024]{1,0:T(8,128)(2,1)S(1)}, u32[]{:S(2)}, u32[]{:S(2)}) collective-permute-start(bf16[288,1024]{1,0:T(8,128)(2,1)S(1)} %get-tuple-element.123), channel_id=1, source_target_pairs={{0,6},{1,7},{2,0},{3,1},{4,2},{5,3},{6,4},{7,5},{8,14},{9,15},{10,... | collective-permute-start | bytes 1769480 | tf_op jit(solution)/shard_map/ppermute | solution.py:30
  103.3 3.7 %shard_map.133.near = bf16[256,4608]{1,0:T(8,128)(2,1)} custom-call(s32[4]{0:T(128)S(1)} %pad_add_fusion.place, bf16[864,2048]{1,0:T(8,128)(2,1)S(1)} %shard_map.123.w013, bf16[288,2048]{1,0:T(8,128)(2,1)S(1)} %shard_map.124.w2, bf16[864,2048]{1,0:T(8,128)(2,1)S(1)} %collective-permute-done.8.v013, bf16[288,2048]{1,0:T(8,128)(2,1)S(1)} %collective-permute-done.11.v2, ...), custom_call_target="tpu_custom_call" | custom-call | tf_op jit(solution)/shard_map/pallas_call | solution.py:36
  108.6 2.0 %collective-permute-start.21 = (bf16[288,256]{1,0:T(8,128)(2,1)S(1)}, bf16[288,256]{1,0:T(8,128)(2,1)S(1)}, u32[]{:S(2)}, u32[]{:S(2)}) collective-permute-start(bf16[288,256]{1,0:T(8,128)(2,1)S(1)} %multiply_convert_fusion.m0), channel_id=1, source_target_pairs={{0,16},{1,17},{2,18},{3,19},{4,20},{5,21},{6,22},{7,23},{8,24},{9,... | collective-permute-start | bytes 442376 | tf_op jit(solution)/shard_map/ppermute | solution.py:30
  110.6 3.6 %collective-permute-start.20 = (bf16[288,256]{1,0:T(8,128)(2,1)S(1)}, bf16[288,256]{1,0:T(8,128)(2,1)S(1)}, u32[]{:S(2)}, u32[]{:S(2)}) collective-permute-start(bf16[288,256]{1,0:T(8,128)(2,1)S(1)} %multiply_convert_fusion.m0), channel_id=1, source_target_pairs={{0,32},{1,33},{2,34},{3,35},{4,36},{5,37},{6,38},{7,39},{8,40},{9,... | collective-permute-start | bytes 442376 | tf_op jit(solution)/shard_map/ppermute | solution.py:30
  115.2 1.6 %shard_map.134 = bf16[256,4608]{1,0:T(8,128)(2,1)} custom-call(s32[4]{0:T(128)S(1)} %pad_add_fusion.place, bf16[256,2304]{1,0:T(8,128)(2,1)S(1)} %collective-permute-done.22.far, bf16[256,4608]{1,0:T(8,128)(2,1)} %shard_map.133.near), custom_call_target="tpu_custom_call", output_to_operand_aliasing={{}: (2, {})} | custom-call | tf_op jit(solution)/shard_map/pallas_call | solution.py:36
  116.8 3.8 %shard_map.136 = (f32[288,2,1024]{2,1,0:T(2,128)}, f32[288,2,1024]{2,1,0:T(2,128)}, f32[288,1024]{1,0:T(8,128)S(1)}) custom-call(s32[4]{0:T(128)S(1)} %pad_add_fusion.place, f32[288,1024]{1,0:T(8,128)S(1)} %get-tuple-element.113.m_key, f32[288,1024]{1,0:T(8,128)S(1)} %get-tuple-element.114.v_key, f32[288,1024]{1,0:T(8,128)S(1)} %get-tuple-element.115.w, ...), custom_call_target="tpu_custom_call" | custom-call | tf_op jit(solution)/shard_map/pallas_call | solution.py:36
  120.6 3.1 %shard_map.137 = (f32[288,2,1024]{2,1,0:T(2,128)}, f32[288,1024]{1,0:T(8,128)}, f32[288,1024]{1,0:T(8,128)}) custom-call(s32[4]{0:T(128)S(1)} %pad_add_fusion.place, bf16[288,256]{1,0:T(8,128)(2,1)S(1)} %multiply_convert_fusion.m0, bf16[288,256]{1,0:T(8,128)(2,1)S(1)} %collective-permute-done.19.m1, bf16[288,256]{1,0:T(8,128)(2,1)S(1)} %collective-permute-done.20.m2, ...), custom_call_target="tpu_custom_call" | custom-call | tf_op jit(solution)/shard_map/pallas_call | solution.py:36
  (69 shorter events, 15.2 us)
Async XLA Ops:
  2.4 4.0 %copy-start = (f32[1,288,2,1024]{3,2,1,0:T(2,128)S(1)}, f32[1,288,2,1024]{3,2,1,0:T(2,128)}, u32[]{:S(2)}) copy-start(f32[1,288,2,1024]{3,2,1,0:T(2,128)} %param.9) | copy-start | bytes 7077892
  3.0 30.4 %collective-permute-start = (bf16[256,2304]{1,0:T(8,128)(2,1)S(1)}, bf16[256,2304]{1,0:T(8,128)(2,1)S(1)}, u32[]{:S(2)}, u32[]{:S(2)}) collective-permute-start(bf16[256,2304]{1,0:T(8,128)(2,1)S(1)} %shard_map.118), channel_id=1, source_target_pairs={{0,8},{1,9},{2,10},{3,11},{4,12},{5,13},{6,14},{7,15},{8,0},{9,1},... | collective-permute-start | bytes 3538952 | tf_op jit(solution)/shard_map/ppermute | solution.py:30
  6.4 6.2 %copy-start.9 = (bf16[1,256,2,1024]{3,2,1,0:T(2,128)(2,1)S(1)}, bf16[1,256,2,1024]{3,2,1,0:T(2,128)(2,1)}, u32[]{:S(2)}) copy-start(bf16[1,256,2,1024]{3,2,1,0:T(2,128)(2,1)} %param.8) | copy-start | bytes 3145732
  6.4 7.6 %copy-start.2 = (f32[1,288,2,1024]{3,2,1,0:T(2,128)S(1)}, f32[1,288,2,1024]{3,2,1,0:T(2,128)}, u32[]{:S(2)}) copy-start(f32[1,288,2,1024]{3,2,1,0:T(2,128)} %param.11) | copy-start | bytes 7077892
  9.3 28.7 %collective-permute-start.2 = (bf16[288,2048]{1,0:T(8,128)(2,1)S(1)}, bf16[288,2048]{1,0:T(8,128)(2,1)S(1)}, u32[]{:S(2)}, u32[]{:S(2)}) collective-permute-start(bf16[288,2048]{1,0:T(8,128)(2,1)S(1)} %shard_map.119.refs_0_), channel_id=1, source_target_pairs={{0,2},{1,3},{2,4},{3,5},{4,6},{5,7},{6,0},{7,1},{8,10},{9,11},{10,... | collective-permute-start | bytes 3538952 | tf_op jit(solution)/shard_map/ppermute | solution.py:30
  10.9 27.1 %collective-permute-start.1 = (bf16[288,2048]{1,0:T(8,128)(2,1)S(1)}, bf16[288,2048]{1,0:T(8,128)(2,1)S(1)}, u32[]{:S(2)}, u32[]{:S(2)}) collective-permute-start(bf16[288,2048]{1,0:T(8,128)(2,1)S(1)} %shard_map.119.refs_0_), channel_id=1, source_target_pairs={{0,6},{1,7},{2,0},{3,1},{4,2},{5,3},{6,4},{7,5},{8,14},{9,15},{10,... | collective-permute-start | bytes 3538952 | tf_op jit(solution)/shard_map/ppermute | solution.py:30
  13.0 31.7 %copy-start.5 = (bf16[256,1024]{1,0:T(8,128)(2,1)}, bf16[256,1024]{1,0:T(8,128)(2,1)S(1)}, u32[]{:S(2)}) copy-start(bf16[256,1024]{1,0:T(8,128)(2,1)S(1)} %get-tuple-element.133.c_own.tokens) | copy-start | bytes 1572868
  13.0 31.7 %collective-permute-start.3 = (bf16[256,1024]{1,0:T(8,128)(2,1)S(1)}, bf16[256,1024]{1,0:T(8,128)(2,1)S(1)}, u32[]{:S(2)}, u32[]{:S(2)}) collective-permute-start(bf16[256,1024]{1,0:T(8,128)(2,1)S(1)} %get-tuple-element.133.c_own.tokens), channel_id=1, source_target_pairs={{0,8},{1,9},{2,10},{3,11},{4,12},{5,13},{6,14},{7,15},{8,0},{9,1},... | collective-permute-start | bytes 1572872 | tf_op jit(solution)/shard_map/ppermute | solution.py:30
  14.5 19.0 %copy-start.4 = (bf16[1,256,4608]{2,1,0:T(8,128)(2,1)S(1)}, bf16[1,256,4608]{2,1,0:T(8,128)(2,1)}, u32[]{:S(2)}) copy-start(bf16[1,256,4608]{2,1,0:T(8,128)(2,1)} %param.7) | copy-start | bytes 7077892
  16.3 38.5 %collective-permute-start.5 = (bf16[256,1024]{1,0:T(8,128)(2,1)S(1)}, bf16[256,1024]{1,0:T(8,128)(2,1)S(1)}, u32[]{:S(2)}, u32[]{:S(2)}) collective-permute-start(bf16[256,1024]{1,0:T(8,128)(2,1)S(1)} %get-tuple-element.84.c_own.tokens), channel_id=1, source_target_pairs={{0,8},{1,9},{2,10},{3,11},{4,12},{5,13},{6,14},{7,15},{8,0},{9,1},... | collective-permute-start | bytes 1572872 | tf_op jit(solution)/shard_map/ppermute | solution.py:30
  38.9 15.9 %collective-permute-start.7 = (bf16[144,2048]{1,0:T(8,128)(2,1)S(1)}, bf16[144,2048]{1,0:T(8,128)(2,1)S(1)}, u32[]{:S(2)}, u32[]{:S(2)}) collective-permute-start(bf16[144,2048]{1,0:T(8,128)(2,1)S(1)} %slice.15), channel_id=1, source_target_pairs={{0,6},{1,7},{2,0},{3,1},{4,2},{5,3},{6,4},{7,5},{8,14},{9,15},{10,... | collective-permute-start | bytes 1769480 | tf_op jit(solution)/shard_map/ppermute | solution.py:30
  41.9 14.5 %collective-permute-start.6 = (bf16[144,2048]{1,0:T(8,128)(2,1)S(1)}, bf16[144,2048]{1,0:T(8,128)(2,1)S(1)}, u32[]{:S(2)}, u32[]{:S(2)}) collective-permute-start(bf16[144,2048]{1,0:T(8,128)(2,1)S(1)} %slice.14), channel_id=1, source_target_pairs={{0,2},{1,3},{2,4},{3,5},{4,6},{5,7},{6,0},{7,1},{8,10},{9,11},{10,... | collective-permute-start | bytes 1769480 | tf_op jit(solution)/shard_map/ppermute | solution.py:30
  41.9 14.5 %collective-permute-start.8 = (bf16[864,2048]{1,0:T(8,128)(2,1)S(1)}, bf16[864,2048]{1,0:T(8,128)(2,1)S(1)}, u32[]{:S(2)}, u32[]{:S(2)}) collective-permute-start(bf16[864,2048]{1,0:T(8,128)(2,1)S(1)} %shard_map.123.w013), channel_id=1, source_target_pairs={{0,1},{1,0},{2,3},{3,2},{4,5},{5,4},{6,7},{7,6},{8,9},{9,8},{10,11... | collective-permute-start | bytes 10616840 | tf_op jit(solution)/shard_map/ppermute | solution.py:30
  49.4 7.8 %collective-permute-start.4 = (bf16[4,288,1024]{2,1,0:T(8,128)(2,1)S(1)}, bf16[4,288,1024]{2,1,0:T(8,128)(2,1)S(1)}, u32[]{:S(2)}, u32[]{:S(2)}) collective-permute-start(bf16[4,288,1024]{2,1,0:T(8,128)(2,1)S(1)} %get-tuple-element.83), channel_id=1, source_target_pairs={{0,1},{1,0},{2,3},{3,2},{4,5},{5,4},{6,7},{7,6},{8,9},{9,8},{10,11... | collective-permute-start | bytes 7077896 | tf_op jit(solution)/shard_map/ppermute | solution.py:30
  57.1 8.9 %collective-permute-start.11 = (bf16[288,2048]{1,0:T(8,128)(2,1)S(1)}, bf16[288,2048]{1,0:T(8,128)(2,1)S(1)}, u32[]{:S(2)}, u32[]{:S(2)}) collective-permute-start(bf16[288,2048]{1,0:T(8,128)(2,1)S(1)} %shard_map.124.w2), channel_id=1, source_target_pairs={{0,1},{1,0},{2,3},{3,2},{4,5},{5,4},{6,7},{7,6},{8,9},{9,8},{10,11... | collective-permute-start | bytes 3538952 | tf_op jit(solution)/shard_map/ppermute | solution.py:30
  57.9 11.1 %collective-permute-start.9 = (bf16[144,1024]{1,0:T(8,128)(2,1)S(1)}, bf16[144,1024]{1,0:T(8,128)(2,1)S(1)}, u32[]{:S(2)}, u32[]{:S(2)}) collective-permute-start(bf16[144,1024]{1,0:T(8,128)(2,1)S(1)} %get-tuple-element.90), channel_id=1, source_target_pairs={{0,2},{1,3},{2,4},{3,5},{4,6},{5,7},{6,0},{7,1},{8,10},{9,11},{10,... | collective-permute-start | bytes 884744 | tf_op jit(solution)/shard_map/ppermute | solution.py:30
  57.9 11.0 %collective-permute-start.10 = (bf16[144,1024]{1,0:T(8,128)(2,1)S(1)}, bf16[144,1024]{1,0:T(8,128)(2,1)S(1)}, u32[]{:S(2)}, u32[]{:S(2)}) collective-permute-start(bf16[144,1024]{1,0:T(8,128)(2,1)S(1)} %get-tuple-element.91), channel_id=1, source_target_pairs={{0,6},{1,7},{2,0},{3,1},{4,2},{5,3},{6,4},{7,5},{8,14},{9,15},{10,... | collective-permute-start | bytes 884744 | tf_op jit(solution)/shard_map/ppermute | solution.py:30
  65.9 13.1 %collective-permute-start.14 = (bf16[4,288,1024]{2,1,0:T(8,128)(2,1)S(1)}, bf16[4,288,1024]{2,1,0:T(8,128)(2,1)S(1)}, u32[]{:S(2)}, u32[]{:S(2)}) collective-permute-start(bf16[4,288,1024]{2,1,0:T(8,128)(2,1)S(1)} %get-tuple-element.94), channel_id=1, source_target_pairs={{0,1},{1,0},{2,3},{3,2},{4,5},{5,4},{6,7},{7,6},{8,9},{9,8},{10,11... | collective-permute-start | bytes 7077896 | tf_op jit(solution)/shard_map/ppermute | solution.py:30
  69.8 17.4 %collective-permute-start.12 = (bf16[288,1024]{1,0:T(8,128)(2,1)S(1)}, bf16[288,1024]{1,0:T(8,128)(2,1)S(1)}, u32[]{:S(2)}, u32[]{:S(2)}) collective-permute-start(bf16[288,1024]{1,0:T(8,128)(2,1)S(1)} %get-tuple-element.98), channel_id=1, source_target_pairs={{0,2},{1,3},{2,4},{3,5},{4,6},{5,7},{6,0},{7,1},{8,10},{9,11},{10,... | collective-permute-start | bytes 1769480 | tf_op jit(solution)/shard_map/ppermute | solution.py:30
  69.9 16.9 %collective-permute-start.13 = (bf16[288,1024]{1,0:T(8,128)(2,1)S(1)}, bf16[288,1024]{1,0:T(8,128)(2,1)S(1)}, u32[]{:S(2)}, u32[]{:S(2)}) collective-permute-start(bf16[288,1024]{1,0:T(8,128)(2,1)S(1)} %get-tuple-element.99), channel_id=1, source_target_pairs={{0,6},{1,7},{2,0},{3,1},{4,2},{5,3},{6,4},{7,5},{8,14},{9,15},{10,... | collective-permute-start | bytes 1769480 | tf_op jit(solution)/shard_map/ppermute | solution.py:30
  77.2 37.0 %collective-permute-start.22 = (bf16[256,2304]{1,0:T(8,128)(2,1)S(1)}, bf16[256,2304]{1,0:T(8,128)(2,1)S(1)}, u32[]{:S(2)}, u32[]{:S(2)}) collective-permute-start(bf16[256,2304]{1,0:T(8,128)(2,1)S(1)} %shard_map.129), channel_id=1, source_target_pairs={{0,8},{1,9},{2,10},{3,11},{4,12},{5,13},{6,14},{7,15},{8,0},{9,1},... | collective-permute-start | bytes 3538952 | tf_op jit(solution)/shard_map/ppermute | solution.py:30
  79.6 17.3 %collective-permute-start.23 = (bf16[144,1024]{1,0:T(8,128)(2,1)S(1)}, bf16[144,1024]{1,0:T(8,128)(2,1)S(1)}, u32[]{:S(2)}, u32[]{:S(2)}) collective-permute-start(bf16[144,1024]{1,0:T(8,128)(2,1)S(1)} %get-tuple-element.103), channel_id=1, source_target_pairs={{0,2},{1,3},{2,4},{3,5},{4,6},{5,7},{6,0},{7,1},{8,10},{9,11},{10,... | collective-permute-start | bytes 884744 | tf_op jit(solution)/shard_map/ppermute | solution.py:30
  79.7 16.2 %collective-permute-start.24 = (bf16[144,1024]{1,0:T(8,128)(2,1)S(1)}, bf16[144,1024]{1,0:T(8,128)(2,1)S(1)}, u32[]{:S(2)}, u32[]{:S(2)}) collective-permute-start(bf16[144,1024]{1,0:T(8,128)(2,1)S(1)} %get-tuple-element.120), channel_id=1, source_target_pairs={{0,6},{1,7},{2,0},{3,1},{4,2},{5,3},{6,4},{7,5},{8,14},{9,15},{10,... | collective-permute-start | bytes 884744 | tf_op jit(solution)/shard_map/ppermute | solution.py:30
  90.4 8.5 %collective-permute-start.15 = (bf16[288,256]{1,0:T(8,128)(2,1)S(1)}, bf16[288,256]{1,0:T(8,128)(2,1)S(1)}, u32[]{:S(2)}, u32[]{:S(2)}) collective-permute-start(bf16[288,256]{1,0:T(8,128)(2,1)S(1)} %get-tuple-element.108), channel_id=1, source_target_pairs={{0,16},{1,17},{2,18},{3,19},{4,20},{5,21},{6,22},{7,23},{8,24},{9,... | collective-permute-start | bytes 442376 | tf_op jit(solution)/shard_map/ppermute | solution.py:30
  92.3 10.1 %collective-permute-start.16 = (bf16[288,256]{1,0:T(8,128)(2,1)S(1)}, bf16[288,256]{1,0:T(8,128)(2,1)S(1)}, u32[]{:S(2)}, u32[]{:S(2)}) collective-permute-start(bf16[288,256]{1,0:T(8,128)(2,1)S(1)} %get-tuple-element.109), channel_id=1, source_target_pairs={{0,32},{1,33},{2,34},{3,35},{4,36},{5,37},{6,38},{7,39},{8,40},{9,... | collective-permute-start | bytes 442376 | tf_op jit(solution)/shard_map/ppermute | solution.py:30
  95.9 6.5 %collective-permute-start.17 = (bf16[288,256]{1,0:T(8,128)(2,1)S(1)}, bf16[288,256]{1,0:T(8,128)(2,1)S(1)}, u32[]{:S(2)}, u32[]{:S(2)}) collective-permute-start(bf16[288,256]{1,0:T(8,128)(2,1)S(1)} %get-tuple-element.110), channel_id=1, source_target_pairs={{0,48},{1,49},{2,50},{3,51},{4,52},{5,53},{6,54},{7,55},{8,56},{9,... | collective-permute-start | bytes 442376 | tf_op jit(solution)/shard_map/ppermute | solution.py:30
  97.9 18.9 %collective-permute-start.25 = (bf16[288,1024]{1,0:T(8,128)(2,1)S(1)}, bf16[288,1024]{1,0:T(8,128)(2,1)S(1)}, u32[]{:S(2)}, u32[]{:S(2)}) collective-permute-start(bf16[288,1024]{1,0:T(8,128)(2,1)S(1)} %get-tuple-element.122), channel_id=1, source_target_pairs={{0,2},{1,3},{2,4},{3,5},{4,6},{5,7},{6,0},{7,1},{8,10},{9,11},{10,... | collective-permute-start | bytes 1769480 | tf_op jit(solution)/shard_map/ppermute | solution.py:30
  98.8 18.0 %collective-permute-start.26 = (bf16[288,1024]{1,0:T(8,128)(2,1)S(1)}, bf16[288,1024]{1,0:T(8,128)(2,1)S(1)}, u32[]{:S(2)}, u32[]{:S(2)}) collective-permute-start(bf16[288,1024]{1,0:T(8,128)(2,1)S(1)} %get-tuple-element.123), channel_id=1, source_target_pairs={{0,6},{1,7},{2,0},{3,1},{4,2},{5,3},{6,4},{7,5},{8,14},{9,15},{10,... | collective-permute-start | bytes 1769480 | tf_op jit(solution)/shard_map/ppermute | solution.py:30
  102.5 6.0 %collective-permute-start.18 = (bf16[288,256]{1,0:T(8,128)(2,1)S(1)}, bf16[288,256]{1,0:T(8,128)(2,1)S(1)}, u32[]{:S(2)}, u32[]{:S(2)}) collective-permute-start(bf16[288,256]{1,0:T(8,128)(2,1)S(1)} %get-tuple-element.130), channel_id=1, source_target_pairs={{0,64},{1,65},{2,66},{3,67},{4,68},{5,69},{6,70},{7,71},{8,72},{9,... | collective-permute-start | bytes 442376 | tf_op jit(solution)/shard_map/ppermute | solution.py:30
  108.6 12.0 %collective-permute-start.21 = (bf16[288,256]{1,0:T(8,128)(2,1)S(1)}, bf16[288,256]{1,0:T(8,128)(2,1)S(1)}, u32[]{:S(2)}, u32[]{:S(2)}) collective-permute-start(bf16[288,256]{1,0:T(8,128)(2,1)S(1)} %multiply_convert_fusion.m0), channel_id=1, source_target_pairs={{0,16},{1,17},{2,18},{3,19},{4,20},{5,21},{6,22},{7,23},{8,24},{9,... | collective-permute-start | bytes 442376 | tf_op jit(solution)/shard_map/ppermute | solution.py:30
  110.6 10.0 %collective-permute-start.20 = (bf16[288,256]{1,0:T(8,128)(2,1)S(1)}, bf16[288,256]{1,0:T(8,128)(2,1)S(1)}, u32[]{:S(2)}, u32[]{:S(2)}) collective-permute-start(bf16[288,256]{1,0:T(8,128)(2,1)S(1)} %multiply_convert_fusion.m0), channel_id=1, source_target_pairs={{0,32},{1,33},{2,34},{3,35},{4,36},{5,37},{6,38},{7,39},{8,40},{9,... | collective-permute-start | bytes 442376 | tf_op jit(solution)/shard_map/ppermute | solution.py:30
  114.2 6.5 %collective-permute-start.19 = (bf16[288,256]{1,0:T(8,128)(2,1)S(1)}, bf16[288,256]{1,0:T(8,128)(2,1)S(1)}, u32[]{:S(2)}, u32[]{:S(2)}) collective-permute-start(bf16[288,256]{1,0:T(8,128)(2,1)S(1)} %multiply_convert_fusion.m0), channel_id=1, source_target_pairs={{0,48},{1,49},{2,50},{3,51},{4,52},{5,53},{6,54},{7,55},{8,56},{9,... | collective-permute-start | bytes 442376 | tf_op jit(solution)/shard_map/ppermute | solution.py:30
  (5 other events, 15.2 us)

commit v5 on v4

--- a/solution.py
+++ b/solution.py
@@ -483,11 +483,11 @@
         [shape((rows, 2, feat), F32)] + [shape((rows, feat), F32)] * 2,
         place,
         (*means, anchor, momentum, inner),
-        [half_quarter] * 4 + [half_rows] * 3,
-        [half_both] + [half_rows] * 2,
-        [pltpu.VMEM((hr, feat), F32)],
-        grid=(2,),
+        [whole(rows, qc)] * 4 + [whole(rows, feat)] * 3,
+        [whole(rows, 2, feat)] + [whole(rows, feat)] * 2,
+        [pltpu.VMEM((rows, feat), F32)],
         moved=9 * 2**20,
+        vmem=24,
     )
 
     return (

time: 124 us -> 124 us (level)
  transfers between devices with their start and end apart: 27 -> 27, of which waited for: 8 -> 8; matrix products, arithmetic and copies ran while one was open for 0% -> 0% of each run, Pallas kernels for 34% -> 33%
where the time goes in v5:
time: 124 us
  Pallas kernels  45.7 us (37%)
  starting transfers between devices  43.3 us (35%)
  waiting for transfers between devices  31.4 us (25%)
  local copies, waits for them, and re-layouts  2.6 us (2%)
    pallas_call x20, Pallas kernels, call(): pl.pallas_call(kernel, out_shape=out_shape, grid_spec=pltpu.PrefetchScala...  45.7 us
    ppermute x27, starting transfers between devices, shift(): return lax.ppermute(value, AXES, pairs)  43.3 us
    ppermute x27, waiting for transfers between devices, shift(): return lax.ppermute(value, AXES, pairs)  31.4 us
  transfers between devices with their start and end apart: 27, of which 8 were waited for; matrix products, arithmetic and copies ran while one was open for 0% of the time, Pallas kernels for 33%

profile of v5, /device:TPU:0, one launch (start us, length us, event | category | flops | bytes accessed | tf_op | source)
XLA Modules:
  0.0 124.1 jit_solution(12950926408146641470)
XLA Ops:
  0.7 1.7 %copy-done.3 = bf16[1,256,4608]{2,1,0:T(8,128)(2,1)S(1)} copy-done((bf16[1,256,4608]{2,1,0:T(8,128)(2,1)S(1)}, bf16[1,256,4608]{2,1,0:T(8,128)(2,1)}, u32[]{:S(2)}) %copy-start.3) | copy-done | bytes 2359320
  3.0 3.4 %collective-permute-start = (bf16[256,2304]{1,0:T(8,128)(2,1)S(1)}, bf16[256,2304]{1,0:T(8,128)(2,1)S(1)}, u32[]{:S(2)}, u32[]{:S(2)}) collective-permute-start(bf16[256,2304]{1,0:T(8,128)(2,1)S(1)} %shard_map.118), channel_id=1, source_target_pairs={{0,8},{1,9},{2,10},{3,11},{4,12},{5,13},{6,14},{7,15},{8,0},{9,1},... | collective-permute-start | bytes 3538952 | tf_op jit(solution)/shard_map/ppermute | solution.py:30
  6.4 2.9 %shard_map.119.refs_0_ = bf16[288,2048]{1,0:T(8,128)(2,1)S(1)} custom-call(s32[4]{0:T(128)S(1)} %pad_add_fusion.place, f32[288,2,1024]{2,1,0:T(2,128)S(1)} %bitcast.19), custom_call_target="tpu_custom_call" | custom-call | flops 49999998976 | bytes 500000000 | tf_op jit(solution)/shard_map/pallas_call | solution.py:36
  9.3 1.6 %collective-permute-start.2 = (bf16[288,2048]{1,0:T(8,128)(2,1)S(1)}, bf16[288,2048]{1,0:T(8,128)(2,1)S(1)}, u32[]{:S(2)}, u32[]{:S(2)}) collective-permute-start(bf16[288,2048]{1,0:T(8,128)(2,1)S(1)} %shard_map.119.refs_0_), channel_id=1, source_target_pairs={{0,2},{1,3},{2,4},{3,5},{4,6},{5,7},{6,0},{7,1},{8,10},{9,11},{10,... | collective-permute-start | bytes 3538952 | tf_op jit(solution)/shard_map/ppermute | solution.py:30
  10.9 1.7 %collective-permute-start.1 = (bf16[288,2048]{1,0:T(8,128)(2,1)S(1)}, bf16[288,2048]{1,0:T(8,128)(2,1)S(1)}, u32[]{:S(2)}, u32[]{:S(2)}) collective-permute-start(bf16[288,2048]{1,0:T(8,128)(2,1)S(1)} %shard_map.119.refs_0_), channel_id=1, source_target_pairs={{0,6},{1,7},{2,0},{3,1},{4,2},{5,3},{6,4},{7,5},{8,14},{9,15},{10,... | collective-permute-start | bytes 3538952 | tf_op jit(solution)/shard_map/ppermute | solution.py:30
  14.5 1.8 %shard_map.120 = (f32[288,1024]{1,0:T(8,128)S(1)}, f32[288,1024]{1,0:T(8,128)S(1)}, f32[288,1024]{1,0:T(8,128)S(1)}, f32[288,1024]{1,0:T(8,128)S(1)}, f32[288,1024]{1,0:T(8,128)S(1)}, /*index=5*/f32[288,1024]{1,0:T(8,128)S(1)}) custom-call(s32[4]{0:T(128)S(1)} %pad_add_fusion.place, f32[288,2,1024]{2,1,0:T(2,128)S(1)} %bitcast.20, ...), custom_call_target="tpu_custom_call" | custom-call | tf_op jit(solution)/shard_map/pallas_call | solution.py:36
  16.3 2.2 %collective-permute-start.5 = (bf16[256,1024]{1,0:T(8,128)(2,1)S(1)}, bf16[256,1024]{1,0:T(8,128)(2,1)S(1)}, u32[]{:S(2)}, u32[]{:S(2)}) collective-permute-start(bf16[256,1024]{1,0:T(8,128)(2,1)S(1)} %get-tuple-element.84.c_own.tokens), channel_id=1, source_target_pairs={{0,8},{1,9},{2,10},{3,11},{4,12},{5,13},{6,14},{7,15},{8,0},{9,1},... | collective-permute-start | bytes 1572872 | tf_op jit(solution)/shard_map/ppermute | solution.py:30
  18.5 14.9 %collective-permute-done.far = bf16[256,2304]{1,0:T(8,128)(2,1)S(1)} collective-permute-done((bf16[256,2304]{1,0:T(8,128)(2,1)S(1)}, bf16[256,2304]{1,0:T(8,128)(2,1)S(1)}, u32[]{:S(2)}, u32[]{:S(2)}) %collective-permute-start) | collective-permute-done | bytes 1179680 | tf_op jit(solution)/shard_map/ppermute | solution.py:30
  34.2 3.8 %collective-permute-done.2.refs_2_ = bf16[288,2048]{1,0:T(8,128)(2,1)S(1)} collective-permute-done((bf16[288,2048]{1,0:T(8,128)(2,1)S(1)}, bf16[288,2048]{1,0:T(8,128)(2,1)S(1)}, u32[]{:S(2)}, u32[]{:S(2)}) %collective-permute-start.2) | collective-permute-done | bytes 1179680 | tf_op jit(solution)/shard_map/ppermute | solution.py:30
  38.9 3.0 %collective-permute-start.7 = (bf16[144,2048]{1,0:T(8,128)(2,1)S(1)}, bf16[144,2048]{1,0:T(8,128)(2,1)S(1)}, u32[]{:S(2)}, u32[]{:S(2)}) collective-permute-start(bf16[144,2048]{1,0:T(8,128)(2,1)S(1)} %slice.15), channel_id=1, source_target_pairs={{0,6},{1,7},{2,0},{3,1},{4,2},{5,3},{6,4},{7,5},{8,14},{9,15},{10,... | collective-permute-start | bytes 1769480 | tf_op jit(solution)/shard_map/ppermute | solution.py:30
  41.9 2.8 %collective-permute-done.3.c_far.tokens = bf16[256,1024]{1,0:T(8,128)(2,1)S(1)} collective-permute-done((bf16[256,1024]{1,0:T(8,128)(2,1)S(1)}, bf16[256,1024]{1,0:T(8,128)(2,1)S(1)}, u32[]{:S(2)}, u32[]{:S(2)}) %collective-permute-start.3) | collective-permute-done | bytes 524320 | tf_op jit(solution)/shard_map/ppermute | solution.py:30
  44.7 4.7 %shard_map.122 = (bf16[4,288,1024]{2,1,0:T(8,128)(2,1)S(1)}, bf16[4,288,1024]{2,1,0:T(8,128)(2,1)S(1)}) custom-call(s32[4]{0:T(128)S(1)} %pad_add_fusion.place, bf16[512,2304]{1,0:T(8,128)(2,1)S(1)} %shard_map.121.a_both, bf16[256,1024]{1,0:T(8,128)(2,1)S(1)} %get-tuple-element.133.c_own.tokens, bf16[256,1024]{1,0:T(8,128)(2,1)S(1)} %collective-permute-done.3.c_far.tokens), custom_call_target="tpu_custom_call" | custom-call | flops 49999998976 | bytes 500000000 | tf_op jit(solution)/shard_map/pallas_call | solution.py:36
  49.5 5.3 %collective-permute-done.5.c_far.tokens = bf16[256,1024]{1,0:T(8,128)(2,1)S(1)} collective-permute-done((bf16[256,1024]{1,0:T(8,128)(2,1)S(1)}, bf16[256,1024]{1,0:T(8,128)(2,1)S(1)}, u32[]{:S(2)}, u32[]{:S(2)}) %collective-permute-start.5) | collective-permute-done | bytes 524320 | tf_op jit(solution)/shard_map/ppermute | solution.py:30
  54.8 1.6 %collective-permute-done.6.refs_0_ = bf16[144,2048]{1,0:T(8,128)(2,1)S(1)} collective-permute-done((bf16[144,2048]{1,0:T(8,128)(2,1)S(1)}, bf16[144,2048]{1,0:T(8,128)(2,1)S(1)}, u32[]{:S(2)}, u32[]{:S(2)}) %collective-permute-start.6) | collective-permute-done | bytes 589856 | tf_op jit(solution)/shard_map/ppermute | solution.py:30
  57.9 3.2 %collective-permute-start.10 = (bf16[144,1024]{1,0:T(8,128)(2,1)S(1)}, bf16[144,1024]{1,0:T(8,128)(2,1)S(1)}, u32[]{:S(2)}, u32[]{:S(2)}) collective-permute-start(bf16[144,1024]{1,0:T(8,128)(2,1)S(1)} %get-tuple-element.91), channel_id=1, source_target_pairs={{0,6},{1,7},{2,0},{3,1},{4,2},{5,3},{6,4},{7,5},{8,14},{9,15},{10,... | collective-permute-start | bytes 884744 | tf_op jit(solution)/shard_map/ppermute | solution.py:30
  61.2 4.7 %shard_map.126 = (bf16[4,288,1024]{2,1,0:T(8,128)(2,1)S(1)}, bf16[4,288,1024]{2,1,0:T(8,128)(2,1)S(1)}) custom-call(s32[4]{0:T(128)S(1)} %pad_add_fusion.place, bf16[512,2304]{1,0:T(8,128)(2,1)S(1)} %shard_map.121.a_both, bf16[256,1024]{1,0:T(8,128)(2,1)S(1)} %get-tuple-element.84.c_own.tokens, bf16[256,1024]{1,0:T(8,128)(2,1)S(1)} %collective-permute-done.5.c_far.tokens), custom_call_target="tpu_custom_call" | custom-call | flops 49999998976 | bytes 500000000 | tf_op jit(solution)/shard_map/pallas_call | solution.py:36
  66.0 2.9 %shard_map.127.rest_0_ = f32[256,2304]{1,0:T(8,128)S(1)} custom-call(s32[4]{0:T(128)S(1)} %pad_add_fusion.place, bf16[864,2048]{1,0:T(8,128)(2,1)S(1)} %shard_map.123.w013, bf16[288,2048]{1,0:T(8,128)(2,1)S(1)} %shard_map.124.w2, bf16[864,2048]{1,0:T(8,128)(2,1)S(1)} %collective-permute-done.8.v013, bf16[288,2048]{1,0:T(8,128)(2,1)S(1)} %collective-permute-done.11.v2, ...), custom_call_target="tpu_custom_call" | custom-call | tf_op jit(solution)/shard_map/pallas_call | solution.py:36
  69.9 3.2 %collective-permute-start.13 = (bf16[288,1024]{1,0:T(8,128)(2,1)S(1)}, bf16[288,1024]{1,0:T(8,128)(2,1)S(1)}, u32[]{:S(2)}, u32[]{:S(2)}) collective-permute-start(bf16[288,1024]{1,0:T(8,128)(2,1)S(1)} %get-tuple-element.99), channel_id=1, source_target_pairs={{0,6},{1,7},{2,0},{3,1},{4,2},{5,3},{6,4},{7,5},{8,14},{9,15},{10,... | collective-permute-start | bytes 1769480 | tf_op jit(solution)/shard_map/ppermute | solution.py:30
  73.1 4.1 %shard_map.129 = bf16[256,2304]{1,0:T(8,128)(2,1)S(1)} custom-call(s32[4]{0:T(128)S(1)} %pad_add_fusion.place, bf16[864,2048]{1,0:T(8,128)(2,1)S(1)} %shard_map.123.w013, bf16[288,2048]{1,0:T(8,128)(2,1)S(1)} %shard_map.124.w2, bf16[864,2048]{1,0:T(8,128)(2,1)S(1)} %collective-permute-done.8.v013, bf16[288,2048]{1,0:T(8,128)(2,1)S(1)} %collective-permute-done.11.v2, ...), custom_call_target="tpu_custom_call" | custom-call | flops 49999998976 | bytes 500000000 | tf_op jit(solution)/shard_map/pallas_call | solution.py:36
  77.2 1.7 %collective-permute-start.22 = (bf16[256,2304]{1,0:T(8,128)(2,1)S(1)}, bf16[256,2304]{1,0:T(8,128)(2,1)S(1)}, u32[]{:S(2)}, u32[]{:S(2)}) collective-permute-start(bf16[256,2304]{1,0:T(8,128)(2,1)S(1)} %shard_map.129), channel_id=1, source_target_pairs={{0,8},{1,9},{2,10},{3,11},{4,12},{5,13},{6,14},{7,15},{8,0},{9,1},... | collective-permute-start | bytes 3538952 | tf_op jit(solution)/shard_map/ppermute | solution.py:30
  79.7 3.2 %collective-permute-start.24 = (bf16[144,1024]{1,0:T(8,128)(2,1)S(1)}, bf16[144,1024]{1,0:T(8,128)(2,1)S(1)}, u32[]{:S(2)}, u32[]{:S(2)}) collective-permute-start(bf16[144,1024]{1,0:T(8,128)(2,1)S(1)} %get-tuple-element.120), channel_id=1, source_target_pairs={{0,6},{1,7},{2,0},{3,1},{4,2},{5,3},{6,4},{7,5},{8,14},{9,15},{10,... | collective-permute-start | bytes 884744 | tf_op jit(solution)/shard_map/ppermute | solution.py:30
  82.9 2.9 %shard_map.131.rest_0_ = f32[256,2304]{1,0:T(8,128)S(1)} custom-call(s32[4]{0:T(128)S(1)} %pad_add_fusion.place, bf16[864,2048]{1,0:T(8,128)(2,1)S(1)} %shard_map.123.w013, bf16[288,2048]{1,0:T(8,128)(2,1)S(1)} %shard_map.124.w2, bf16[864,2048]{1,0:T(8,128)(2,1)S(1)} %collective-permute-done.8.v013, bf16[288,2048]{1,0:T(8,128)(2,1)S(1)} %collective-permute-done.11.v2, ...), custom_call_target="tpu_custom_call" | custom-call | tf_op jit(solution)/shard_map/pallas_call | solution.py:36
  87.2 3.1 %shard_map.132 = (f32[288,256]{1,0:T(8,128)S(1)}, bf16[288,256]{1,0:T(8,128)(2,1)S(1)}, bf16[288,256]{1,0:T(8,128)(2,1)S(1)}, bf16[288,256]{1,0:T(8,128)(2,1)S(1...) custom-call(s32[4]{0:T(128)S(1)} %pad_add_fusion.place, f32[288,1024]{1,0:T(8,128)S(1)} %get-tuple-element.78.w, ...), custom_call_target="tpu_custom_call" | custom-call | flops 49999998976 | bytes 500000000 | tf_op jit(solution)/shard_map/pallas_call | solution.py:36
  90.4 2.0 %collective-permute-start.15 = (bf16[288,256]{1,0:T(8,128)(2,1)S(1)}, bf16[288,256]{1,0:T(8,128)(2,1)S(1)}, u32[]{:S(2)}, u32[]{:S(2)}) collective-permute-start(bf16[288,256]{1,0:T(8,128)(2,1)S(1)} %get-tuple-element.108), channel_id=1, source_target_pairs={{0,16},{1,17},{2,18},{3,19},{4,20},{5,21},{6,22},{7,23},{8,24},{9,... | collective-permute-start | bytes 442376 | tf_op jit(solution)/shard_map/ppermute | solution.py:30
  92.3 3.6 %collective-permute-start.16 = (bf16[288,256]{1,0:T(8,128)(2,1)S(1)}, bf16[288,256]{1,0:T(8,128)(2,1)S(1)}, u32[]{:S(2)}, u32[]{:S(2)}) collective-permute-start(bf16[288,256]{1,0:T(8,128)(2,1)S(1)} %get-tuple-element.109), channel_id=1, source_target_pairs={{0,32},{1,33},{2,34},{3,35},{4,36},{5,37},{6,38},{7,39},{8,40},{9,... | collective-permute-start | bytes 442376 | tf_op jit(solution)/shard_map/ppermute | solution.py:30
  98.8 3.6 %collective-permute-start.26 = (bf16[288,1024]{1,0:T(8,128)(2,1)S(1)}, bf16[288,1024]{1,0:T(8,128)(2,1)S(1)}, u32[]{:S(2)}, u32[]{:S(2)}) collective-permute-start(bf16[288,1024]{1,0:T(8,128)(2,1)S(1)} %get-tuple-element.123), channel_id=1, source_target_pairs={{0,6},{1,7},{2,0},{3,1},{4,2},{5,3},{6,4},{7,5},{8,14},{9,15},{10,... | collective-permute-start | bytes 1769480 | tf_op jit(solution)/shard_map/ppermute | solution.py:30
  103.3 3.7 %shard_map.133.near = bf16[256,4608]{1,0:T(8,128)(2,1)} custom-call(s32[4]{0:T(128)S(1)} %pad_add_fusion.place, bf16[864,2048]{1,0:T(8,128)(2,1)S(1)} %shard_map.123.w013, bf16[288,2048]{1,0:T(8,128)(2,1)S(1)} %shard_map.124.w2, bf16[864,2048]{1,0:T(8,128)(2,1)S(1)} %collective-permute-done.8.v013, bf16[288,2048]{1,0:T(8,128)(2,1)S(1)} %collective-permute-done.11.v2, ...), custom_call_target="tpu_custom_call" | custom-call | tf_op jit(solution)/shard_map/pallas_call | solution.py:36
  108.6 2.0 %collective-permute-start.21 = (bf16[288,256]{1,0:T(8,128)(2,1)S(1)}, bf16[288,256]{1,0:T(8,128)(2,1)S(1)}, u32[]{:S(2)}, u32[]{:S(2)}) collective-permute-start(bf16[288,256]{1,0:T(8,128)(2,1)S(1)} %multiply_convert_fusion.m0), channel_id=1, source_target_pairs={{0,16},{1,17},{2,18},{3,19},{4,20},{5,21},{6,22},{7,23},{8,24},{9,... | collective-permute-start | bytes 442376 | tf_op jit(solution)/shard_map/ppermute | solution.py:30
  110.6 3.6 %collective-permute-start.20 = (bf16[288,256]{1,0:T(8,128)(2,1)S(1)}, bf16[288,256]{1,0:T(8,128)(2,1)S(1)}, u32[]{:S(2)}, u32[]{:S(2)}) collective-permute-start(bf16[288,256]{1,0:T(8,128)(2,1)S(1)} %multiply_convert_fusion.m0), channel_id=1, source_target_pairs={{0,32},{1,33},{2,34},{3,35},{4,36},{5,37},{6,38},{7,39},{8,40},{9,... | collective-permute-start | bytes 442376 | tf_op jit(solution)/shard_map/ppermute | solution.py:30
  115.2 1.6 %shard_map.134 = bf16[256,4608]{1,0:T(8,128)(2,1)} custom-call(s32[4]{0:T(128)S(1)} %pad_add_fusion.place, bf16[256,2304]{1,0:T(8,128)(2,1)S(1)} %collective-permute-done.22.far, bf16[256,4608]{1,0:T(8,128)(2,1)} %shard_map.133.near), custom_call_target="tpu_custom_call", output_to_operand_aliasing={{}: (2, {})} | custom-call | tf_op jit(solution)/shard_map/pallas_call | solution.py:36
  116.8 3.8 %shard_map.136 = (f32[288,2,1024]{2,1,0:T(2,128)}, f32[288,2,1024]{2,1,0:T(2,128)}, f32[288,1024]{1,0:T(8,128)S(1)}) custom-call(s32[4]{0:T(128)S(1)} %pad_add_fusion.place, f32[288,1024]{1,0:T(8,128)S(1)} %get-tuple-element.113.m_key, f32[288,1024]{1,0:T(8,128)S(1)} %get-tuple-element.114.v_key, f32[288,1024]{1,0:T(8,128)S(1)} %get-tuple-element.115.w, ...), custom_call_target="tpu_custom_call" | custom-call | tf_op jit(solution)/shard_map/pallas_call | solution.py:36
  120.6 3.5 %shard_map.137 = (f32[288,2,1024]{2,1,0:T(2,128)}, f32[288,1024]{1,0:T(8,128)}, f32[288,1024]{1,0:T(8,128)}) custom-call(s32[4]{0:T(128)S(1)} %pad_add_fusion.place, bf16[288,256]{1,0:T(8,128)(2,1)S(1)} %multiply_convert_fusion.m0, bf16[288,256]{1,0:T(8,128)(2,1)S(1)} %collective-permute-done.19.m1, bf16[288,256]{1,0:T(8,128)(2,1)S(1)} %collective-permute-done.20.m2, ...), custom_call_target="tpu_custom_call" | custom-call | tf_op jit(solution)/shard_map/pallas_call | solution.py:36
  (69 shorter events, 15.2 us)
Async XLA Ops:
  2.4 4.0 %copy-start = (f32[1,288,2,1024]{3,2,1,0:T(2,128)S(1)}, f32[1,288,2,1024]{3,2,1,0:T(2,128)}, u32[]{:S(2)}) copy-start(f32[1,288,2,1024]{3,2,1,0:T(2,128)} %param.9) | copy-start | bytes 7077892
  3.0 30.4 %collective-permute-start = (bf16[256,2304]{1,0:T(8,128)(2,1)S(1)}, bf16[256,2304]{1,0:T(8,128)(2,1)S(1)}, u32[]{:S(2)}, u32[]{:S(2)}) collective-permute-start(bf16[256,2304]{1,0:T(8,128)(2,1)S(1)} %shard_map.118), channel_id=1, source_target_pairs={{0,8},{1,9},{2,10},{3,11},{4,12},{5,13},{6,14},{7,15},{8,0},{9,1},... | collective-permute-start | bytes 3538952 | tf_op jit(solution)/shard_map/ppermute | solution.py:30
  6.4 6.2 %copy-start.9 = (bf16[1,256,2,1024]{3,2,1,0:T(2,128)(2,1)S(1)}, bf16[1,256,2,1024]{3,2,1,0:T(2,128)(2,1)}, u32[]{:S(2)}) copy-start(bf16[1,256,2,1024]{3,2,1,0:T(2,128)(2,1)} %param.8) | copy-start | bytes 3145732
  6.4 7.6 %copy-start.2 = (f32[1,288,2,1024]{3,2,1,0:T(2,128)S(1)}, f32[1,288,2,1024]{3,2,1,0:T(2,128)}, u32[]{:S(2)}) copy-start(f32[1,288,2,1024]{3,2,1,0:T(2,128)} %param.11) | copy-start | bytes 7077892
  9.3 28.7 %collective-permute-start.2 = (bf16[288,2048]{1,0:T(8,128)(2,1)S(1)}, bf16[288,2048]{1,0:T(8,128)(2,1)S(1)}, u32[]{:S(2)}, u32[]{:S(2)}) collective-permute-start(bf16[288,2048]{1,0:T(8,128)(2,1)S(1)} %shard_map.119.refs_0_), channel_id=1, source_target_pairs={{0,2},{1,3},{2,4},{3,5},{4,6},{5,7},{6,0},{7,1},{8,10},{9,11},{10,... | collective-permute-start | bytes 3538952 | tf_op jit(solution)/shard_map/ppermute | solution.py:30
  10.9 27.1 %collective-permute-start.1 = (bf16[288,2048]{1,0:T(8,128)(2,1)S(1)}, bf16[288,2048]{1,0:T(8,128)(2,1)S(1)}, u32[]{:S(2)}, u32[]{:S(2)}) collective-permute-start(bf16[288,2048]{1,0:T(8,128)(2,1)S(1)} %shard_map.119.refs_0_), channel_id=1, source_target_pairs={{0,6},{1,7},{2,0},{3,1},{4,2},{5,3},{6,4},{7,5},{8,14},{9,15},{10,... | collective-permute-start | bytes 3538952 | tf_op jit(solution)/shard_map/ppermute | solution.py:30
  13.0 31.7 %copy-start.5 = (bf16[256,1024]{1,0:T(8,128)(2,1)}, bf16[256,1024]{1,0:T(8,128)(2,1)S(1)}, u32[]{:S(2)}) copy-start(bf16[256,1024]{1,0:T(8,128)(2,1)S(1)} %get-tuple-element.133.c_own.tokens) | copy-start | bytes 1572868
  13.0 31.7 %collective-permute-start.3 = (bf16[256,1024]{1,0:T(8,128)(2,1)S(1)}, bf16[256,1024]{1,0:T(8,128)(2,1)S(1)}, u32[]{:S(2)}, u32[]{:S(2)}) collective-permute-start(bf16[256,1024]{1,0:T(8,128)(2,1)S(1)} %get-tuple-element.133.c_own.tokens), channel_id=1, source_target_pairs={{0,8},{1,9},{2,10},{3,11},{4,12},{5,13},{6,14},{7,15},{8,0},{9,1},... | collective-permute-start | bytes 1572872 | tf_op jit(solution)/shard_map/ppermute | solution.py:30
  14.5 19.0 %copy-start.4 = (bf16[1,256,4608]{2,1,0:T(8,128)(2,1)S(1)}, bf16[1,256,4608]{2,1,0:T(8,128)(2,1)}, u32[]{:S(2)}) copy-start(bf16[1,256,4608]{2,1,0:T(8,128)(2,1)} %param.7) | copy-start | bytes 7077892
  16.3 38.5 %collective-permute-start.5 = (bf16[256,1024]{1,0:T(8,128)(2,1)S(1)}, bf16[256,1024]{1,0:T(8,128)(2,1)S(1)}, u32[]{:S(2)}, u32[]{:S(2)}) collective-permute-start(bf16[256,1024]{1,0:T(8,128)(2,1)S(1)} %get-tuple-element.84.c_own.tokens), channel_id=1, source_target_pairs={{0,8},{1,9},{2,10},{3,11},{4,12},{5,13},{6,14},{7,15},{8,0},{9,1},... | collective-permute-start | bytes 1572872 | tf_op jit(solution)/shard_map/ppermute | solution.py:30
  38.9 15.9 %collective-permute-start.7 = (bf16[144,2048]{1,0:T(8,128)(2,1)S(1)}, bf16[144,2048]{1,0:T(8,128)(2,1)S(1)}, u32[]{:S(2)}, u32[]{:S(2)}) collective-permute-start(bf16[144,2048]{1,0:T(8,128)(2,1)S(1)} %slice.15), channel_id=1, source_target_pairs={{0,6},{1,7},{2,0},{3,1},{4,2},{5,3},{6,4},{7,5},{8,14},{9,15},{10,... | collective-permute-start | bytes 1769480 | tf_op jit(solution)/shard_map/ppermute | solution.py:30
  41.9 14.5 %collective-permute-start.6 = (bf16[144,2048]{1,0:T(8,128)(2,1)S(1)}, bf16[144,2048]{1,0:T(8,128)(2,1)S(1)}, u32[]{:S(2)}, u32[]{:S(2)}) collective-permute-start(bf16[144,2048]{1,0:T(8,128)(2,1)S(1)} %slice.14), channel_id=1, source_target_pairs={{0,2},{1,3},{2,4},{3,5},{4,6},{5,7},{6,0},{7,1},{8,10},{9,11},{10,... | collective-permute-start | bytes 1769480 | tf_op jit(solution)/shard_map/ppermute | solution.py:30
  41.9 14.5 %collective-permute-start.8 = (bf16[864,2048]{1,0:T(8,128)(2,1)S(1)}, bf16[864,2048]{1,0:T(8,128)(2,1)S(1)}, u32[]{:S(2)}, u32[]{:S(2)}) collective-permute-start(bf16[864,2048]{1,0:T(8,128)(2,1)S(1)} %shard_map.123.w013), channel_id=1, source_target_pairs={{0,1},{1,0},{2,3},{3,2},{4,5},{5,4},{6,7},{7,6},{8,9},{9,8},{10,11... | collective-permute-start | bytes 10616840 | tf_op jit(solution)/shard_map/ppermute | solution.py:30
  49.4 7.8 %collective-permute-start.4 = (bf16[4,288,1024]{2,1,0:T(8,128)(2,1)S(1)}, bf16[4,288,1024]{2,1,0:T(8,128)(2,1)S(1)}, u32[]{:S(2)}, u32[]{:S(2)}) collective-permute-start(bf16[4,288,1024]{2,1,0:T(8,128)(2,1)S(1)} %get-tuple-element.83), channel_id=1, source_target_pairs={{0,1},{1,0},{2,3},{3,2},{4,5},{5,4},{6,7},{7,6},{8,9},{9,8},{10,11... | collective-permute-start | bytes 7077896 | tf_op jit(solution)/shard_map/ppermute | solution.py:30
  57.1 8.9 %collective-permute-start.11 = (bf16[288,2048]{1,0:T(8,128)(2,1)S(1)}, bf16[288,2048]{1,0:T(8,128)(2,1)S(1)}, u32[]{:S(2)}, u32[]{:S(2)}) collective-permute-start(bf16[288,2048]{1,0:T(8,128)(2,1)S(1)} %shard_map.124.w2), channel_id=1, source_target_pairs={{0,1},{1,0},{2,3},{3,2},{4,5},{5,4},{6,7},{7,6},{8,9},{9,8},{10,11... | collective-permute-start | bytes 3538952 | tf_op jit(solution)/shard_map/ppermute | solution.py:30
  57.9 11.1 %collective-permute-start.9 = (bf16[144,1024]{1,0:T(8,128)(2,1)S(1)}, bf16[144,1024]{1,0:T(8,128)(2,1)S(1)}, u32[]{:S(2)}, u32[]{:S(2)}) collective-permute-start(bf16[144,1024]{1,0:T(8,128)(2,1)S(1)} %get-tuple-element.90), channel_id=1, source_target_pairs={{0,2},{1,3},{2,4},{3,5},{4,6},{5,7},{6,0},{7,1},{8,10},{9,11},{10,... | collective-permute-start | bytes 884744 | tf_op jit(solution)/shard_map/ppermute | solution.py:30
  57.9 11.0 %collective-permute-start.10 = (bf16[144,1024]{1,0:T(8,128)(2,1)S(1)}, bf16[144,1024]{1,0:T(8,128)(2,1)S(1)}, u32[]{:S(2)}, u32[]{:S(2)}) collective-permute-start(bf16[144,1024]{1,0:T(8,128)(2,1)S(1)} %get-tuple-element.91), channel_id=1, source_target_pairs={{0,6},{1,7},{2,0},{3,1},{4,2},{5,3},{6,4},{7,5},{8,14},{9,15},{10,... | collective-permute-start | bytes 884744 | tf_op jit(solution)/shard_map/ppermute | solution.py:30
  65.9 13.1 %collective-permute-start.14 = (bf16[4,288,1024]{2,1,0:T(8,128)(2,1)S(1)}, bf16[4,288,1024]{2,1,0:T(8,128)(2,1)S(1)}, u32[]{:S(2)}, u32[]{:S(2)}) collective-permute-start(bf16[4,288,1024]{2,1,0:T(8,128)(2,1)S(1)} %get-tuple-element.94), channel_id=1, source_target_pairs={{0,1},{1,0},{2,3},{3,2},{4,5},{5,4},{6,7},{7,6},{8,9},{9,8},{10,11... | collective-permute-start | bytes 7077896 | tf_op jit(solution)/shard_map/ppermute | solution.py:30
  69.8 17.4 %collective-permute-start.12 = (bf16[288,1024]{1,0:T(8,128)(2,1)S(1)}, bf16[288,1024]{1,0:T(8,128)(2,1)S(1)}, u32[]{:S(2)}, u32[]{:S(2)}) collective-permute-start(bf16[288,1024]{1,0:T(8,128)(2,1)S(1)} %get-tuple-element.98), channel_id=1, source_target_pairs={{0,2},{1,3},{2,4},{3,5},{4,6},{5,7},{6,0},{7,1},{8,10},{9,11},{10,... | collective-permute-start | bytes 1769480 | tf_op jit(solution)/shard_map/ppermute | solution.py:30
  69.9 16.9 %collective-permute-start.13 = (bf16[288,1024]{1,0:T(8,128)(2,1)S(1)}, bf16[288,1024]{1,0:T(8,128)(2,1)S(1)}, u32[]{:S(2)}, u32[]{:S(2)}) collective-permute-start(bf16[288,1024]{1,0:T(8,128)(2,1)S(1)} %get-tuple-element.99), channel_id=1, source_target_pairs={{0,6},{1,7},{2,0},{3,1},{4,2},{5,3},{6,4},{7,5},{8,14},{9,15},{10,... | collective-permute-start | bytes 1769480 | tf_op jit(solution)/shard_map/ppermute | solution.py:30
  77.2 37.0 %collective-permute-start.22 = (bf16[256,2304]{1,0:T(8,128)(2,1)S(1)}, bf16[256,2304]{1,0:T(8,128)(2,1)S(1)}, u32[]{:S(2)}, u32[]{:S(2)}) collective-permute-start(bf16[256,2304]{1,0:T(8,128)(2,1)S(1)} %shard_map.129), channel_id=1, source_target_pairs={{0,8},{1,9},{2,10},{3,11},{4,12},{5,13},{6,14},{7,15},{8,0},{9,1},... | collective-permute-start | bytes 3538952 | tf_op jit(solution)/shard_map/ppermute | solution.py:30
  79.6 17.3 %collective-permute-start.23 = (bf16[144,1024]{1,0:T(8,128)(2,1)S(1)}, bf16[144,1024]{1,0:T(8,128)(2,1)S(1)}, u32[]{:S(2)}, u32[]{:S(2)}) collective-permute-start(bf16[144,1024]{1,0:T(8,128)(2,1)S(1)} %get-tuple-element.103), channel_id=1, source_target_pairs={{0,2},{1,3},{2,4},{3,5},{4,6},{5,7},{6,0},{7,1},{8,10},{9,11},{10,... | collective-permute-start | bytes 884744 | tf_op jit(solution)/shard_map/ppermute | solution.py:30
  79.7 16.2 %collective-permute-start.24 = (bf16[144,1024]{1,0:T(8,128)(2,1)S(1)}, bf16[144,1024]{1,0:T(8,128)(2,1)S(1)}, u32[]{:S(2)}, u32[]{:S(2)}) collective-permute-start(bf16[144,1024]{1,0:T(8,128)(2,1)S(1)} %get-tuple-element.120), channel_id=1, source_target_pairs={{0,6},{1,7},{2,0},{3,1},{4,2},{5,3},{6,4},{7,5},{8,14},{9,15},{10,... | collective-permute-start | bytes 884744 | tf_op jit(solution)/shard_map/ppermute | solution.py:30
  90.4 8.5 %collective-permute-start.15 = (bf16[288,256]{1,0:T(8,128)(2,1)S(1)}, bf16[288,256]{1,0:T(8,128)(2,1)S(1)}, u32[]{:S(2)}, u32[]{:S(2)}) collective-permute-start(bf16[288,256]{1,0:T(8,128)(2,1)S(1)} %get-tuple-element.108), channel_id=1, source_target_pairs={{0,16},{1,17},{2,18},{3,19},{4,20},{5,21},{6,22},{7,23},{8,24},{9,... | collective-permute-start | bytes 442376 | tf_op jit(solution)/shard_map/ppermute | solution.py:30
  92.3 10.1 %collective-permute-start.16 = (bf16[288,256]{1,0:T(8,128)(2,1)S(1)}, bf16[288,256]{1,0:T(8,128)(2,1)S(1)}, u32[]{:S(2)}, u32[]{:S(2)}) collective-permute-start(bf16[288,256]{1,0:T(8,128)(2,1)S(1)} %get-tuple-element.109), channel_id=1, source_target_pairs={{0,32},{1,33},{2,34},{3,35},{4,36},{5,37},{6,38},{7,39},{8,40},{9,... | collective-permute-start | bytes 442376 | tf_op jit(solution)/shard_map/ppermute | solution.py:30
  95.9 6.5 %collective-permute-start.17 = (bf16[288,256]{1,0:T(8,128)(2,1)S(1)}, bf16[288,256]{1,0:T(8,128)(2,1)S(1)}, u32[]{:S(2)}, u32[]{:S(2)}) collective-permute-start(bf16[288,256]{1,0:T(8,128)(2,1)S(1)} %get-tuple-element.110), channel_id=1, source_target_pairs={{0,48},{1,49},{2,50},{3,51},{4,52},{5,53},{6,54},{7,55},{8,56},{9,... | collective-permute-start | bytes 442376 | tf_op jit(solution)/shard_map/ppermute | solution.py:30
  97.9 18.9 %collective-permute-start.25 = (bf16[288,1024]{1,0:T(8,128)(2,1)S(1)}, bf16[288,1024]{1,0:T(8,128)(2,1)S(1)}, u32[]{:S(2)}, u32[]{:S(2)}) collective-permute-start(bf16[288,1024]{1,0:T(8,128)(2,1)S(1)} %get-tuple-element.122), channel_id=1, source_target_pairs={{0,2},{1,3},{2,4},{3,5},{4,6},{5,7},{6,0},{7,1},{8,10},{9,11},{10,... | collective-permute-start | bytes 1769480 | tf_op jit(solution)/shard_map/ppermute | solution.py:30
  98.8 18.0 %collective-permute-start.26 = (bf16[288,1024]{1,0:T(8,128)(2,1)S(1)}, bf16[288,1024]{1,0:T(8,128)(2,1)S(1)}, u32[]{:S(2)}, u32[]{:S(2)}) collective-permute-start(bf16[288,1024]{1,0:T(8,128)(2,1)S(1)} %get-tuple-element.123), channel_id=1, source_target_pairs={{0,6},{1,7},{2,0},{3,1},{4,2},{5,3},{6,4},{7,5},{8,14},{9,15},{10,... | collective-permute-start | bytes 1769480 | tf_op jit(solution)/shard_map/ppermute | solution.py:30
  102.5 6.0 %collective-permute-start.18 = (bf16[288,256]{1,0:T(8,128)(2,1)S(1)}, bf16[288,256]{1,0:T(8,128)(2,1)S(1)}, u32[]{:S(2)}, u32[]{:S(2)}) collective-permute-start(bf16[288,256]{1,0:T(8,128)(2,1)S(1)} %get-tuple-element.130), channel_id=1, source_target_pairs={{0,64},{1,65},{2,66},{3,67},{4,68},{5,69},{6,70},{7,71},{8,72},{9,... | collective-permute-start | bytes 442376 | tf_op jit(solution)/shard_map/ppermute | solution.py:30
  108.6 12.0 %collective-permute-start.21 = (bf16[288,256]{1,0:T(8,128)(2,1)S(1)}, bf16[288,256]{1,0:T(8,128)(2,1)S(1)}, u32[]{:S(2)}, u32[]{:S(2)}) collective-permute-start(bf16[288,256]{1,0:T(8,128)(2,1)S(1)} %multiply_convert_fusion.m0), channel_id=1, source_target_pairs={{0,16},{1,17},{2,18},{3,19},{4,20},{5,21},{6,22},{7,23},{8,24},{9,... | collective-permute-start | bytes 442376 | tf_op jit(solution)/shard_map/ppermute | solution.py:30
  110.6 10.0 %collective-permute-start.20 = (bf16[288,256]{1,0:T(8,128)(2,1)S(1)}, bf16[288,256]{1,0:T(8,128)(2,1)S(1)}, u32[]{:S(2)}, u32[]{:S(2)}) collective-permute-start(bf16[288,256]{1,0:T(8,128)(2,1)S(1)} %multiply_convert_fusion.m0), channel_id=1, source_target_pairs={{0,32},{1,33},{2,34},{3,35},{4,36},{5,37},{6,38},{7,39},{8,40},{9,... | collective-permute-start | bytes 442376 | tf_op jit(solution)/shard_map/ppermute | solution.py:30
  114.2 6.5 %collective-permute-start.19 = (bf16[288,256]{1,0:T(8,128)(2,1)S(1)}, bf16[288,256]{1,0:T(8,128)(2,1)S(1)}, u32[]{:S(2)}, u32[]{:S(2)}) collective-permute-start(bf16[288,256]{1,0:T(8,128)(2,1)S(1)} %multiply_convert_fusion.m0), channel_id=1, source_target_pairs={{0,48},{1,49},{2,50},{3,51},{4,52},{5,53},{6,54},{7,55},{8,56},{9,... | collective-permute-start | bytes 442376 | tf_op jit(solution)/shard_map/ppermute | solution.py:30
  (5 other events, 15.2 us)
